TPU v7x, 256 devices: a whole 4x4x8 slice. The times are simulated.
256 devices in a mesh: dp: 128 (over y_hi, x, z, core), tensor: 2 (over y_lo).
Axes of the slice: x: 4, y: 4 (y_hi: 2, y_lo: 2; y = y_hi * 2 + y_lo), z: 8, core: 2. Of those that a mesh axis runs over, the one named last changes fastest.
Arguments:
- image_raw: bfloat16 [8192, 1152], P(('dp', 'tensor')), may hold values from -0.1875 to 0.1875
- text_raw: bfloat16 [8192, 1152], P('dp'), may hold values from -0.1875 to 0.1875
- logit_scale: float32 [], replicated, may hold values from 8 to 24
- logit_bias: float32 [], replicated, may hold values from -4 to -1
- pair_offset: int32 [8192], P(('dp', 'tensor')), may hold values from 0 to 448
- normed_patches: bfloat16 [93312, 1152], P('dp'), may hold values from -24 to 24
- head_cotangent: bfloat16 [93312, 1152], P('dp'), may hold values from -0.25 to 0.25
- hidden_pre: bfloat16 [93312, 4304], P('dp', 'tensor'), may hold values from -6 to 6
- pool_share: float32 [93312], P('dp'), may hold values from 0.0005 to 0.005
- down_weight: bfloat16 [4304, 1152], P('tensor'), may hold values from -0.09375 to 0.09375
Outputs:
- image_grad: bfloat16 [8192, 1152], P(('dp', 'tensor'))
- text_grad: bfloat16 [8192, 1152], P('dp')
- up_grad: float32 [1152, 4304], P('dp', 'tensor')
All inputs are finite; a program needn't handle non-finite values.
Results may differ from a plain program's by a relative error of at most 0.0058.
Values may be sent and summed in bfloat16 or wider, within the bound.
No kernel may reach another device: no remote copies, remote signals or barrier semaphores. Data moves between devices by JAX's collectives and lax.ppermute only.
A program may use at most 128 MiB of HBM per device.

v0:
```python
import functools

import jax
import jax.numpy as jnp
from jax import lax
from jax.experimental import pallas as pl
from jax.experimental.pallas import tpu as pltpu
from jax.sharding import PartitionSpec as P

WINDOW = 8
N_YH, N_X, N_Z, N_CORE = 2, 4, 8, 2
N_DP = N_YH * N_X * N_Z * N_CORE
N_TENSOR = 2
LANES = 128
LIGHT = pl.CostEstimate(flops=1, bytes_accessed=1, transcendentals=0)

epsilon = 1e-06
gelu_root = 0.7978845608028654
gelu_cubic = 0.044715

f32 = jnp.float32
bf16 = jnp.bfloat16


def encode(yh, x, z, core):
    return (((yh % N_YH) * N_X + x % N_X) * N_Z + z % N_Z) * N_CORE + core % N_CORE


def torus_pairs(yh=0, x=0, z=0, core=0):
    pairs = []
    for j in range(N_DP):
        own = (j // (N_CORE * N_Z * N_X), j // (N_CORE * N_Z) % N_X, j // N_CORE % N_Z, j % N_CORE)
        pairs.append((j, encode(own[0] + yh, own[1] + x, own[2] + z, own[3] + core)))
    return pairs


def torus_send(array, **shift):
    return lax.ppermute(array, "dp", torus_pairs(**shift))


def ring_send(array, by, only=None):
    pairs = [(j, (j + by) % N_DP) for j in range(N_DP) if only is None or j % N_CORE == only]
    return lax.ppermute(array, "dp", pairs)


def tensor_swap(array):
    return lax.ppermute(array, "tensor", [(0, 1), (1, 0)])


def unit_rows(raw_rows):
    widened = raw_rows.astype(f32)
    lengths = jnp.sqrt(jnp.sum(widened * widened, axis=-1, keepdims=True) + epsilon)
    return (widened / lengths, lengths)


def project_back(unit_part, lengths, direction):
    radial = jnp.sum(unit_part * direction, axis=-1, keepdims=True)
    return (direction - unit_part * radial) / lengths


def gelu_slope(hidden_in):
    square = hidden_in * hidden_in
    tangent = jnp.tanh(hidden_in * (gelu_root + gelu_root * gelu_cubic * square))
    inner_slope = hidden_in * (0.5 * gelu_root + 1.5 * gelu_root * gelu_cubic * square)
    return 0.5 + 0.5 * tangent + (1.0 - tangent * tangent) * inner_slope


def dot_nt(a, b):
    return lax.dot_general(a, b, (((1,), (1,)), ((), ())), preferred_element_type=f32)


def dot_tn(a, b):
    return lax.dot_general(a, b, (((0,), (0,)), ((), ())), preferred_element_type=f32)


def key_rows(raw):
    return unit_rows(raw)[0].astype(bf16)


def text_key_kernel(half, place_ref, raw_ref, half_ref):
    begin = pl.multiple_of(place_ref[1] * half, half)
    half_ref[...] = key_rows(raw_ref[pl.ds(begin, half), :])


def text_half_key(place, text_raw, half):
    return pl.pallas_call(
        functools.partial(text_key_kernel, half),
        in_specs=[pl.BlockSpec(memory_space=pltpu.SMEM), pl.BlockSpec(memory_space=pltpu.VMEM)],
        out_specs=pl.BlockSpec(memory_space=pltpu.VMEM),
        out_shape=jax.ShapeDtypeStruct((half, text_raw.shape[1]), bf16),
    )(place, text_raw)


def pair_kernel(place_ref, scalar_ref, value_ref, window_value_ref, valid_ref, own_ref, other_ref, *refs):
    window_refs = refs[:-8]
    own_part, other_part, zero_ref, text_own, text_sibling, text_far, key_ref, window_key = refs[-8:]
    half = own_ref.shape[0]
    key_ref[:half, :] = key_rows(own_ref[...])
    key_ref[half:, :] = key_rows(other_ref[...])
    begin = 0
    for ref in window_refs:
        window_key[begin : begin + ref.shape[0], :] = ref[...]
        begin += ref.shape[0]
    logits = scalar_ref[0] * dot_nt(key_ref[...], window_key[...]) + scalar_ref[1]
    target = (value_ref[...] == window_value_ref[...]).astype(f32)
    weight = jnp.where(valid_ref[...] > 0, jax.nn.sigmoid(logits) - target, 0.0).astype(bf16)
    part = jnp.dot(weight, window_key[...], preferred_element_type=f32)
    own_part[...] = part[:half]
    other_part[...] = part[half:].astype(bf16)
    text_part = dot_tn(weight, key_ref[...])
    count = text_own.shape[0]
    text_own[...] = text_part[:count]
    text_sibling[...] = text_part[count : 2 * count].astype(bf16)
    text_far[...] = text_part[2 * count :].astype(bf16)
    zero_ref[...] = jnp.where(place_ref[1] == 0, part[:1], part[half : half + 1])


def pair_products(place, scalars, value, window_value, valid, own, other, window):
    width = own.shape[1]
    rows = value.shape[0]
    depth = window_value.shape[0]
    smem = pl.BlockSpec(memory_space=pltpu.SMEM)
    vmem = pl.BlockSpec(memory_space=pltpu.VMEM)
    return pl.pallas_call(
        pair_kernel,
        in_specs=[smem, smem] + [vmem] * (5 + len(window)),
        out_specs=[vmem] * 6,
        out_shape=[
            jax.ShapeDtypeStruct((rows // 2, width), f32),
            jax.ShapeDtypeStruct((rows // 2, width), bf16),
            jax.ShapeDtypeStruct((1, width), f32),
            jax.ShapeDtypeStruct((2 * rows, width), f32),
            jax.ShapeDtypeStruct((2 * rows, width), bf16),
            jax.ShapeDtypeStruct((depth - 4 * rows, width), bf16),
        ],
        scratch_shapes=[pltpu.VMEM((rows, width), bf16), pltpu.VMEM((depth, width), bf16)],
        compiler_params=pltpu.CompilerParams(vmem_limit_bytes=16 * 2**20),
        cost_estimate=LIGHT,
    )(
        place,
        scalars,
        value[:, None],
        window_value[None, :],
        valid.astype(jnp.int32)[None, :],
        own,
        other,
        *window,
    )


def pooled_kernel(place_ref, scalar_ref, own_ref, other_ref, mine_ref, theirs_ref, pooled_ref):
    raw = jnp.where(place_ref[1] == 0, own_ref[:1, :].astype(f32), other_ref[:1, :].astype(f32))
    unit, length = unit_rows(raw)
    direction = scalar_ref[0] * (mine_ref[...] + theirs_ref[...])
    pooled_ref[...] = project_back(unit, length, direction).astype(bf16)


def pooled_row(place, scalars, own, other, mine, theirs):
    smem = pl.BlockSpec(memory_space=pltpu.SMEM)
    vmem = pl.BlockSpec(memory_space=pltpu.VMEM)
    return pl.pallas_call(
        pooled_kernel,
        in_specs=[smem, smem] + [vmem] * 4,
        out_specs=vmem,
        out_shape=jax.ShapeDtypeStruct(mine.shape, bf16),
    )(place, scalars, own, other, mine, theirs)


def transpose_kernel(patches, normed_ref, out_ref):
    block = normed_ref[...]
    kept = lax.broadcasted_iota(jnp.int32, block.shape, 0) < patches
    out_ref[...] = jnp.where(kept, block, jnp.zeros_like(block)).T


def transposed(normed, rows):
    patches, width = normed.shape
    step = 3 * LANES
    return pl.pallas_call(
        functools.partial(transpose_kernel, patches),
        grid=(width // step,),
        in_specs=[pl.BlockSpec((rows, step), lambda i: (0, i))],
        out_specs=pl.BlockSpec((step, rows), lambda i: (i, 0)),
        out_shape=jax.ShapeDtypeStruct((width, rows), bf16),
        compiler_params=pltpu.CompilerParams(vmem_limit_bytes=8 * 2**20),
        cost_estimate=LIGHT,
    )(normed)


def copy_all(pairs, sems, first):
    copies = [pltpu.make_async_copy(src, dst, sems.at[first + i]) for i, (src, dst) in enumerate(pairs)]
    for copy in copies:
        copy.start()
    return copies


def base_kernel(place_ref, share_ref, weight_tail, hidden_tail, cotangent_hbm, weight_hbm, hidden_hbm, *refs):
    base_hbm, slope_hbm, cotangent, weight, hidden, base, slope, sems = refs
    patches, columns = base.shape
    start = columns - LANES
    step = start // 2
    begin = place_ref[0] * start
    halves = [pl.ds(pl.multiple_of(begin + i * step, step), step) for i in range(2)]
    wheres = [pl.ds(i * step, step) for i in range(2)]
    loads = copy_all(
        [
            (hidden_hbm.at[:, halves[0]], hidden.at[:, wheres[0]]),
            (cotangent_hbm, cotangent),
            (weight_hbm.at[halves[0], :], weight.at[wheres[0], :]),
            (hidden_hbm.at[:, halves[1]], hidden.at[:, wheres[1]]),
            (weight_hbm.at[halves[1], :], weight.at[wheres[1], :]),
        ],
        sems,
        0,
    )
    share = share_ref[...].T[:patches, :1]

    def block(weight_rows, hidden_block, where, ready):
        kept = gelu_slope(hidden_block.astype(f32))
        slope[:, where] = (share * kept).astype(bf16)
        for copy in ready:
            copy.wait()
        base[:, where] = (dot_nt(cotangent[...], weight_rows[...]) * kept).astype(bf16)

    def store(where, first):
        return copy_all(
            [(base.at[:, where], base_hbm.at[:, where]), (slope.at[:, where], slope_hbm.at[:, where])], sems, first
        )

    loads[0].wait()
    block(weight.at[wheres[0], :], hidden[:, wheres[0]], wheres[0], loads[1:3])
    stores = store(wheres[0], 5)
    loads[3].wait()
    block(weight.at[wheres[1], :], hidden[:, wheres[1]], wheres[1], loads[4:])
    stores += store(wheres[1], 7)
    where = pl.ds(start, LANES)
    block(weight_tail, hidden_tail[...], where, [])
    stores += store(where, 9)
    for copy in stores:
        copy.wait()


def hidden_base(place, columns, cotangent, share, weight, hidden):
    patches, width = cotangent.shape
    start = columns - LANES
    tiles = start // LANES
    hbm = pl.BlockSpec(memory_space=pl.ANY)
    out = jax.ShapeDtypeStruct((patches, columns), bf16)
    return pl.pallas_call(
        base_kernel,
        grid_spec=pltpu.PrefetchScalarGridSpec(
            num_scalar_prefetch=1,
            grid=(1,),
            in_specs=[
                pl.BlockSpec(share.shape, lambda i, place: (0, 0)),
                pl.BlockSpec((LANES, width), lambda i, place: (tiles * (1 + place[0]), 0)),
                pl.BlockSpec((patches, LANES), lambda i, place: (0, tiles * (1 + place[0]))),
                hbm,
                hbm,
                hbm,
            ],
            out_specs=[hbm, hbm],
            scratch_shapes=[
                pltpu.VMEM((patches, width), bf16),
                pltpu.VMEM((start, width), bf16),
                pltpu.VMEM((patches, start), bf16),
                pltpu.VMEM((patches, columns), bf16),
                pltpu.VMEM((patches, columns), bf16),
                pltpu.SemaphoreType.DMA((11,)),
            ],
        ),
        out_shape=[out, out],
        compiler_params=pltpu.CompilerParams(vmem_limit_bytes=60 * 2**20),
        cost_estimate=LIGHT,
    )(place, share, weight, hidden, cotangent, weight, hidden)


def block_rows(targets_ref, height, dy, dx):
    return pl.ds(pl.multiple_of(targets_ref[dy * N_X + dx] * height, 16), height)


def terms_kernel(
    place_ref,
    targets_ref,
    pooled0_ref,
    pooled1_ref,
    weight_tail,
    normed0_hbm,
    normed1_hbm,
    base0_hbm,
    base1_hbm,
    slope0_hbm,
    slope1_hbm,
    weight_hbm,
    a_keep,
    a_sent1,
    a_sent2,
    a_sent3,
    c_keep,
    c_sent,
    weight,
    normed,
    base,
    slope,
    sum_a,
    sum_c,
    stage_a,
    stage_c,
    sems,
):
    _, patches, columns = base.shape
    width = weight.shape[1]
    start = columns - LANES
    split = a_keep.shape[2]
    height = a_keep.shape[1]
    begin = pl.multiple_of(place_ref[0] * start, start)
    part_a, part_c = pl.ds(0, split), pl.ds(split, columns - split)
    images = ((slope0_hbm, base0_hbm, normed0_hbm), (slope1_hbm, base1_hbm, normed1_hbm))
    pairs = [(weight_hbm.at[pl.ds(begin, start), :], weight)]
    for i, (slope_hbm, base_hbm, normed_hbm) in enumerate(images):
        pairs += [
            (slope_hbm.at[:, part_c], slope.at[i, :, part_c]),
            (base_hbm.at[:, part_c], base.at[i, :, part_c]),
            (normed_hbm, normed.at[i]),
        ]
    for i, (slope_hbm, base_hbm, normed_hbm) in enumerate(images):
        pairs += [
            (slope_hbm.at[:, part_a], slope.at[i, :, part_a]),
            (base_hbm.at[:, part_a], base.at[i, :, part_a]),
        ]
    loads = copy_all(pairs, sems, 0)
    pooled = jnp.concatenate(
        [jnp.broadcast_to(ref[...].astype(f32), (8, width)) for ref in (pooled0_ref, pooled1_ref)], axis=0
    ).astype(bf16)
    loads[0].wait()
    lift = jnp.concatenate([dot_nt(pooled, weight[...]), dot_nt(pooled, weight_tail[...])], axis=1)

    def product(image, first, last):
        lifted = lift[8 * image : 8 * image + 1, first:last] * slope[image, :, first:last].astype(f32)
        grad = (base[image, :, first:last].astype(f32) + lifted).astype(bf16)
        return jnp.dot(normed[image, :, :patches], grad, preferred_element_type=f32)

    for copy in loads[1:4]:
        copy.wait()
    sum_c[...] = product(0, split, columns)
    for copy in loads[4:7]:
        copy.wait()
    sum_c[...] += product(1, split, columns)
    stores = copy_all(
        [(sum_c.at[block_rows(targets_ref, height, 0, dx), :], c_keep.at[dx]) for dx in range(N_X)], sems, 11
    )
    for dx in range(N_X):
        stage_c[dx] = sum_c[block_rows(targets_ref, height, 1, dx), :].astype(bf16)
    stores += copy_all([(stage_c, c_sent)], sems, 15)
    for copy in loads[7:]:
        copy.wait()
    sum_a[...] = product(0, 0, split) + product(1, 0, split)
    stores += copy_all(
        [(sum_a.at[block_rows(targets_ref, height, dy, 0), :], a_keep.at[dy]) for dy in range(N_YH)], sems, 16
    )
    for dx, out in ((1, a_sent1), (2, a_sent2), (3, a_sent3)):
        for dy in range(N_YH):
            stage_a[dx - 1, dy] = sum_a[block_rows(targets_ref, height, dy, dx), :].astype(bf16)
        stores += copy_all([(stage_a.at[dx - 1], out)], sems, 17 + dx)
    for copy in stores:
        copy.wait()


def up_terms(place, targets, split, normed_t, base, slope, weight, pooled):
    width, depth = normed_t[0].shape
    patches, columns = base[0].shape
    height = width // (N_YH * N_X)
    hbm = pl.BlockSpec(memory_space=pl.ANY)
    tiles = columns // LANES - 1
    row = pl.BlockSpec((1, width), lambda i, place, targets: (0, 0))
    part_a, part_c = (N_YH, height, split), (N_X, height, columns - split)
    return pl.pallas_call(
        terms_kernel,
        grid_spec=pltpu.PrefetchScalarGridSpec(
            num_scalar_prefetch=2,
            grid=(1,),
            in_specs=[
                row,
                row,
                pl.BlockSpec((LANES, width), lambda i, place, targets: (tiles * (1 + place[0]), 0)),
            ]
            + [hbm] * 7,
            out_specs=[hbm] * 6,
            scratch_shapes=[
                pltpu.VMEM((columns - LANES, width), bf16),
                pltpu.VMEM((2, width, depth), bf16),
                pltpu.VMEM((2, patches, columns), bf16),
                pltpu.VMEM((2, patches, columns), bf16),
                pltpu.VMEM((width, split), f32),
                pltpu.VMEM((width, columns - split), f32),
                pltpu.VMEM((N_X - 1,) + part_a, bf16),
                pltpu.VMEM(part_c, bf16),
                pltpu.SemaphoreType.DMA((21,)),
            ],
        ),
        out_shape=[
            jax.ShapeDtypeStruct(part_a, f32),
            jax.ShapeDtypeStruct(part_a, bf16),
            jax.ShapeDtypeStruct(part_a, bf16),
            jax.ShapeDtypeStruct(part_a, bf16),
            jax.ShapeDtypeStruct(part_c, f32),
            jax.ShapeDtypeStruct(part_c, bf16),
        ],
        compiler_params=pltpu.CompilerParams(vmem_limit_bytes=60 * 2**20),
        cost_estimate=LIGHT,
    )(place, targets, *pooled, weight, *normed_t, *base, *slope, weight)


def per_device(
    image_raw,
    text_raw,
    logit_scale,
    logit_bias,
    pair_offset,
    normed_patches,
    head_cotangent,
    hidden_pre,
    pool_share,
    down_weight,
):
    place = lax.axis_index("dp")
    tensor_index = lax.axis_index("tensor")
    yh = place // (N_CORE * N_Z * N_X)
    x = place // (N_CORE * N_Z) % N_X
    z = place // N_CORE % N_Z
    core = place % N_CORE
    image_rows, width = image_raw.shape
    text_rows = text_raw.shape[0]
    half = text_rows // N_TENSOR
    hidden_here = hidden_pre.shape[1]
    spot = jnp.stack([core, tensor_index]).astype(jnp.int32)
    scalars = jnp.stack([logit_scale, logit_bias])

    text_half = text_half_key(spot, text_raw, half)
    text_half, image_raw, pair_offset, normed_patches, head_cotangent, hidden_pre, pool_share = lax.optimization_barrier(
        (text_half, image_raw, pair_offset, normed_patches, head_cotangent, hidden_pre, pool_share)
    )
    text_far = ring_send(text_half, 7, only=1)
    text_near = jnp.concatenate([text_half, ring_send(text_half, 2)], axis=0)
    image_other = tensor_swap(image_raw)
    text_near, image_other, cotangent_own = lax.optimization_barrier((text_near, image_other, head_cotangent))
    text_next = ring_send(text_near, 4)
    rels = jnp.concatenate(
        [
            jnp.array([0, 2, 4, 6], jnp.int32),
            jnp.array([-1, 1, 3, 5], jnp.int32) + 2 * core,
            jnp.array([7], jnp.int32) + 2 * core,
        ]
    )
    text_row = jnp.arange(half, dtype=jnp.int32) + tensor_index * half
    text_value = (text_row[None, :] - text_rows * rels[:, None]).reshape(-1)
    text_valid = jnp.repeat((rels >= 0) & (rels < WINDOW), half)

    offset_other = tensor_swap(pair_offset)
    row = jnp.arange(image_rows, dtype=jnp.int32)
    own_row = row + tensor_index * image_rows
    other_row = row + (1 - tensor_index) * image_rows
    image_value = jnp.concatenate([own_row - pair_offset, other_row - offset_other])

    columns = 9 * LANES
    start = 8 * LANES
    cotangent_other = torus_send(head_cotangent, core=1)
    hidden_other = torus_send(hidden_pre, core=1)
    share_other = torus_send(pool_share, core=1)
    share_own, share_other = [
        jnp.broadcast_to(jnp.pad(part, (0, 6 * LANES - part.shape[0]))[None, :], (8, 6 * LANES))
        for part in (pool_share, share_other)
    ]
    base_own, slope_own = hidden_base(
        spot, columns, cotangent_own, share_own, down_weight, hidden_pre
    )
    text_next, text_far, base_own, slope_own = lax.optimization_barrier((text_next, text_far, base_own, slope_own))
    text_window = [text_near, text_next, torus_send(text_near, core=1), torus_send(text_next, core=1), text_far]
    normed_own = transposed(normed_patches, 6 * LANES)
    normed_other = torus_send(normed_own, core=1)

    text_last = text_window[3]
    text_last, share_other = lax.optimization_barrier((text_last, share_other))
    text_window[3] = text_last
    image_part, image_swapped, zero_row, text_own, text_sibling, far = pair_products(
        spot, scalars, image_value, text_value, text_valid, image_raw, image_other, text_window
    )
    zero_theirs = tensor_swap(zero_row)

    near = 2 * half
    returned = torus_send(text_sibling, core=1)
    far = ring_send(far, -7, only=0)
    image_swapped = tensor_swap(image_swapped)
    zero_row, returned, cotangent_other = lax.optimization_barrier((zero_row, returned, cotangent_other))
    text_next = ring_send((text_own[near:] + returned[near:].astype(f32)).astype(bf16), -4)

    base_other, slope_other = hidden_base(
        spot, columns, cotangent_other, share_other, down_weight, hidden_other
    )
    zero_theirs, base_other, slope_other = lax.optimization_barrier((zero_theirs, base_other, slope_other))
    pooled = pooled_row(spot, scalars, image_raw, image_other, zero_row, zero_theirs)
    pooled_other = torus_send(pooled, core=1)
    pooled_other, text_next, far, image_swapped = lax.optimization_barrier(
        (pooled_other, text_next, far, image_swapped)
    )

    split = 5 * LANES
    targets = jnp.stack(
        [(yh + dy) % N_YH * N_X + (x + dx) % N_X for dy in range(N_YH) for dx in range(N_X)]
    ).astype(jnp.int32)
    a_keep, a_sent1, a_sent2, a_sent3, c_keep, c_sent = up_terms(
        spot,
        targets,
        split,
        [normed_own, normed_other],
        [base_own, base_other],
        [slope_own, slope_other],
        down_weight,
        [pooled, pooled_other],
    )
    a_keep, image_part, late_text, late_image = lax.optimization_barrier((a_keep, image_part, text_raw, image_raw))
    c_come = torus_send(c_sent, yh=1)
    a_come = [torus_send(part, x=dx) for dx, part in ((2, a_sent2), (1, a_sent1), (3, a_sent3))]
    c_keep = c_keep + c_come.astype(f32)
    c_keep, a_keep, text_own, returned, text_next = lax.optimization_barrier(
        (c_keep, a_keep, text_own, returned, text_next)
    )
    a_keep = a_keep + (a_come[0].astype(f32) + a_come[1].astype(f32) + a_come[2].astype(f32))
    c_come = [torus_send(c_keep[dx].astype(bf16), x=dx) for dx in (2, 1, 3)]
    a_come = torus_send(a_keep[1].astype(bf16), yh=1)
    total = jnp.concatenate(
        [
            a_keep[0] + a_come.astype(f32),
            c_keep[0] + (c_come[0].astype(f32) + c_come[1].astype(f32) + c_come[2].astype(f32)),
        ],
        axis=1,
    )

    text_near = text_own[:near] + returned[:near].astype(f32) + text_next.astype(f32)
    text_back = ring_send(text_near[half:].astype(bf16), -2)
    total, text_back = lax.optimization_barrier((total, text_back))
    text_dir = logit_scale * (text_near[:half] + text_back.astype(f32) + far.astype(f32))
    text_unit, text_length = unit_rows(lax.dynamic_slice_in_dim(late_text, tensor_index * half, half, 0))
    text_mine = project_back(text_unit, text_length, text_dir).astype(bf16)

    image_unit, image_length = unit_rows(late_image)
    image_dir = logit_scale * (image_part + image_swapped.astype(f32))
    image_grad = project_back(image_unit, image_length, image_dir).astype(bf16)

    rows_chip = total.shape[0] // N_Z
    chunks = total.reshape(N_Z // 2, 2, rows_chip, columns)
    swap_pairs = [(j, j ^ N_CORE) for j in range(N_DP)]
    chunk = lax.dynamic_index_in_dim(chunks, 1 - z % 2, 1, keepdims=False).astype(bf16)
    chunks = lax.dynamic_index_in_dim(chunks, z % 2, 1, keepdims=False)
    chunks = chunks + lax.ppermute(chunk, "dp", swap_pairs).astype(f32)
    total = lax.dynamic_index_in_dim(chunks, z // 2, 0, keepdims=False)
    for hop in (2, 1, 3):
        chunk = lax.dynamic_index_in_dim(chunks, (z // 2 + hop) % (N_Z // 2), 0, keepdims=False).astype(bf16)
        total = total + torus_send(chunk, z=2 * hop).astype(f32)
    text_theirs = tensor_swap(text_mine)
    total, text_theirs, image_grad = lax.optimization_barrier((total, text_theirs, image_grad))
    rows_here = rows_chip // N_CORE
    mine = jnp.where(core == 0, total[:rows_here], total[rows_here:])
    theirs = torus_send(jnp.where(core == 0, total[rows_here:], total[:rows_here]), core=1)
    left = jnp.where(core == 0, mine, theirs)
    right = jnp.where(core == 0, theirs, mine)
    up_grad = jnp.concatenate([left, right[:, columns - start : hidden_here - start]], axis=1)

    text_grad = jnp.where(
        tensor_index == 0,
        jnp.concatenate([text_mine, text_theirs], axis=0),
        jnp.concatenate([text_theirs, text_mine], axis=0),
    )
    return (image_grad, text_grad, up_grad)


def solution(mesh):
    return jax.shard_map(
        per_device,
        mesh=mesh,
        in_specs=(
            P(("dp", "tensor"), None),
            P("dp", None),
            P(),
            P(),
            P(("dp", "tensor")),
            P("dp", None),
            P("dp", None),
            P("dp", "tensor"),
            P("dp"),
            P("tensor", None),
        ),
        out_specs=(P(("dp", "tensor"), None), P("dp", None), P("dp", "tensor")),
        check_vma=False,
    )
```

profile of v0, /device:TPU:1, one launch (start us, length us, event | category | flops | bytes accessed | tf_op | source)
XLA Modules:
  0.0 133.8 jit_solution(6512940322758925015)
XLA Ops:
  0.6 0.7 pad_add_fusion.place_ref
  1.3 1.7 %shard_map.148 = bf16[32,1152]{1,0:T(8,128)(2,1)} custom-call(s32[2]{0:T(128)} %pad_add_fusion.place_ref, bf16[64,1152]{1,0:T(8,128)(2,1)} %raw_ref.1), custom_call_target="tpu_custom_call" | custom-call | tf_op jit(solution)/shard_map/pallas_call | solution.py:86
  3.0 3.2 %collective-permute-start.11 = (bf16[729,2152]{1,0:T(8,128)(2,1)}, bf16[729,2152]{1,0:T(8,128)(2,1)}, u32[]{:S(2)}, u32[]{:S(2)}) collective-permute-start(bf16[729,2152]{1,0:T(8,128)(2,1)} %hidden_hbm), channel_id=1, source_target_pairs={{0,2},{2,0},{4,6},{6,4},{8,10},{10,8},{12,14},{14,12},{16,18},{18,... | collective-permute-start | bytes 9412856 | tf_op jit(solution)/shard_map/ppermute | solution.py:38
  6.2 8.0 %collective-permute-start.4 = (bf16[32,1152]{1,0:T(8,128)(2,1)}, bf16[32,1152]{1,0:T(8,128)(2,1)S(1)}, u32[]{:S(2)}, u32[]{:S(2)}) collective-permute-start(bf16[32,1152]{1,0:T(8,128)(2,1)} %shard_map.148), channel_id=1, source_target_pairs={{2,16},{6,20},{10,24},{14,28},{18,32},{22,36},{26,40},{30,44},{34,... | collective-permute-start | bytes 221192 | tf_op jit(solution)/shard_map/ppermute | solution.py:43
  14.2 1.4 %collective-permute-start.1 = (bf16[32,1152]{1,0:T(8,128)(2,1)}, bf16[32,1152]{1,0:T(8,128)(2,1)S(1)}, u32[]{:S(2)}, u32[]{:S(2)}) collective-permute-start(bf16[32,1152]{1,0:T(8,128)(2,1)} %own_ref.1), channel_id=1, source_target_pairs={{0,1},{1,0},{2,3},{3,2},{4,5},{5,4},{6,7},{7,6},{8,9},{9,8},{10,11... | collective-permute-start | bytes 221192 | tf_op jit(solution)/shard_map/ppermute | solution.py:47
  15.6 0.7 iota_multiply_fusion
  16.4 1.5 %copy-done.3 = bf16[729,1152]{1,0:T(8,128)(2,1)S(1)} copy-done((bf16[729,1152]{1,0:T(8,128)(2,1)S(1)}, bf16[729,1152]{1,0:T(8,128)(2,1)}, u32[]{:S(2)}) %copy-start.3) | copy-done | bytes 1679640
  17.9 0.8 shard_map.153.normed0_hbm
  18.7 0.6 collective-permute-start.16
  19.4 1.3 collective-permute-start.3
  22.0 0.4 collective-permute-start.7
  22.7 0.6 broadcast_in_dim.10.share_ref
  23.3 9.0 %shard_map.149 = (bf16[729,1152]{1,0:T(8,128)(2,1)}, bf16[729,1152]{1,0:T(8,128)(2,1)}) custom-call(s32[2]{0:T(128)} %pad_add_fusion.place_ref, f32[8,768]{1,0:T(8,128)} %broadcast_in_dim.10.share_ref, bf16[2152,1152]{1,0:T(8,128)(2,1)} %weight_hbm.5, bf16[729,2152]{1,0:T(8,128)(2,1)} %hidden_hbm, bf16[729,1152]{1,0:T(8,128)(2,1)} %cotangent_hbm, ...), custom_call_target="tpu_custom_call" | custom-call | flops 1 | bytes 1 | tf_op jit(solution)/shard_map/pallas_call | solution.py:248
  32.3 0.9 collective-permute-done.3.refs_1_
  33.2 0.3 collective-permute-start.2
  33.5 2.1 %collective-permute-done.2 = s32[32]{0:T(128)S(1)} collective-permute-done((s32[32]{0:T(128)S(1)}, s32[32]{0:T(128)S(1)}, u32[]{:S(2)}, u32[]{:S(2)}) %collective-permute-start.2) | collective-permute-done | bytes 160 | tf_op jit(solution)/shard_map/ppermute | solution.py:47
  35.6 2.0 %collective-permute-start.5 = (bf16[64,1152]{1,0:T(8,128)(2,1)S(1)}, bf16[64,1152]{1,0:T(8,128)(2,1)S(1)}, u32[]{:S(2)}, u32[]{:S(2)}) collective-permute-start(bf16[64,1152]{1,0:T(8,128)(2,1)S(1)} %pad_maximum_fusion.1.refs_0_), channel_id=1, source_target_pairs={{0,2},{2,0},{4,6},{6,4},{8,10},{10,8},{12,14},{14,12},{16,18},{18,... | collective-permute-start | bytes 442376 | tf_op jit(solution)/shard_map/ppermute | solution.py:38
  37.8 1.2 collective-permute-done.6.refs_3_
  39.0 0.6 broadcast_in_dim.11.share_ref
  39.6 1.6 %shard_map.150 = (f32[32,1152]{1,0:T(8,128)S(1)}, bf16[32,1152]{1,0:T(8,128)(2,1)S(1)}, f32[1,1152]{1,0:T(1,128)S(1)}, f32[128,1152]{1,0:T(8,128)S(1)}, bf16[128...) custom-call(s32[2]{0:T(128)S(1)} %copy-done.5, f32[2]{0:T(128)S(1)} %pad_maximum_fusion.3.scalar_ref, ...), custom_call_target="tpu_custom_call" | custom-call | flops 1 | bytes 1 | tf_op jit(solution)/shard_map/pallas_call | solution.py:124
  41.2 0.3 collective-permute-start.8
  41.5 1.4 %collective-permute-done.8 = bf16[128,1152]{1,0:T(8,128)(2,1)S(1)} collective-permute-done((bf16[128,1152]{1,0:T(8,128)(2,1)S(1)}, bf16[128,1152]{1,0:T(8,128)(2,1)S(1)}, u32[]{:S(2)}, u32[]{:S(2)}) %collective-permute-start.8) | collective-permute-done | bytes 294944 | tf_op jit(solution)/shard_map/ppermute | solution.py:38
  42.9 0.7 add_convert_fusion
  43.5 5.4 %collective-permute-start.13 = (bf16[64,1152]{1,0:T(8,128)(2,1)}, bf16[64,1152]{1,0:T(8,128)(2,1)S(1)}, u32[]{:S(2)}, u32[]{:S(2)}) collective-permute-start(bf16[64,1152]{1,0:T(8,128)(2,1)} %add_convert_fusion), channel_id=1, source_target_pairs={{0,248},{2,250},{4,252},{6,254},{8,0},{10,2},{12,4},{14,6},{16,8},... | collective-permute-start | bytes 442376 | tf_op jit(solution)/shard_map/ppermute | solution.py:43
  49.0 1.3 collective-permute-start.14
  50.3 0.3 collective-permute-start.15
  50.5 1.3 collective-permute-start.10
  51.8 8.9 %shard_map.151 = (bf16[729,1152]{1,0:T(8,128)(2,1)}, bf16[729,1152]{1,0:T(8,128)(2,1)}) custom-call(s32[2]{0:T(128)} %pad_add_fusion.place_ref, f32[8,768]{1,0:T(8,128)} %broadcast_in_dim.11.share_ref, bf16[2152,1152]{1,0:T(8,128)(2,1)} %weight_hbm.5, bf16[729,2152]{1,0:T(8,128)(2,1)} %collective-permute-done.11.hidden_tail.hidden_hbm, ...), custom_call_target="tpu_custom_call" | custom-call | flops 1 | bytes 1 | tf_op jit(solution)/shard_map/pallas_call | solution.py:248
  60.8 0.6 copy-done.12
  61.3 1.7 %shard_map.152.pooled0_ref = bf16[1,1152]{1,0:T(2,128)(2,1)} custom-call(s32[2]{0:T(128)} %pad_add_fusion.place_ref, f32[2]{0:T(128)} %copy-done.7, bf16[32,1152]{1,0:T(8,128)(2,1)} %own_ref.1, bf16[32,1152]{1,0:T(8,128)(2,1)} %copy-done.4, f32[1,1152]{1,0:T(1,128)} %copy-done.6, f32[1,1152]{1,0:T(1,128)} %copy-done.12), custom_call_target="tpu_custom_call" | custom-call | tf_op jit(solution)/shard_map/pallas_call | solution.py:161
  63.1 2.5 %collective-permute-start.12 = (bf16[1,1152]{1,0:T(2,128)(2,1)}, bf16[1,1152]{1,0:T(2,128)(2,1)S(1)}, u32[]{:S(2)}, u32[]{:S(2)}) collective-permute-start(bf16[1,1152]{1,0:T(2,128)(2,1)} %shard_map.152.pooled0_ref), channel_id=1, source_target_pairs={{0,2},{2,0},{4,6},{6,4},{8,10},{10,8},{12,14},{14,12},{16,18},{18,... | collective-permute-start | bytes 6920 | tf_op jit(solution)/shard_map/ppermute | solution.py:38
  65.6 0.6 stack.56.targets_ref
  66.2 0.4 collective-permute-done.12.pooled1_ref
  66.6 0.6 copy-done.11
  67.2 12.6 %shard_map.154 = (f32[2,144,640]{2,1,0:T(8,128)}, bf16[2,144,640]{2,1,0:T(8,128)(2,1)}, bf16[2,144,640]{2,1,0:T(8,128)(2,1)}, bf16[2,144,640]{2,1,0:T(8,128)(2,1...) custom-call(s32[2]{0:T(128)} %pad_add_fusion.place_ref, s32[8]{0:T(128)} %stack.56.targets_ref, ...), custom_call_target="tpu_custom_call" | custom-call | flops 1 | bytes 1 | tf_op jit(solution)/shard_map/pallas_call | solution.py:376
  79.8 0.1 fusion.4
  79.9 1.5 %collective-permute-start.17 = (bf16[4,144,512]{2,1,0:T(8,128)(2,1)}, bf16[4,144,512]{2,1,0:T(8,128)(2,1)S(1)}, u32[]{:S(2)}, u32[]{:S(2)}) collective-permute-start(bf16[4,144,512]{2,1,0:T(8,128)(2,1)} %get-tuple-element.92), channel_id=1, source_target_pairs={{0,128},{2,130},{4,132},{6,134},{8,136},{10,138},{12,140},{14,142}... | collective-permute-start | bytes 1769480 | tf_op jit(solution)/shard_map/ppermute | solution.py:38
  81.4 0.2 collective-permute-start.19
  81.6 2.4 %collective-permute-start.20 = (bf16[2,144,640]{2,1,0:T(8,128)(2,1)}, bf16[2,144,640]{2,1,0:T(8,128)(2,1)S(1)}, u32[]{:S(2)}, u32[]{:S(2)}) collective-permute-start(bf16[2,144,640]{2,1,0:T(8,128)(2,1)} %get-tuple-element.100), channel_id=1, source_target_pairs={{0,96},{2,98},{4,100},{6,102},{8,104},{10,106},{12,108},{14,110},{... | collective-permute-start | bytes 1105928 | tf_op jit(solution)/shard_map/ppermute | solution.py:38
  84.2 0.2 multiply_reduce_fusion
  84.4 0.7 divide_convert_fusion
  85.1 11.4 %collective-permute-done.17 = bf16[4,144,512]{2,1,0:T(8,128)(2,1)S(1)} collective-permute-done((bf16[4,144,512]{2,1,0:T(8,128)(2,1)}, bf16[4,144,512]{2,1,0:T(8,128)(2,1)S(1)}, u32[]{:S(2)}, u32[]{:S(2)}) %collective-permute-start.17) | collective-permute-done | bytes 589856 | tf_op jit(solution)/shard_map/ppermute | solution.py:38
  96.5 1.5 %convert_add_fusion = f32[4,144,512]{2,1,0:T(8,128)S(1)} fusion(f32[4,144,512]{2,1,0:T(8,128)} %get-tuple-element.91, bf16[4,144,512]{2,1,0:T(8,128)(2,1)S(1)} %collective-permute-done.17), kind=kLoop, calls=%fused_computation | loop fusion | flops 589824 | bytes 2949120 | tf_op jit(solution)/shard_map/add | solution.py:523
  98.1 1.0 collective-permute-start.25
  99.3 0.7 collective-permute-start.23
  99.9 1.0 collective-permute-done.19
  100.9 1.4 %collective-permute-start.24 = (bf16[144,512]{1,0:T(8,128)(2,1)S(1)}, bf16[144,512]{1,0:T(8,128)(2,1)S(1)}, u32[]{:S(2)}, u32[]{:S(2)}) collective-permute-start(bf16[144,512]{1,0:T(8,128)(2,1)S(1)} %get-tuple-element.120), channel_id=1, source_target_pairs={{0,96},{2,98},{4,100},{6,102},{8,104},{10,106},{12,108},{14,110},{... | collective-permute-start | bytes 442376 | tf_op jit(solution)/shard_map/ppermute | solution.py:38
  102.3 0.2 add_add_fusion
  102.5 1.7 %collective-permute-start.21 = (bf16[144,640]{1,0:T(8,128)(2,1)S(1)}, bf16[144,640]{1,0:T(8,128)(2,1)S(1)}, u32[]{:S(2)}, u32[]{:S(2)}) collective-permute-start(bf16[144,640]{1,0:T(8,128)(2,1)S(1)} %fusion.2), channel_id=1, source_target_pairs={{0,128},{2,130},{4,132},{6,134},{8,136},{10,138},{12,140},{14,142}... | collective-permute-start | bytes 552968 | tf_op jit(solution)/shard_map/ppermute | solution.py:38
  104.3 0.6 collective-permute-done.22
  104.9 4.5 %collective-permute-done.23 = bf16[144,512]{1,0:T(8,128)(2,1)S(1)} collective-permute-done((bf16[144,512]{1,0:T(8,128)(2,1)S(1)}, bf16[144,512]{1,0:T(8,128)(2,1)S(1)}, u32[]{:S(2)}, u32[]{:S(2)}) %collective-permute-start.23) | collective-permute-done | bytes 147488 | tf_op jit(solution)/shard_map/ppermute | solution.py:38
  109.7 0.5 collective-permute-start.26
  110.2 0.2 multiply_reduce_fusion.1
  110.4 4.2 %collective-permute-done.26 = bf16[4,18,1152]{2,1,0:T(8,128)(2,1)S(1)} collective-permute-done((bf16[4,18,1152]{2,1,0:T(8,128)(2,1)S(1)}, bf16[4,18,1152]{2,1,0:T(8,128)(2,1)S(1)}, u32[]{:S(2)}, u32[]{:S(2)}) %collective-permute-start.26) | collective-permute-done | bytes 165920 | tf_op jit(solution)/shard_map/ppermute | solution.py:554
  114.6 4.8 %collective-permute-start.27 = (bf16[18,1152]{1,0:T(8,128)(2,1)S(1)}, bf16[18,1152]{1,0:T(8,128)(2,1)S(1)}, u32[]{:S(2)}, u32[]{:S(2)}) collective-permute-start(bf16[18,1152]{1,0:T(8,128)(2,1)S(1)} %get-tuple-element.122), channel_id=1, source_target_pairs={{0,16},{2,18},{4,20},{6,22},{8,24},{10,26},{12,28},{14,30},{16,0},... | collective-permute-start | bytes 124424 | tf_op jit(solution)/shard_map/ppermute | solution.py:38
  119.4 0.6 collective-permute-start.28
  120.0 3.0 %collective-permute-start.29 = (bf16[18,1152]{1,0:T(8,128)(2,1)S(1)}, bf16[18,1152]{1,0:T(8,128)(2,1)S(1)}, u32[]{:S(2)}, u32[]{:S(2)}) collective-permute-start(bf16[18,1152]{1,0:T(8,128)(2,1)S(1)} %get-tuple-element.123), channel_id=1, source_target_pairs={{0,24},{2,26},{4,28},{6,30},{8,0},{10,2},{12,4},{14,6},{16,8},{18,... | collective-permute-start | bytes 124424 | tf_op jit(solution)/shard_map/ppermute | solution.py:38
  123.2 2.0 %collective-permute-done.28 = bf16[18,1152]{1,0:T(8,128)(2,1)S(1)} collective-permute-done((bf16[18,1152]{1,0:T(8,128)(2,1)S(1)}, bf16[18,1152]{1,0:T(8,128)(2,1)S(1)}, u32[]{:S(2)}, u32[]{:S(2)}) %collective-permute-start.28) | collective-permute-done | bytes 41504 | tf_op jit(solution)/shard_map/ppermute | solution.py:38
  125.2 0.6 collective-permute-done.29
  125.9 0.5 collective-permute-done.30
  126.4 5.7 %collective-permute-start.31 = (f32[9,1152]{1,0:T(8,128)S(1)}, f32[9,1152]{1,0:T(8,128)S(1)}, u32[]{:S(2)}, u32[]{:S(2)}) collective-permute-start(f32[9,1152]{1,0:T(8,128)S(1)} %slice_select_fusion), channel_id=1, source_target_pairs={{0,2},{2,0},{4,6},{6,4},{8,10},{10,8},{12,14},{14,12},{16,18},{18,... | collective-permute-start | bytes 124424 | tf_op jit(solution)/shard_map/ppermute | solution.py:38
  132.1 0.7 maximum_select_fusion
  132.8 0.2 collective-permute-done.31
  133.1 0.7 pad_maximum_fusion.2
  (86 shorter events, 1.8 us)
Async XLA Ops:
  3.0 47.5 %collective-permute-start.11 = (bf16[729,2152]{1,0:T(8,128)(2,1)}, bf16[729,2152]{1,0:T(8,128)(2,1)}, u32[]{:S(2)}, u32[]{:S(2)}) collective-permute-start(bf16[729,2152]{1,0:T(8,128)(2,1)} %hidden_hbm), channel_id=1, source_target_pairs={{0,2},{2,0},{4,6},{6,4},{8,10},{10,8},{12,14},{14,12},{16,18},{18,... | collective-permute-start | bytes 9412856 | tf_op jit(solution)/shard_map/ppermute | solution.py:38
  6.2 12.5 %collective-permute-start = (bf16[32,1152]{1,0:T(8,128)(2,1)}, bf16[32,1152]{1,0:T(8,128)(2,1)S(1)}, u32[]{:S(2)}, u32[]{:S(2)}) collective-permute-start(bf16[32,1152]{1,0:T(8,128)(2,1)} %shard_map.148), channel_id=1, source_target_pairs={{0,4},{2,6},{4,8},{6,10},{8,12},{10,14},{12,16},{14,18},{16,20},{1... | collective-permute-start | bytes 221192 | tf_op jit(solution)/shard_map/ppermute | solution.py:43
  6.2 15.7 %collective-permute-start.4 = (bf16[32,1152]{1,0:T(8,128)(2,1)}, bf16[32,1152]{1,0:T(8,128)(2,1)S(1)}, u32[]{:S(2)}, u32[]{:S(2)}) collective-permute-start(bf16[32,1152]{1,0:T(8,128)(2,1)} %shard_map.148), channel_id=1, source_target_pairs={{2,16},{6,20},{10,24},{14,28},{18,32},{22,36},{26,40},{30,44},{34,... | collective-permute-start | bytes 221192 | tf_op jit(solution)/shard_map/ppermute | solution.py:43
  14.2 5.2 %collective-permute-start.1 = (bf16[32,1152]{1,0:T(8,128)(2,1)}, bf16[32,1152]{1,0:T(8,128)(2,1)S(1)}, u32[]{:S(2)}, u32[]{:S(2)}) collective-permute-start(bf16[32,1152]{1,0:T(8,128)(2,1)} %own_ref.1), channel_id=1, source_target_pairs={{0,1},{1,0},{2,3},{3,2},{4,5},{5,4},{6,7},{7,6},{8,9},{9,8},{10,11... | collective-permute-start | bytes 221192 | tf_op jit(solution)/shard_map/ppermute | solution.py:47
  15.6 27.3 %collective-permute-start.9 = (bf16[729,1152]{1,0:T(8,128)(2,1)}, bf16[729,1152]{1,0:T(8,128)(2,1)}, u32[]{:S(2)}, u32[]{:S(2)}) collective-permute-start(bf16[729,1152]{1,0:T(8,128)(2,1)} %cotangent_hbm), channel_id=1, source_target_pairs={{0,2},{2,0},{4,6},{6,4},{8,10},{10,8},{12,14},{14,12},{16,18},{18,... | collective-permute-start | bytes 5038856 | tf_op jit(solution)/shard_map/ppermute | solution.py:38
  16.4 1.5 %copy-start.3 = (bf16[729,1152]{1,0:T(8,128)(2,1)S(1)}, bf16[729,1152]{1,0:T(8,128)(2,1)}, u32[]{:S(2)}) copy-start(bf16[729,1152]{1,0:T(8,128)(2,1)} %normed_ref) | copy-start | bytes 5038852
  17.9 1.5 %copy-start.10 = (bf16[32,1152]{1,0:T(8,128)(2,1)S(1)}, bf16[32,1152]{1,0:T(8,128)(2,1)}, u32[]{:S(2)}) copy-start(bf16[32,1152]{1,0:T(8,128)(2,1)} %shard_map.148) | copy-start | bytes 221188
  17.9 2.8 %copy-start.14 = (s32[32]{0:T(128)S(1)}, s32[32]{0:T(128)}, u32[]{:S(2)}) copy-start(s32[32]{0:T(128)} %param.17) | copy-start | bytes 388
  17.9 4.1 %copy-start.13 = (f32[729]{0:T(1024)S(1)}, f32[729]{0:T(1024)}, u32[]{:S(2)}) copy-start(f32[729]{0:T(1024)} %param.21) | copy-start | bytes 8752
  18.7 13.6 %copy-start = (bf16[1152,768]{1,0:T(8,128)(2,1)}, bf16[1152,768]{1,0:T(8,128)(2,1)S(1)}, u32[]{:S(2)}) copy-start(bf16[1152,768]{1,0:T(8,128)(2,1)S(1)} %shard_map.153.normed0_hbm) | copy-start | bytes 5308420
  18.7 47.9 %collective-permute-start.16 = (bf16[1152,768]{1,0:T(8,128)(2,1)S(1)}, bf16[1152,768]{1,0:T(8,128)(2,1)}, u32[]{:S(2)}, u32[]{:S(2)}) collective-permute-start(bf16[1152,768]{1,0:T(8,128)(2,1)S(1)} %shard_map.153.normed0_hbm), channel_id=1, source_target_pairs={{0,2},{2,0},{4,6},{6,4},{8,10},{10,8},{12,14},{14,12},{16,18},{18,... | collective-permute-start | bytes 5308424 | tf_op jit(solution)/shard_map/ppermute | solution.py:38
  19.4 20.2 %copy-start.4 = (bf16[32,1152]{1,0:T(8,128)(2,1)}, bf16[32,1152]{1,0:T(8,128)(2,1)S(1)}, u32[]{:S(2)}) copy-start(bf16[32,1152]{1,0:T(8,128)(2,1)S(1)} %collective-permute-done.1.other_ref) | copy-start | bytes 221188
  19.4 13.8 %collective-permute-start.3 = (bf16[64,1152]{1,0:T(8,128)(2,1)S(1)}, bf16[64,1152]{1,0:T(8,128)(2,1)S(1)}, u32[]{:S(2)}, u32[]{:S(2)}) collective-permute-start(bf16[64,1152]{1,0:T(8,128)(2,1)S(1)} %pad_maximum_fusion.1.refs_0_), channel_id=1, source_target_pairs={{0,8},{2,10},{4,12},{6,14},{8,16},{10,18},{12,20},{14,22},{16,24},... | collective-permute-start | bytes 442376 | tf_op jit(solution)/shard_map/ppermute | solution.py:43
  22.0 15.6 %collective-permute-start.7 = (f32[729]{0:T(1024)S(1)}, f32[729]{0:T(1024)S(1)}, u32[]{:S(2)}, u32[]{:S(2)}) collective-permute-start(f32[729]{0:T(1024)S(1)} %copy-done.13), channel_id=1, source_target_pairs={{0,2},{2,0},{4,6},{6,4},{8,10},{10,8},{12,14},{14,12},{16,18},{18,... | collective-permute-start | bytes 8756 | tf_op jit(solution)/shard_map/ppermute | solution.py:38
  22.4 17.1 %copy-start.7 = (f32[2]{0:T(128)}, f32[2]{0:T(128)S(1)}, u32[]{:S(2)}) copy-start(f32[2]{0:T(128)S(1)} %pad_maximum_fusion.3.scalar_ref) | copy-start | bytes 28
  23.3 16.3 %copy-start.1 = (bf16[32,1152]{1,0:T(8,128)(2,1)S(1)}, bf16[32,1152]{1,0:T(8,128)(2,1)}, u32[]{:S(2)}) copy-start(bf16[32,1152]{1,0:T(8,128)(2,1)} %own_ref.1) | copy-start | bytes 221188
  23.3 16.3 %copy-start.5 = (s32[2]{0:T(128)S(1)}, s32[2]{0:T(128)}, u32[]{:S(2)}) copy-start(s32[2]{0:T(128)} %pad_add_fusion.place_ref) | copy-start | bytes 28
  33.2 2.4 %collective-permute-start.2 = (s32[32]{0:T(128)S(1)}, s32[32]{0:T(128)S(1)}, u32[]{:S(2)}, u32[]{:S(2)}) collective-permute-start(s32[32]{0:T(128)S(1)} %copy-done.14), channel_id=1, source_target_pairs={{0,1},{1,0},{2,3},{3,2},{4,5},{5,4},{6,7},{7,6},{8,9},{9,8},{10,11... | collective-permute-start | bytes 392 | tf_op jit(solution)/shard_map/ppermute | solution.py:47
  35.6 4.0 %collective-permute-start.5 = (bf16[64,1152]{1,0:T(8,128)(2,1)S(1)}, bf16[64,1152]{1,0:T(8,128)(2,1)S(1)}, u32[]{:S(2)}, u32[]{:S(2)}) collective-permute-start(bf16[64,1152]{1,0:T(8,128)(2,1)S(1)} %pad_maximum_fusion.1.refs_0_), channel_id=1, source_target_pairs={{0,2},{2,0},{4,6},{6,4},{8,10},{10,8},{12,14},{14,12},{16,18},{18,... | collective-permute-start | bytes 442376 | tf_op jit(solution)/shard_map/ppermute | solution.py:38
  37.6 1.4 %collective-permute-start.6 = (bf16[64,1152]{1,0:T(8,128)(2,1)S(1)}, bf16[64,1152]{1,0:T(8,128)(2,1)S(1)}, u32[]{:S(2)}, u32[]{:S(2)}) collective-permute-start(bf16[64,1152]{1,0:T(8,128)(2,1)S(1)} %collective-permute-done.3.refs_1_), channel_id=1, source_target_pairs={{0,2},{2,0},{4,6},{6,4},{8,10},{10,8},{12,14},{14,12},{16,18},{18,... | collective-permute-start | bytes 442376 | tf_op jit(solution)/shard_map/ppermute | solution.py:38
  41.2 19.6 %copy-start.6 = (f32[1,1152]{1,0:T(1,128)}, f32[1,1152]{1,0:T(1,128)S(1)}, u32[]{:S(2)}) copy-start(f32[1,1152]{1,0:T(1,128)S(1)} %get-tuple-element.75.mine_ref) | copy-start | bytes 13828
  41.2 1.7 %collective-permute-start.8 = (bf16[128,1152]{1,0:T(8,128)(2,1)S(1)}, bf16[128,1152]{1,0:T(8,128)(2,1)S(1)}, u32[]{:S(2)}, u32[]{:S(2)}) collective-permute-start(bf16[128,1152]{1,0:T(8,128)(2,1)S(1)} %get-tuple-element.74), channel_id=1, source_target_pairs={{0,2},{2,0},{4,6},{6,4},{8,10},{10,8},{12,14},{14,12},{16,18},{18,... | collective-permute-start | bytes 884744 | tf_op jit(solution)/shard_map/ppermute | solution.py:38
  43.5 22.6 %collective-permute-start.13 = (bf16[64,1152]{1,0:T(8,128)(2,1)}, bf16[64,1152]{1,0:T(8,128)(2,1)S(1)}, u32[]{:S(2)}, u32[]{:S(2)}) collective-permute-start(bf16[64,1152]{1,0:T(8,128)(2,1)} %add_convert_fusion), channel_id=1, source_target_pairs={{0,248},{2,250},{4,252},{6,254},{8,0},{10,2},{12,4},{14,6},{16,8},... | collective-permute-start | bytes 442376 | tf_op jit(solution)/shard_map/ppermute | solution.py:43
  49.0 17.2 %collective-permute-start.14 = (bf16[32,1152]{1,0:T(8,128)(2,1)S(1)}, bf16[32,1152]{1,0:T(8,128)(2,1)S(1)}, u32[]{:S(2)}, u32[]{:S(2)}) collective-permute-start(bf16[32,1152]{1,0:T(8,128)(2,1)S(1)} %get-tuple-element.83), channel_id=1, source_target_pairs={{0,242},{4,246},{8,250},{12,254},{16,2},{20,6},{24,10},{28,14},{32... | collective-permute-start | bytes 221192 | tf_op jit(solution)/shard_map/ppermute | solution.py:43
  50.3 15.9 %collective-permute-start.15 = (bf16[32,1152]{1,0:T(8,128)(2,1)S(1)}, bf16[32,1152]{1,0:T(8,128)(2,1)S(1)}, u32[]{:S(2)}, u32[]{:S(2)}) collective-permute-start(bf16[32,1152]{1,0:T(8,128)(2,1)S(1)} %get-tuple-element.84), channel_id=1, source_target_pairs={{0,1},{1,0},{2,3},{3,2},{4,5},{5,4},{6,7},{7,6},{8,9},{9,8},{10,11... | collective-permute-start | bytes 221192 | tf_op jit(solution)/shard_map/ppermute | solution.py:47
  50.5 10.2 %collective-permute-start.10 = (f32[1,1152]{1,0:T(1,128)S(1)}, f32[1,1152]{1,0:T(1,128)S(1)}, u32[]{:S(2)}, u32[]{:S(2)}) collective-permute-start(f32[1,1152]{1,0:T(1,128)S(1)} %get-tuple-element.75.mine_ref), channel_id=1, source_target_pairs={{0,1},{1,0},{2,3},{3,2},{4,5},{5,4},{6,7},{7,6},{8,9},{9,8},{10,11... | collective-permute-start | bytes 13832 | tf_op jit(solution)/shard_map/ppermute | solution.py:47
  60.7 0.6 copy-start.12
  63.1 3.5 %collective-permute-start.12 = (bf16[1,1152]{1,0:T(2,128)(2,1)}, bf16[1,1152]{1,0:T(2,128)(2,1)S(1)}, u32[]{:S(2)}, u32[]{:S(2)}) collective-permute-start(bf16[1,1152]{1,0:T(2,128)(2,1)} %shard_map.152.pooled0_ref), channel_id=1, source_target_pairs={{0,2},{2,0},{4,6},{6,4},{8,10},{10,8},{12,14},{14,12},{16,18},{18,... | collective-permute-start | bytes 6920 | tf_op jit(solution)/shard_map/ppermute | solution.py:38
  66.2 13.6 %copy-start.2 = (bf16[32,1152]{1,0:T(8,128)(2,1)S(1)}, bf16[32,1152]{1,0:T(8,128)(2,1)}, u32[]{:S(2)}) copy-start(bf16[32,1152]{1,0:T(8,128)(2,1)} %own_ref.1) | copy-start | bytes 221188
  66.2 17.9 %copy-start.8 = (bf16[64,1152]{1,0:T(8,128)(2,1)S(1)}, bf16[64,1152]{1,0:T(8,128)(2,1)}, u32[]{:S(2)}) copy-start(bf16[64,1152]{1,0:T(8,128)(2,1)} %raw_ref.1) | copy-start | bytes 442372
  66.6 0.6 copy-start.11
  79.9 16.6 %collective-permute-start.17 = (bf16[4,144,512]{2,1,0:T(8,128)(2,1)}, bf16[4,144,512]{2,1,0:T(8,128)(2,1)S(1)}, u32[]{:S(2)}, u32[]{:S(2)}) collective-permute-start(bf16[4,144,512]{2,1,0:T(8,128)(2,1)} %get-tuple-element.92), channel_id=1, source_target_pairs={{0,128},{2,130},{4,132},{6,134},{8,136},{10,138},{12,140},{14,142}... | collective-permute-start | bytes 1769480 | tf_op jit(solution)/shard_map/ppermute | solution.py:38
  81.4 17.9 %collective-permute-start.18 = (bf16[2,144,640]{2,1,0:T(8,128)(2,1)}, bf16[2,144,640]{2,1,0:T(8,128)(2,1)S(1)}, u32[]{:S(2)}, u32[]{:S(2)}) collective-permute-start(bf16[2,144,640]{2,1,0:T(8,128)(2,1)} %get-tuple-element.98), channel_id=1, source_target_pairs={{0,64},{2,66},{4,68},{6,70},{8,72},{10,74},{12,76},{14,78},{16,80}... | collective-permute-start | bytes 1105928 | tf_op jit(solution)/shard_map/ppermute | solution.py:38
  81.4 19.5 %collective-permute-start.19 = (bf16[2,144,640]{2,1,0:T(8,128)(2,1)}, bf16[2,144,640]{2,1,0:T(8,128)(2,1)S(1)}, u32[]{:S(2)}, u32[]{:S(2)}) collective-permute-start(bf16[2,144,640]{2,1,0:T(8,128)(2,1)} %get-tuple-element.99), channel_id=1, source_target_pairs={{0,32},{2,34},{4,36},{6,38},{8,40},{10,42},{12,44},{14,46},{16,48}... | collective-permute-start | bytes 1105928 | tf_op jit(solution)/shard_map/ppermute | solution.py:38
  81.6 20.7 %collective-permute-start.20 = (bf16[2,144,640]{2,1,0:T(8,128)(2,1)}, bf16[2,144,640]{2,1,0:T(8,128)(2,1)S(1)}, u32[]{:S(2)}, u32[]{:S(2)}) collective-permute-start(bf16[2,144,640]{2,1,0:T(8,128)(2,1)} %get-tuple-element.100), channel_id=1, source_target_pairs={{0,96},{2,98},{4,100},{6,102},{8,104},{10,106},{12,108},{14,110},{... | collective-permute-start | bytes 1105928 | tf_op jit(solution)/shard_map/ppermute | solution.py:38
  98.0 4.3 %copy-start.9 = (f32[2,144,640]{2,1,0:T(8,128)S(1)}, f32[2,144,640]{2,1,0:T(8,128)}, u32[]{:S(2)}) copy-start(f32[2,144,640]{2,1,0:T(8,128)} %get-tuple-element.97) | copy-start | bytes 2211844
  98.1 11.5 %collective-permute-start.25 = (bf16[32,1152]{1,0:T(8,128)(2,1)S(1)}, bf16[32,1152]{1,0:T(8,128)(2,1)S(1)}, u32[]{:S(2)}, u32[]{:S(2)}) collective-permute-start(bf16[32,1152]{1,0:T(8,128)(2,1)S(1)} %slice.106), channel_id=1, source_target_pairs={{0,252},{2,254},{4,0},{6,2},{8,4},{10,6},{12,8},{14,10},{16,12},{1... | collective-permute-start | bytes 221192 | tf_op jit(solution)/shard_map/ppermute | solution.py:43
  99.2 5.7 %collective-permute-start.22 = (bf16[144,512]{1,0:T(8,128)(2,1)S(1)}, bf16[144,512]{1,0:T(8,128)(2,1)S(1)}, u32[]{:S(2)}, u32[]{:S(2)}) collective-permute-start(bf16[144,512]{1,0:T(8,128)(2,1)S(1)} %get-tuple-element.119), channel_id=1, source_target_pairs={{0,64},{2,66},{4,68},{6,70},{8,72},{10,74},{12,76},{14,78},{16,80}... | collective-permute-start | bytes 442376 | tf_op jit(solution)/shard_map/ppermute | solution.py:38
  99.3 10.1 %collective-permute-start.23 = (bf16[144,512]{1,0:T(8,128)(2,1)S(1)}, bf16[144,512]{1,0:T(8,128)(2,1)S(1)}, u32[]{:S(2)}, u32[]{:S(2)}) collective-permute-start(bf16[144,512]{1,0:T(8,128)(2,1)S(1)} %get-tuple-element.121), channel_id=1, source_target_pairs={{0,32},{2,34},{4,36},{6,38},{8,40},{10,42},{12,44},{14,46},{16,48}... | collective-permute-start | bytes 442376 | tf_op jit(solution)/shard_map/ppermute | solution.py:38
  100.9 8.4 %collective-permute-start.24 = (bf16[144,512]{1,0:T(8,128)(2,1)S(1)}, bf16[144,512]{1,0:T(8,128)(2,1)S(1)}, u32[]{:S(2)}, u32[]{:S(2)}) collective-permute-start(bf16[144,512]{1,0:T(8,128)(2,1)S(1)} %get-tuple-element.120), channel_id=1, source_target_pairs={{0,96},{2,98},{4,100},{6,102},{8,104},{10,106},{12,108},{14,110},{... | collective-permute-start | bytes 442376 | tf_op jit(solution)/shard_map/ppermute | solution.py:38
  102.5 6.9 %collective-permute-start.21 = (bf16[144,640]{1,0:T(8,128)(2,1)S(1)}, bf16[144,640]{1,0:T(8,128)(2,1)S(1)}, u32[]{:S(2)}, u32[]{:S(2)}) collective-permute-start(bf16[144,640]{1,0:T(8,128)(2,1)S(1)} %fusion.2), channel_id=1, source_target_pairs={{0,128},{2,130},{4,132},{6,134},{8,136},{10,138},{12,140},{14,142}... | collective-permute-start | bytes 552968 | tf_op jit(solution)/shard_map/ppermute | solution.py:38
  109.7 4.9 %collective-permute-start.26 = (bf16[4,18,1152]{2,1,0:T(8,128)(2,1)S(1)}, bf16[4,18,1152]{2,1,0:T(8,128)(2,1)S(1)}, u32[]{:S(2)}, u32[]{:S(2)}) collective-permute-start(bf16[4,18,1152]{2,1,0:T(8,128)(2,1)S(1)} %fusion.1), channel_id=1, source_target_pairs={{0,4},{2,6},{4,0},{6,2},{8,12},{10,14},{12,8},{14,10},{16,20},{18,... | collective-permute-start | bytes 497672 | tf_op jit(solution)/shard_map/ppermute | solution.py:554
  114.6 8.6 %collective-permute-start.27 = (bf16[18,1152]{1,0:T(8,128)(2,1)S(1)}, bf16[18,1152]{1,0:T(8,128)(2,1)S(1)}, u32[]{:S(2)}, u32[]{:S(2)}) collective-permute-start(bf16[18,1152]{1,0:T(8,128)(2,1)S(1)} %get-tuple-element.122), channel_id=1, source_target_pairs={{0,16},{2,18},{4,20},{6,22},{8,24},{10,26},{12,28},{14,30},{16,0},... | collective-permute-start | bytes 124424 | tf_op jit(solution)/shard_map/ppermute | solution.py:38
  119.4 5.8 %collective-permute-start.28 = (bf16[18,1152]{1,0:T(8,128)(2,1)S(1)}, bf16[18,1152]{1,0:T(8,128)(2,1)S(1)}, u32[]{:S(2)}, u32[]{:S(2)}) collective-permute-start(bf16[18,1152]{1,0:T(8,128)(2,1)S(1)} %get-tuple-element.124), channel_id=1, source_target_pairs={{0,8},{2,10},{4,12},{6,14},{8,16},{10,18},{12,20},{14,22},{16,24},... | collective-permute-start | bytes 124424 | tf_op jit(solution)/shard_map/ppermute | solution.py:38
  120.0 5.9 %collective-permute-start.29 = (bf16[18,1152]{1,0:T(8,128)(2,1)S(1)}, bf16[18,1152]{1,0:T(8,128)(2,1)S(1)}, u32[]{:S(2)}, u32[]{:S(2)}) collective-permute-start(bf16[18,1152]{1,0:T(8,128)(2,1)S(1)} %get-tuple-element.123), channel_id=1, source_target_pairs={{0,24},{2,26},{4,28},{6,30},{8,0},{10,2},{12,4},{14,6},{16,8},{18,... | collective-permute-start | bytes 124424 | tf_op jit(solution)/shard_map/ppermute | solution.py:38
  123.1 3.3 %collective-permute-start.30 = (bf16[32,1152]{1,0:T(8,128)(2,1)S(1)}, bf16[32,1152]{1,0:T(8,128)(2,1)S(1)}, u32[]{:S(2)}, u32[]{:S(2)}) collective-permute-start(bf16[32,1152]{1,0:T(8,128)(2,1)S(1)} %divide_convert_fusion.1), channel_id=1, source_target_pairs={{0,1},{1,0},{2,3},{3,2},{4,5},{5,4},{6,7},{7,6},{8,9},{9,8},{10,11... | collective-permute-start | bytes 221192 | tf_op jit(solution)/shard_map/ppermute | solution.py:47
  126.4 6.6 %collective-permute-start.31 = (f32[9,1152]{1,0:T(8,128)S(1)}, f32[9,1152]{1,0:T(8,128)S(1)}, u32[]{:S(2)}, u32[]{:S(2)}) collective-permute-start(f32[9,1152]{1,0:T(8,128)S(1)} %slice_select_fusion), channel_id=1, source_target_pairs={{0,2},{2,0},{4,6},{6,4},{8,10},{10,8},{12,14},{14,12},{16,18},{18,... | collective-permute-start | bytes 124424 | tf_op jit(solution)/shard_map/ppermute | solution.py:38
where the time goes:
time: 134 us
  starting transfers between devices  51.9 us (39%)
  Pallas kernels  36.3 us (27%)
  waiting for transfers between devices  31 us (23%)
  other arithmetic  7.23 us (5%)
  local copies, waits for them, and re-layouts  5.06 us (4%)
  between operations  2.34 us (2%)
    ppermute x20, starting transfers between devices, torus_send(): return lax.ppermute(array, 'dp', torus_pairs(**shift))  31.1 us
    ppermute x20, waiting for transfers between devices, torus_send(): return lax.ppermute(array, 'dp', torus_pairs(**shift))  23.3 us
    pallas_call x2, Pallas kernels, hidden_base(): pl.pallas_call(base_kernel, grid_spec=pltpu.PrefetchScalarGridSpec(num_sc...  17.9 us
    ppermute x6, starting transfers between devices, ring_send(): return lax.ppermute(array, 'dp', pairs)  16.9 us
    pallas_call x1, Pallas kernels, up_terms(): pl.pallas_call(terms_kernel, grid_spec=pltpu.PrefetchScalarGridSpec(num_s...  12.6 us
    ppermute x1, waiting for transfers between devices, per_device(): chunks = chunks + lax.ppermute(chunk, 'dp', swap_pairs).astype(f32)  4.18 us
    ppermute x5, starting transfers between devices, tensor_swap(): return lax.ppermute(array, 'tensor', [(0, 1), (1, 0)])  3.34 us
  transfers between devices with their start and end apart: 32, of which 14 were waited for; matrix products, arithmetic and copies ran while one was open for 6% of the time, Pallas kernels for 16%

commit v1 on v0

--- a/solution.py
+++ b/solution.py
@@ -13,6 +13,7 @@
 N_TENSOR = 2
 LANES = 128
 LIGHT = pl.CostEstimate(flops=1, bytes_accessed=1, transcendentals=0)
+HEAVY = pl.CostEstimate(flops=10**10, bytes_accessed=1, transcendentals=0)
 
 epsilon = 1e-06
 gelu_root = 0.7978845608028654
@@ -239,7 +240,7 @@
         copy.wait()
 
 
-def hidden_base(place, columns, cotangent, share, weight, hidden):
+def hidden_base(place, columns, cotangent, share, weight, hidden, cost):
     patches, width = cotangent.shape
     start = columns - LANES
     tiles = start // LANES
@@ -270,7 +271,7 @@
         ),
         out_shape=[out, out],
         compiler_params=pltpu.CompilerParams(vmem_limit_bytes=60 * 2**20),
-        cost_estimate=LIGHT,
+        cost_estimate=cost,
     )(place, share, weight, hidden, cotangent, weight, hidden)
 
 
@@ -442,7 +443,10 @@
     text_far = ring_send(text_half, 7, only=1)
     text_near = jnp.concatenate([text_half, ring_send(text_half, 2)], axis=0)
     image_other = tensor_swap(image_raw)
-    text_near, image_other, cotangent_own = lax.optimization_barrier((text_near, image_other, head_cotangent))
+    text_near, image_other, cotangent_own, offset_sent = lax.optimization_barrier(
+        (text_near, image_other, head_cotangent, pair_offset)
+    )
+    offset_other = tensor_swap(offset_sent)
     text_next = ring_send(text_near, 4)
     rels = jnp.concatenate(
         [
@@ -455,11 +459,6 @@
     text_value = (text_row[None, :] - text_rows * rels[:, None]).reshape(-1)
     text_valid = jnp.repeat((rels >= 0) & (rels < WINDOW), half)
 
-    offset_other = tensor_swap(pair_offset)
-    row = jnp.arange(image_rows, dtype=jnp.int32)
-    own_row = row + tensor_index * image_rows
-    other_row = row + (1 - tensor_index) * image_rows
-    image_value = jnp.concatenate([own_row - pair_offset, other_row - offset_other])
 
     columns = 9 * LANES
     start = 8 * LANES
@@ -471,15 +470,24 @@
         for part in (pool_share, share_other)
     ]
     base_own, slope_own = hidden_base(
-        spot, columns, cotangent_own, share_own, down_weight, hidden_pre
-    )
-    text_next, text_far, base_own, slope_own = lax.optimization_barrier((text_next, text_far, base_own, slope_own))
+        spot, columns, cotangent_own, share_own, down_weight, hidden_pre, HEAVY
+    )
+    text_next, text_far, base_own, slope_own, offset_other = lax.optimization_barrier(
+        (text_next, text_far, base_own, slope_own, offset_other)
+    )
     text_window = [text_near, text_next, torus_send(text_near, core=1), torus_send(text_next, core=1), text_far]
     normed_own = transposed(normed_patches, 6 * LANES)
     normed_other = torus_send(normed_own, core=1)
 
     text_last = text_window[3]
-    text_last, share_other = lax.optimization_barrier((text_last, share_other))
+    row = jnp.arange(image_rows, dtype=jnp.int32)
+    own_row = row + tensor_index * image_rows
+    other_row = row + (1 - tensor_index) * image_rows
+    image_value = jnp.concatenate([own_row - pair_offset, other_row - offset_other])
+    targets = jnp.stack(
+        [(yh + dy) % N_YH * N_X + (x + dx) % N_X for dy in range(N_YH) for dx in range(N_X)]
+    ).astype(jnp.int32)
+    text_last, share_other, targets = lax.optimization_barrier((text_last, share_other, targets))
     text_window[3] = text_last
     image_part, image_swapped, zero_row, text_own, text_sibling, far = pair_products(
         spot, scalars, image_value, text_value, text_valid, image_raw, image_other, text_window
@@ -488,25 +496,19 @@
 
     near = 2 * half
     returned = torus_send(text_sibling, core=1)
-    far = ring_send(far, -7, only=0)
     image_swapped = tensor_swap(image_swapped)
     zero_row, returned, cotangent_other = lax.optimization_barrier((zero_row, returned, cotangent_other))
     text_next = ring_send((text_own[near:] + returned[near:].astype(f32)).astype(bf16), -4)
 
     base_other, slope_other = hidden_base(
-        spot, columns, cotangent_other, share_other, down_weight, hidden_other
+        spot, columns, cotangent_other, share_other, down_weight, hidden_other, LIGHT
     )
     zero_theirs, base_other, slope_other = lax.optimization_barrier((zero_theirs, base_other, slope_other))
     pooled = pooled_row(spot, scalars, image_raw, image_other, zero_row, zero_theirs)
     pooled_other = torus_send(pooled, core=1)
-    pooled_other, text_next, far, image_swapped = lax.optimization_barrier(
-        (pooled_other, text_next, far, image_swapped)
-    )
+    pooled_other, text_next, image_swapped = lax.optimization_barrier((pooled_other, text_next, image_swapped))
 
     split = 5 * LANES
-    targets = jnp.stack(
-        [(yh + dy) % N_YH * N_X + (x + dx) % N_X for dy in range(N_YH) for dx in range(N_X)]
-    ).astype(jnp.int32)
     a_keep, a_sent1, a_sent2, a_sent3, c_keep, c_sent = up_terms(
         spot,
         targets,
@@ -521,9 +523,10 @@
     c_come = torus_send(c_sent, yh=1)
     a_come = [torus_send(part, x=dx) for dx, part in ((2, a_sent2), (1, a_sent1), (3, a_sent3))]
     c_keep = c_keep + c_come.astype(f32)
-    c_keep, a_keep, text_own, returned, text_next = lax.optimization_barrier(
-        (c_keep, a_keep, text_own, returned, text_next)
-    )
+    c_keep, a_keep, text_own, returned, text_next, far = lax.optimization_barrier(
+        (c_keep, a_keep, text_own, returned, text_next, far)
+    )
+    far = ring_send(far, -7, only=0)
     a_keep = a_keep + (a_come[0].astype(f32) + a_come[1].astype(f32) + a_come[2].astype(f32))
     c_come = [torus_send(c_keep[dx].astype(bf16), x=dx) for dx in (2, 1, 3)]
     a_come = torus_send(a_keep[1].astype(bf16), yh=1)

time: 134 us -> 127 us (0.948)
  starting transfers between devices: 51.9 us -> 45.4 us
    ppermute x20, starting transfers between devices: 31.1 us -> 21.6 us  [torus_send(): return lax.ppermute(array, 'dp', torus_pairs(**shift))]
    ppermute x6, waiting for transfers between devices: 0.9 us -> 6.51 us  [ring_send(): return lax.ppermute(array, 'dp', pairs)]
    ppermute x1, waiting for transfers between devices: 4.18 us -> 0.81 us  [per_device(): chunks = chunks + lax.ppermute(chunk, 'dp', swap_pairs).astype(f32)]
    ppermute x6, starting transfers between devices: 16.9 us -> 19.6 us  [ring_send(): return lax.ppermute(array, 'dp', pairs)]
    ppermute x5, waiting for transfers between devices: 2.6 us -> 0.52 us  [tensor_swap(): return lax.ppermute(array, 'tensor', [(0, 1), (1, 0)])]
    unnamed x30 -> x34, local copies, waits for them, and re-layouts: 2.68 us -> 2.69 us
  transfers between devices with their start and end apart: 32 -> 32, of which waited for: 14 -> 14; matrix products, arithmetic and copies ran while one was open for 6% -> 6% of each run, Pallas kernels for 16% -> 17%
where the time goes in v1:
time: 127 us
  starting transfers between devices  45.4 us (36%)
  Pallas kernels  36.3 us (29%)
  waiting for transfers between devices  30 us (24%)
  other arithmetic  7.17 us (6%)
  local copies, waits for them, and re-layouts  5.26 us (4%)
  between operations  2.44 us (2%)
    ppermute x20, waiting for transfers between devices, torus_send(): return lax.ppermute(array, 'dp', torus_pairs(**shift))  22.2 us
    ppermute x20, starting transfers between devices, torus_send(): return lax.ppermute(array, 'dp', torus_pairs(**shift))  21.6 us
    ppermute x6, starting transfers between devices, ring_send(): return lax.ppermute(array, 'dp', pairs)  19.6 us
    pallas_call x2, Pallas kernels, hidden_base(): pl.pallas_call(base_kernel, grid_spec=pltpu.PrefetchScalarGridSpec(num_sc...  17.9 us
    pallas_call x1, Pallas kernels, up_terms(): pl.pallas_call(terms_kernel, grid_spec=pltpu.PrefetchScalarGridSpec(num_s...  12.6 us
    ppermute x6, waiting for transfers between devices, ring_send(): return lax.ppermute(array, 'dp', pairs)  6.51 us
    ppermute x5, starting transfers between devices, tensor_swap(): return lax.ppermute(array, 'tensor', [(0, 1), (1, 0)])  3.35 us
    unnamed x34, local copies, waits for them, and re-layouts  2.69 us
  transfers between devices with their start and end apart: 32, of which 14 were waited for; matrix products, arithmetic and copies ran while one was open for 6% of the time, Pallas kernels for 17%

profile of v1, /device:TPU:1, one launch (start us, length us, event | category | flops | bytes accessed | tf_op | source)
XLA Modules:
  0.0 126.6 jit_solution(61638873304587793)
XLA Ops:
  0.6 0.6 pad_add_fusion.place_ref
  1.3 1.7 %shard_map.148 = bf16[32,1152]{1,0:T(8,128)(2,1)} custom-call(s32[2]{0:T(128)} %pad_add_fusion.place_ref, bf16[64,1152]{1,0:T(8,128)(2,1)} %raw_ref.1), custom_call_target="tpu_custom_call" | custom-call | tf_op jit(solution)/shard_map/pallas_call | solution.py:87
  2.9 2.5 %collective-permute-start = (bf16[32,1152]{1,0:T(8,128)(2,1)}, bf16[32,1152]{1,0:T(8,128)(2,1)S(1)}, u32[]{:S(2)}, u32[]{:S(2)}) collective-permute-start(bf16[32,1152]{1,0:T(8,128)(2,1)} %shard_map.148), channel_id=1, source_target_pairs={{0,4},{2,6},{4,8},{6,10},{8,12},{10,14},{12,16},{14,18},{16,20},{1... | collective-permute-start | bytes 221192 | tf_op jit(solution)/shard_map/ppermute | solution.py:44
  5.4 8.7 %collective-permute-start.3 = (bf16[32,1152]{1,0:T(8,128)(2,1)}, bf16[32,1152]{1,0:T(8,128)(2,1)S(1)}, u32[]{:S(2)}, u32[]{:S(2)}) collective-permute-start(bf16[32,1152]{1,0:T(8,128)(2,1)} %shard_map.148), channel_id=1, source_target_pairs={{2,16},{6,20},{10,24},{14,28},{18,32},{22,36},{26,40},{30,44},{34,... | collective-permute-start | bytes 221192 | tf_op jit(solution)/shard_map/ppermute | solution.py:44
  14.1 1.4 %collective-permute-start.1 = (bf16[32,1152]{1,0:T(8,128)(2,1)}, bf16[32,1152]{1,0:T(8,128)(2,1)S(1)}, u32[]{:S(2)}, u32[]{:S(2)}) collective-permute-start(bf16[32,1152]{1,0:T(8,128)(2,1)} %own_ref.1), channel_id=1, source_target_pairs={{0,1},{1,0},{2,3},{3,2},{4,5},{5,4},{6,7},{7,6},{8,9},{9,8},{10,11... | collective-permute-start | bytes 221192 | tf_op jit(solution)/shard_map/ppermute | solution.py:48
  15.5 0.5 collective-permute-start.11
  16.0 0.7 fusion.12
  16.7 0.7 iota_multiply_fusion
  18.9 1.5 %copy-done.3 = bf16[729,1152]{1,0:T(8,128)(2,1)S(1)} copy-done((bf16[729,1152]{1,0:T(8,128)(2,1)S(1)}, bf16[729,1152]{1,0:T(8,128)(2,1)}, u32[]{:S(2)}) %copy-start.3) | copy-done | bytes 1679640
  20.4 0.9 shard_map.153.normed0_hbm
  21.6 0.8 stack.56.targets_ref
  22.4 0.5 collective-permute-start.15
  22.9 1.3 %collective-permute-start.2 = (bf16[64,1152]{1,0:T(8,128)(2,1)S(1)}, bf16[64,1152]{1,0:T(8,128)(2,1)S(1)}, u32[]{:S(2)}, u32[]{:S(2)}) collective-permute-start(bf16[64,1152]{1,0:T(8,128)(2,1)S(1)} %pad_maximum_fusion.1.refs_0_), channel_id=1, source_target_pairs={{0,8},{2,10},{4,12},{6,14},{8,16},{10,18},{12,20},{14,22},{16,24},... | collective-permute-start | bytes 442376 | tf_op jit(solution)/shard_map/ppermute | solution.py:44
  24.2 0.2 collective-permute-start.4
  24.4 0.6 broadcast_in_dim.8.share_ref
  25.0 9.0 %shard_map.149 = (bf16[729,1152]{1,0:T(8,128)(2,1)}, bf16[729,1152]{1,0:T(8,128)(2,1)}) custom-call(s32[2]{0:T(128)} %pad_add_fusion.place_ref, f32[8,768]{1,0:T(8,128)} %broadcast_in_dim.8.share_ref, bf16[2152,1152]{1,0:T(8,128)(2,1)} %weight_hbm.5, bf16[729,2152]{1,0:T(8,128)(2,1)} %hidden_hbm, bf16[729,1152]{1,0:T(8,128)(2,1)} %cotangent_hbm, ...), custom_call_target="tpu_custom_call" | custom-call | flops 10000000000 | bytes 1 | tf_op jit(solution)/shard_map/pallas_call | solution.py:249
  34.1 0.7 collective-permute-start.7
  34.8 1.9 %collective-permute-done.2.refs_1_ = bf16[64,1152]{1,0:T(8,128)(2,1)S(1)} collective-permute-done((bf16[64,1152]{1,0:T(8,128)(2,1)S(1)}, bf16[64,1152]{1,0:T(8,128)(2,1)S(1)}, u32[]{:S(2)}, u32[]{:S(2)}) %collective-permute-start.2) | collective-permute-done | bytes 147488 | tf_op jit(solution)/shard_map/ppermute | solution.py:44
  36.7 0.9 collective-permute-start.5
  37.7 0.1 copy.18.value_ref
  37.8 0.8 collective-permute-done.5.refs_3_
  38.6 0.6 broadcast_in_dim.9.share_ref
  39.3 1.6 %shard_map.150 = (f32[32,1152]{1,0:T(8,128)S(1)}, bf16[32,1152]{1,0:T(8,128)(2,1)S(1)}, f32[1,1152]{1,0:T(1,128)S(1)}, f32[128,1152]{1,0:T(8,128)S(1)}, bf16[128...) custom-call(s32[2]{0:T(128)S(1)} %copy-done.5, f32[2]{0:T(128)S(1)} %pad_maximum_fusion.3.scalar_ref, ...), custom_call_target="tpu_custom_call" | custom-call | flops 1 | bytes 1 | tf_op jit(solution)/shard_map/pallas_call | solution.py:125
  40.8 0.6 collective-permute-start.8
  41.5 1.2 collective-permute-done.8
  42.7 5.1 %collective-permute-start.13 = (bf16[64,1152]{1,0:T(8,128)(2,1)S(1)}, bf16[64,1152]{1,0:T(8,128)(2,1)S(1)}, u32[]{:S(2)}, u32[]{:S(2)}) collective-permute-start(bf16[64,1152]{1,0:T(8,128)(2,1)S(1)} %add_convert_fusion), channel_id=1, source_target_pairs={{0,248},{2,250},{4,252},{6,254},{8,0},{10,2},{12,4},{14,6},{16,8},... | collective-permute-start | bytes 442376 | tf_op jit(solution)/shard_map/ppermute | solution.py:44
  47.9 1.4 %collective-permute-start.10 = (f32[1,1152]{1,0:T(1,128)S(1)}, f32[1,1152]{1,0:T(1,128)S(1)}, u32[]{:S(2)}, u32[]{:S(2)}) collective-permute-start(f32[1,1152]{1,0:T(1,128)S(1)} %get-tuple-element.81.mine_ref), channel_id=1, source_target_pairs={{0,1},{1,0},{2,3},{3,2},{4,5},{5,4},{6,7},{7,6},{8,9},{9,8},{10,11... | collective-permute-start | bytes 13832 | tf_op jit(solution)/shard_map/ppermute | solution.py:48
  49.3 8.9 %shard_map.151 = (bf16[729,1152]{1,0:T(8,128)(2,1)}, bf16[729,1152]{1,0:T(8,128)(2,1)}) custom-call(s32[2]{0:T(128)} %pad_add_fusion.place_ref, f32[8,768]{1,0:T(8,128)} %broadcast_in_dim.9.share_ref, bf16[2152,1152]{1,0:T(8,128)(2,1)} %weight_hbm.5, bf16[729,2152]{1,0:T(8,128)(2,1)} %collective-permute-done.11.hidden_tail.hidden_hbm, ...), custom_call_target="tpu_custom_call" | custom-call | flops 1 | bytes 1 | tf_op jit(solution)/shard_map/pallas_call | solution.py:249
  58.3 0.6 copy-done.14
  58.8 1.7 %shard_map.152.pooled0_ref = bf16[1,1152]{1,0:T(2,128)(2,1)} custom-call(s32[2]{0:T(128)} %pad_add_fusion.place_ref, f32[2]{0:T(128)} %copy-done.7, bf16[32,1152]{1,0:T(8,128)(2,1)} %own_ref.1, bf16[32,1152]{1,0:T(8,128)(2,1)} %copy-done.4, f32[1,1152]{1,0:T(1,128)} %copy-done.6, f32[1,1152]{1,0:T(1,128)} %copy-done.14), custom_call_target="tpu_custom_call" | custom-call | tf_op jit(solution)/shard_map/pallas_call | solution.py:162
  60.6 1.0 collective-permute-start.12
  61.6 1.0 collective-permute-done.12.pooled1_ref
  62.6 0.6 copy-done.13
  63.2 12.6 %shard_map.154 = (f32[2,144,640]{2,1,0:T(8,128)}, bf16[2,144,640]{2,1,0:T(8,128)(2,1)}, bf16[2,144,640]{2,1,0:T(8,128)(2,1)}, bf16[2,144,640]{2,1,0:T(8,128)(2,1...) custom-call(s32[2]{0:T(128)} %pad_add_fusion.place_ref, s32[8]{0:T(128)} %stack.56.targets_ref, ...), custom_call_target="tpu_custom_call" | custom-call | flops 1 | bytes 1 | tf_op jit(solution)/shard_map/pallas_call | solution.py:377
  75.8 0.1 fusion.4
  76.0 2.3 %collective-permute-start.16 = (bf16[4,144,512]{2,1,0:T(8,128)(2,1)}, bf16[4,144,512]{2,1,0:T(8,128)(2,1)S(1)}, u32[]{:S(2)}, u32[]{:S(2)}) collective-permute-start(bf16[4,144,512]{2,1,0:T(8,128)(2,1)} %get-tuple-element.97), channel_id=1, source_target_pairs={{0,128},{2,130},{4,132},{6,134},{8,136},{10,138},{12,140},{14,142}... | collective-permute-start | bytes 1769480 | tf_op jit(solution)/shard_map/ppermute | solution.py:39
  78.2 2.7 %collective-permute-start.19 = (bf16[2,144,640]{2,1,0:T(8,128)(2,1)}, bf16[2,144,640]{2,1,0:T(8,128)(2,1)S(1)}, u32[]{:S(2)}, u32[]{:S(2)}) collective-permute-start(bf16[2,144,640]{2,1,0:T(8,128)(2,1)} %get-tuple-element.106), channel_id=1, source_target_pairs={{0,96},{2,98},{4,100},{6,102},{8,104},{10,106},{12,108},{14,110},{... | collective-permute-start | bytes 1105928 | tf_op jit(solution)/shard_map/ppermute | solution.py:39
  80.9 0.1 fusion.3
  81.0 0.2 multiply_reduce_fusion
  81.3 0.7 divide_convert_fusion
  82.0 10.3 %collective-permute-done.16 = bf16[4,144,512]{2,1,0:T(8,128)(2,1)S(1)} collective-permute-done((bf16[4,144,512]{2,1,0:T(8,128)(2,1)}, bf16[4,144,512]{2,1,0:T(8,128)(2,1)S(1)}, u32[]{:S(2)}, u32[]{:S(2)}) %collective-permute-start.16) | collective-permute-done | bytes 589856 | tf_op jit(solution)/shard_map/ppermute | solution.py:39
  92.3 1.5 %convert_add_fusion = f32[4,144,512]{2,1,0:T(8,128)S(1)} fusion(f32[4,144,512]{2,1,0:T(8,128)} %get-tuple-element.96, bf16[4,144,512]{2,1,0:T(8,128)(2,1)S(1)} %collective-permute-done.16), kind=kLoop, calls=%fused_computation | loop fusion | flops 589824 | bytes 2949120 | tf_op jit(solution)/shard_map/add | solution.py:525
  93.9 0.8 collective-permute-start.24
  95.0 2.8 %collective-permute-done.18 = bf16[2,144,640]{2,1,0:T(8,128)(2,1)S(1)} collective-permute-done((bf16[2,144,640]{2,1,0:T(8,128)(2,1)}, bf16[2,144,640]{2,1,0:T(8,128)(2,1)S(1)}, u32[]{:S(2)}, u32[]{:S(2)}) %collective-permute-start.18) | collective-permute-done | bytes 368672 | tf_op jit(solution)/shard_map/ppermute | solution.py:39
  97.8 0.2 add_add_fusion
  98.0 2.5 %collective-permute-start.20 = (bf16[144,640]{1,0:T(8,128)(2,1)S(1)}, bf16[144,640]{1,0:T(8,128)(2,1)S(1)}, u32[]{:S(2)}, u32[]{:S(2)}) collective-permute-start(bf16[144,640]{1,0:T(8,128)(2,1)S(1)} %fusion.2), channel_id=1, source_target_pairs={{0,128},{2,130},{4,132},{6,134},{8,136},{10,138},{12,140},{14,142}... | collective-permute-start | bytes 552968 | tf_op jit(solution)/shard_map/ppermute | solution.py:39
  100.5 1.3 %collective-permute-start.29 = (bf16[32,1152]{1,0:T(8,128)(2,1)S(1)}, bf16[32,1152]{1,0:T(8,128)(2,1)S(1)}, u32[]{:S(2)}, u32[]{:S(2)}) collective-permute-start(bf16[32,1152]{1,0:T(8,128)(2,1)S(1)} %get-tuple-element.113), channel_id=1, source_target_pairs={{0,242},{4,246},{8,250},{12,254},{16,2},{20,6},{24,10},{28,14},{32... | collective-permute-start | bytes 221192 | tf_op jit(solution)/shard_map/ppermute | solution.py:44
  101.8 3.0 %collective-permute-done.22 = bf16[144,512]{1,0:T(8,128)(2,1)S(1)} collective-permute-done((bf16[144,512]{1,0:T(8,128)(2,1)S(1)}, bf16[144,512]{1,0:T(8,128)(2,1)S(1)}, u32[]{:S(2)}, u32[]{:S(2)}) %collective-permute-start.22) | collective-permute-done | bytes 147488 | tf_op jit(solution)/shard_map/ppermute | solution.py:39
  105.1 0.8 collective-permute-start.25
  106.0 4.6 %collective-permute-done.29 = bf16[32,1152]{1,0:T(8,128)(2,1)S(1)} collective-permute-done((bf16[32,1152]{1,0:T(8,128)(2,1)S(1)}, bf16[32,1152]{1,0:T(8,128)(2,1)S(1)}, u32[]{:S(2)}, u32[]{:S(2)}) %collective-permute-start.29) | collective-permute-done | bytes 73760 | tf_op jit(solution)/shard_map/ppermute | solution.py:44
  110.5 0.2 multiply_reduce_fusion.1
  110.7 0.8 collective-permute-done.25
  111.6 2.4 %collective-permute-start.26 = (bf16[18,1152]{1,0:T(8,128)(2,1)S(1)}, bf16[18,1152]{1,0:T(8,128)(2,1)S(1)}, u32[]{:S(2)}, u32[]{:S(2)}) collective-permute-start(bf16[18,1152]{1,0:T(8,128)(2,1)S(1)} %get-tuple-element.128), channel_id=1, source_target_pairs={{0,16},{2,18},{4,20},{6,22},{8,24},{10,26},{12,28},{14,30},{16,0},... | collective-permute-start | bytes 124424 | tf_op jit(solution)/shard_map/ppermute | solution.py:39
  114.0 3.6 %collective-permute-start.28 = (bf16[18,1152]{1,0:T(8,128)(2,1)S(1)}, bf16[18,1152]{1,0:T(8,128)(2,1)S(1)}, u32[]{:S(2)}, u32[]{:S(2)}) collective-permute-start(bf16[18,1152]{1,0:T(8,128)(2,1)S(1)} %get-tuple-element.129), channel_id=1, source_target_pairs={{0,24},{2,26},{4,28},{6,30},{8,0},{10,2},{12,4},{14,6},{16,8},{18,... | collective-permute-start | bytes 124424 | tf_op jit(solution)/shard_map/ppermute | solution.py:39
  117.6 0.1 divide_convert_fusion.1
  117.7 0.3 collective-permute-start.30
  118.0 0.7 collective-permute-done.26
  118.8 1.4 %collective-permute-done.27 = bf16[18,1152]{1,0:T(8,128)(2,1)S(1)} collective-permute-done((bf16[18,1152]{1,0:T(8,128)(2,1)S(1)}, bf16[18,1152]{1,0:T(8,128)(2,1)S(1)}, u32[]{:S(2)}, u32[]{:S(2)}) %collective-permute-start.27) | collective-permute-done | bytes 41504 | tf_op jit(solution)/shard_map/ppermute | solution.py:39
  120.1 0.6 collective-permute-done.28
  120.8 0.5 collective-permute-done.30
  121.3 3.7 %collective-permute-start.31 = (f32[9,1152]{1,0:T(8,128)S(1)}, f32[9,1152]{1,0:T(8,128)S(1)}, u32[]{:S(2)}, u32[]{:S(2)}) collective-permute-start(f32[9,1152]{1,0:T(8,128)S(1)} %slice_select_fusion), channel_id=1, source_target_pairs={{0,2},{2,0},{4,6},{6,4},{8,10},{10,8},{12,14},{14,12},{16,18},{18,... | collective-permute-start | bytes 124424 | tf_op jit(solution)/shard_map/ppermute | solution.py:39
  125.0 0.7 maximum_select_fusion
  125.7 0.2 collective-permute-done.31
  126.0 0.7 pad_maximum_fusion.2
  (90 shorter events, 1.6 us)
Async XLA Ops:
  2.9 19.4 %collective-permute-start = (bf16[32,1152]{1,0:T(8,128)(2,1)}, bf16[32,1152]{1,0:T(8,128)(2,1)S(1)}, u32[]{:S(2)}, u32[]{:S(2)}) collective-permute-start(bf16[32,1152]{1,0:T(8,128)(2,1)} %shard_map.148), channel_id=1, source_target_pairs={{0,4},{2,6},{4,8},{6,10},{8,12},{10,14},{12,16},{14,18},{16,20},{1... | collective-permute-start | bytes 221192 | tf_op jit(solution)/shard_map/ppermute | solution.py:44
  5.4 18.8 %collective-permute-start.3 = (bf16[32,1152]{1,0:T(8,128)(2,1)}, bf16[32,1152]{1,0:T(8,128)(2,1)S(1)}, u32[]{:S(2)}, u32[]{:S(2)}) collective-permute-start(bf16[32,1152]{1,0:T(8,128)(2,1)} %shard_map.148), channel_id=1, source_target_pairs={{2,16},{6,20},{10,24},{14,28},{18,32},{22,36},{26,40},{30,44},{34,... | collective-permute-start | bytes 221192 | tf_op jit(solution)/shard_map/ppermute | solution.py:44
  14.1 8.8 %collective-permute-start.1 = (bf16[32,1152]{1,0:T(8,128)(2,1)}, bf16[32,1152]{1,0:T(8,128)(2,1)S(1)}, u32[]{:S(2)}, u32[]{:S(2)}) collective-permute-start(bf16[32,1152]{1,0:T(8,128)(2,1)} %own_ref.1), channel_id=1, source_target_pairs={{0,1},{1,0},{2,3},{3,2},{4,5},{5,4},{6,7},{7,6},{8,9},{9,8},{10,11... | collective-permute-start | bytes 221192 | tf_op jit(solution)/shard_map/ppermute | solution.py:48
  15.5 6.8 %collective-permute-start.6 = (f32[729]{0:T(1024)}, f32[729]{0:T(1024)S(1)}, u32[]{:S(2)}, u32[]{:S(2)}) collective-permute-start(f32[729]{0:T(1024)} %param.21), channel_id=1, source_target_pairs={{0,2},{2,0},{4,6},{6,4},{8,10},{10,8},{12,14},{14,12},{16,18},{18,... | collective-permute-start | bytes 8756 | tf_op jit(solution)/shard_map/ppermute | solution.py:39
  15.5 33.8 %collective-permute-start.11 = (bf16[729,2152]{1,0:T(8,128)(2,1)}, bf16[729,2152]{1,0:T(8,128)(2,1)}, u32[]{:S(2)}, u32[]{:S(2)}) collective-permute-start(bf16[729,2152]{1,0:T(8,128)(2,1)} %hidden_hbm), channel_id=1, source_target_pairs={{0,2},{2,0},{4,6},{6,4},{8,10},{10,8},{12,14},{14,12},{16,18},{18,... | collective-permute-start | bytes 9412856 | tf_op jit(solution)/shard_map/ppermute | solution.py:39
  18.9 1.5 %copy-start.3 = (bf16[729,1152]{1,0:T(8,128)(2,1)S(1)}, bf16[729,1152]{1,0:T(8,128)(2,1)}, u32[]{:S(2)}) copy-start(bf16[729,1152]{1,0:T(8,128)(2,1)} %normed_ref) | copy-start | bytes 5038852
  20.3 18.9 %copy-start.7 = (f32[2]{0:T(128)}, f32[2]{0:T(128)S(1)}, u32[]{:S(2)}) copy-start(f32[2]{0:T(128)S(1)} %pad_maximum_fusion.3.scalar_ref) | copy-start | bytes 28
  20.4 1.0 copy-start.15
  20.4 2.5 %copy-start.12 = (bf16[32,1152]{1,0:T(8,128)(2,1)S(1)}, bf16[32,1152]{1,0:T(8,128)(2,1)}, u32[]{:S(2)}) copy-start(bf16[32,1152]{1,0:T(8,128)(2,1)} %shard_map.148) | copy-start | bytes 221188
  20.4 3.9 %copy-start.16 = (s32[32]{0:T(128)S(1)}, s32[32]{0:T(128)}, u32[]{:S(2)}) copy-start(s32[32]{0:T(128)} %param.17) | copy-start | bytes 388
  21.2 12.8 %copy-start = (bf16[1152,768]{1,0:T(8,128)(2,1)}, bf16[1152,768]{1,0:T(8,128)(2,1)S(1)}, u32[]{:S(2)}) copy-start(bf16[1152,768]{1,0:T(8,128)(2,1)S(1)} %shard_map.153.normed0_hbm) | copy-start | bytes 5308420
  22.4 20.3 %collective-permute-start.9 = (bf16[729,1152]{1,0:T(8,128)(2,1)}, bf16[729,1152]{1,0:T(8,128)(2,1)}, u32[]{:S(2)}, u32[]{:S(2)}) collective-permute-start(bf16[729,1152]{1,0:T(8,128)(2,1)} %cotangent_hbm), channel_id=1, source_target_pairs={{0,2},{2,0},{4,6},{6,4},{8,10},{10,8},{12,14},{14,12},{16,18},{18,... | collective-permute-start | bytes 5038856 | tf_op jit(solution)/shard_map/ppermute | solution.py:39
  22.4 40.2 %collective-permute-start.15 = (bf16[1152,768]{1,0:T(8,128)(2,1)S(1)}, bf16[1152,768]{1,0:T(8,128)(2,1)}, u32[]{:S(2)}, u32[]{:S(2)}) collective-permute-start(bf16[1152,768]{1,0:T(8,128)(2,1)S(1)} %shard_map.153.normed0_hbm), channel_id=1, source_target_pairs={{0,2},{2,0},{4,6},{6,4},{8,10},{10,8},{12,14},{14,12},{16,18},{18,... | collective-permute-start | bytes 5308424 | tf_op jit(solution)/shard_map/ppermute | solution.py:39
  22.9 16.3 %copy-start.4 = (bf16[32,1152]{1,0:T(8,128)(2,1)}, bf16[32,1152]{1,0:T(8,128)(2,1)S(1)}, u32[]{:S(2)}) copy-start(bf16[32,1152]{1,0:T(8,128)(2,1)S(1)} %collective-permute-done.1.other_ref) | copy-start | bytes 221188
  22.9 13.8 %collective-permute-start.2 = (bf16[64,1152]{1,0:T(8,128)(2,1)S(1)}, bf16[64,1152]{1,0:T(8,128)(2,1)S(1)}, u32[]{:S(2)}, u32[]{:S(2)}) collective-permute-start(bf16[64,1152]{1,0:T(8,128)(2,1)S(1)} %pad_maximum_fusion.1.refs_0_), channel_id=1, source_target_pairs={{0,8},{2,10},{4,12},{6,14},{8,16},{10,18},{12,20},{14,22},{16,24},... | collective-permute-start | bytes 442376 | tf_op jit(solution)/shard_map/ppermute | solution.py:44
  24.2 9.8 %collective-permute-start.4 = (s32[32]{0:T(128)S(1)}, s32[32]{0:T(128)S(1)}, u32[]{:S(2)}, u32[]{:S(2)}) collective-permute-start(s32[32]{0:T(128)S(1)} %copy-done.16), channel_id=1, source_target_pairs={{0,1},{1,0},{2,3},{3,2},{4,5},{5,4},{6,7},{7,6},{8,9},{9,8},{10,11... | collective-permute-start | bytes 392 | tf_op jit(solution)/shard_map/ppermute | solution.py:48
  25.0 14.2 %copy-start.1 = (bf16[32,1152]{1,0:T(8,128)(2,1)S(1)}, bf16[32,1152]{1,0:T(8,128)(2,1)}, u32[]{:S(2)}) copy-start(bf16[32,1152]{1,0:T(8,128)(2,1)} %own_ref.1) | copy-start | bytes 221188
  25.0 14.3 %copy-start.5 = (s32[2]{0:T(128)S(1)}, s32[2]{0:T(128)}, u32[]{:S(2)}) copy-start(s32[2]{0:T(128)} %pad_add_fusion.place_ref) | copy-start | bytes 28
  34.1 5.2 %collective-permute-start.7 = (bf16[64,1152]{1,0:T(8,128)(2,1)S(1)}, bf16[64,1152]{1,0:T(8,128)(2,1)S(1)}, u32[]{:S(2)}, u32[]{:S(2)}) collective-permute-start(bf16[64,1152]{1,0:T(8,128)(2,1)S(1)} %pad_maximum_fusion.1.refs_0_), channel_id=1, source_target_pairs={{0,2},{2,0},{4,6},{6,4},{8,10},{10,8},{12,14},{14,12},{16,18},{18,... | collective-permute-start | bytes 442376 | tf_op jit(solution)/shard_map/ppermute | solution.py:39
  36.7 1.9 %collective-permute-start.5 = (bf16[64,1152]{1,0:T(8,128)(2,1)S(1)}, bf16[64,1152]{1,0:T(8,128)(2,1)S(1)}, u32[]{:S(2)}, u32[]{:S(2)}) collective-permute-start(bf16[64,1152]{1,0:T(8,128)(2,1)S(1)} %collective-permute-done.2.refs_1_), channel_id=1, source_target_pairs={{0,2},{2,0},{4,6},{6,4},{8,10},{10,8},{12,14},{14,12},{16,18},{18,... | collective-permute-start | bytes 442376 | tf_op jit(solution)/shard_map/ppermute | solution.py:39
  40.8 17.4 %copy-start.6 = (f32[1,1152]{1,0:T(1,128)}, f32[1,1152]{1,0:T(1,128)S(1)}, u32[]{:S(2)}) copy-start(f32[1,1152]{1,0:T(1,128)S(1)} %get-tuple-element.81.mine_ref) | copy-start | bytes 13828
  40.8 1.9 %collective-permute-start.8 = (bf16[128,1152]{1,0:T(8,128)(2,1)S(1)}, bf16[128,1152]{1,0:T(8,128)(2,1)S(1)}, u32[]{:S(2)}, u32[]{:S(2)}) collective-permute-start(bf16[128,1152]{1,0:T(8,128)(2,1)S(1)} %get-tuple-element.80), channel_id=1, source_target_pairs={{0,2},{2,0},{4,6},{6,4},{8,10},{10,8},{12,14},{14,12},{16,18},{18,... | collective-permute-start | bytes 884744 | tf_op jit(solution)/shard_map/ppermute | solution.py:39
  42.7 15.5 %copy-start.10 = (bf16[128,1152]{1,0:T(8,128)(2,1)}, bf16[128,1152]{1,0:T(8,128)(2,1)S(1)}, u32[]{:S(2)}) copy-start(bf16[128,1152]{1,0:T(8,128)(2,1)S(1)} %collective-permute-done.8) | copy-start | bytes 884740
  42.7 18.9 %collective-permute-start.13 = (bf16[64,1152]{1,0:T(8,128)(2,1)S(1)}, bf16[64,1152]{1,0:T(8,128)(2,1)S(1)}, u32[]{:S(2)}, u32[]{:S(2)}) collective-permute-start(bf16[64,1152]{1,0:T(8,128)(2,1)S(1)} %add_convert_fusion), channel_id=1, source_target_pairs={{0,248},{2,250},{4,252},{6,254},{8,0},{10,2},{12,4},{14,6},{16,8},... | collective-permute-start | bytes 442376 | tf_op jit(solution)/shard_map/ppermute | solution.py:44
  47.8 13.8 %collective-permute-start.14 = (bf16[32,1152]{1,0:T(8,128)(2,1)S(1)}, bf16[32,1152]{1,0:T(8,128)(2,1)S(1)}, u32[]{:S(2)}, u32[]{:S(2)}) collective-permute-start(bf16[32,1152]{1,0:T(8,128)(2,1)S(1)} %get-tuple-element.89), channel_id=1, source_target_pairs={{0,1},{1,0},{2,3},{3,2},{4,5},{5,4},{6,7},{7,6},{8,9},{9,8},{10,11... | collective-permute-start | bytes 221192 | tf_op jit(solution)/shard_map/ppermute | solution.py:48
  47.9 10.3 %collective-permute-start.10 = (f32[1,1152]{1,0:T(1,128)S(1)}, f32[1,1152]{1,0:T(1,128)S(1)}, u32[]{:S(2)}, u32[]{:S(2)}) collective-permute-start(f32[1,1152]{1,0:T(1,128)S(1)} %get-tuple-element.81.mine_ref), channel_id=1, source_target_pairs={{0,1},{1,0},{2,3},{3,2},{4,5},{5,4},{6,7},{7,6},{8,9},{9,8},{10,11... | collective-permute-start | bytes 13832 | tf_op jit(solution)/shard_map/ppermute | solution.py:48
  58.2 0.6 copy-start.14
  60.6 2.1 %collective-permute-start.12 = (bf16[1,1152]{1,0:T(2,128)(2,1)}, bf16[1,1152]{1,0:T(2,128)(2,1)S(1)}, u32[]{:S(2)}, u32[]{:S(2)}) collective-permute-start(bf16[1,1152]{1,0:T(2,128)(2,1)} %shard_map.152.pooled0_ref), channel_id=1, source_target_pairs={{0,2},{2,0},{4,6},{6,4},{8,10},{10,8},{12,14},{14,12},{16,18},{18,... | collective-permute-start | bytes 6920 | tf_op jit(solution)/shard_map/ppermute | solution.py:39
  61.6 14.2 %copy-start.2 = (bf16[32,1152]{1,0:T(8,128)(2,1)S(1)}, bf16[32,1152]{1,0:T(8,128)(2,1)}, u32[]{:S(2)}) copy-start(bf16[32,1152]{1,0:T(8,128)(2,1)} %own_ref.1) | copy-start | bytes 221188
  61.6 19.3 %copy-start.8 = (bf16[64,1152]{1,0:T(8,128)(2,1)S(1)}, bf16[64,1152]{1,0:T(8,128)(2,1)}, u32[]{:S(2)}) copy-start(bf16[64,1152]{1,0:T(8,128)(2,1)} %raw_ref.1) | copy-start | bytes 442372
  62.6 0.6 copy-start.13
  76.0 16.4 %collective-permute-start.16 = (bf16[4,144,512]{2,1,0:T(8,128)(2,1)}, bf16[4,144,512]{2,1,0:T(8,128)(2,1)S(1)}, u32[]{:S(2)}, u32[]{:S(2)}) collective-permute-start(bf16[4,144,512]{2,1,0:T(8,128)(2,1)} %get-tuple-element.97), channel_id=1, source_target_pairs={{0,128},{2,130},{4,132},{6,134},{8,136},{10,138},{12,140},{14,142}... | collective-permute-start | bytes 1769480 | tf_op jit(solution)/shard_map/ppermute | solution.py:39
  78.2 16.6 %collective-permute-start.17 = (bf16[2,144,640]{2,1,0:T(8,128)(2,1)}, bf16[2,144,640]{2,1,0:T(8,128)(2,1)S(1)}, u32[]{:S(2)}, u32[]{:S(2)}) collective-permute-start(bf16[2,144,640]{2,1,0:T(8,128)(2,1)} %get-tuple-element.104), channel_id=1, source_target_pairs={{0,64},{2,66},{4,68},{6,70},{8,72},{10,74},{12,76},{14,78},{16,80}... | collective-permute-start | bytes 1105928 | tf_op jit(solution)/shard_map/ppermute | solution.py:39
  78.2 19.5 %collective-permute-start.18 = (bf16[2,144,640]{2,1,0:T(8,128)(2,1)}, bf16[2,144,640]{2,1,0:T(8,128)(2,1)S(1)}, u32[]{:S(2)}, u32[]{:S(2)}) collective-permute-start(bf16[2,144,640]{2,1,0:T(8,128)(2,1)} %get-tuple-element.105), channel_id=1, source_target_pairs={{0,32},{2,34},{4,36},{6,38},{8,40},{10,42},{12,44},{14,46},{16,48}... | collective-permute-start | bytes 1105928 | tf_op jit(solution)/shard_map/ppermute | solution.py:39
  78.2 19.5 %collective-permute-start.19 = (bf16[2,144,640]{2,1,0:T(8,128)(2,1)}, bf16[2,144,640]{2,1,0:T(8,128)(2,1)S(1)}, u32[]{:S(2)}, u32[]{:S(2)}) collective-permute-start(bf16[2,144,640]{2,1,0:T(8,128)(2,1)} %get-tuple-element.106), channel_id=1, source_target_pairs={{0,96},{2,98},{4,100},{6,102},{8,104},{10,106},{12,108},{14,110},{... | collective-permute-start | bytes 1105928 | tf_op jit(solution)/shard_map/ppermute | solution.py:39
  81.2 12.5 %copy-start.11 = (bf16[128,1152]{1,0:T(8,128)(2,1)S(1)}, bf16[128,1152]{1,0:T(8,128)(2,1)}, u32[]{:S(2)}) copy-start(bf16[128,1152]{1,0:T(8,128)(2,1)} %copy-done.10) | copy-start | bytes 884740
  93.8 4.0 %copy-start.9 = (f32[2,144,640]{2,1,0:T(8,128)S(1)}, f32[2,144,640]{2,1,0:T(8,128)}, u32[]{:S(2)}) copy-start(f32[2,144,640]{2,1,0:T(8,128)} %get-tuple-element.103) | copy-start | bytes 2211844
  93.9 11.1 %collective-permute-start.24 = (bf16[32,1152]{1,0:T(8,128)(2,1)S(1)}, bf16[32,1152]{1,0:T(8,128)(2,1)S(1)}, u32[]{:S(2)}, u32[]{:S(2)}) collective-permute-start(bf16[32,1152]{1,0:T(8,128)(2,1)S(1)} %slice.106), channel_id=1, source_target_pairs={{0,252},{2,254},{4,0},{6,2},{8,4},{10,6},{12,8},{14,10},{16,12},{1... | collective-permute-start | bytes 221192 | tf_op jit(solution)/shard_map/ppermute | solution.py:44
  94.8 5.7 %collective-permute-start.21 = (bf16[144,512]{1,0:T(8,128)(2,1)S(1)}, bf16[144,512]{1,0:T(8,128)(2,1)S(1)}, u32[]{:S(2)}, u32[]{:S(2)}) collective-permute-start(bf16[144,512]{1,0:T(8,128)(2,1)S(1)} %get-tuple-element.125), channel_id=1, source_target_pairs={{0,64},{2,66},{4,68},{6,70},{8,72},{10,74},{12,76},{14,78},{16,80}... | collective-permute-start | bytes 442376 | tf_op jit(solution)/shard_map/ppermute | solution.py:39
  94.9 9.9 %collective-permute-start.22 = (bf16[144,512]{1,0:T(8,128)(2,1)S(1)}, bf16[144,512]{1,0:T(8,128)(2,1)S(1)}, u32[]{:S(2)}, u32[]{:S(2)}) collective-permute-start(bf16[144,512]{1,0:T(8,128)(2,1)S(1)} %get-tuple-element.127), channel_id=1, source_target_pairs={{0,32},{2,34},{4,36},{6,38},{8,40},{10,42},{12,44},{14,46},{16,48}... | collective-permute-start | bytes 442376 | tf_op jit(solution)/shard_map/ppermute | solution.py:39
  97.8 7.0 %collective-permute-start.23 = (bf16[144,512]{1,0:T(8,128)(2,1)S(1)}, bf16[144,512]{1,0:T(8,128)(2,1)S(1)}, u32[]{:S(2)}, u32[]{:S(2)}) collective-permute-start(bf16[144,512]{1,0:T(8,128)(2,1)S(1)} %get-tuple-element.126), channel_id=1, source_target_pairs={{0,96},{2,98},{4,100},{6,102},{8,104},{10,106},{12,108},{14,110},{... | collective-permute-start | bytes 442376 | tf_op jit(solution)/shard_map/ppermute | solution.py:39
  98.0 6.9 %collective-permute-start.20 = (bf16[144,640]{1,0:T(8,128)(2,1)S(1)}, bf16[144,640]{1,0:T(8,128)(2,1)S(1)}, u32[]{:S(2)}, u32[]{:S(2)}) collective-permute-start(bf16[144,640]{1,0:T(8,128)(2,1)S(1)} %fusion.2), channel_id=1, source_target_pairs={{0,128},{2,130},{4,132},{6,134},{8,136},{10,138},{12,140},{14,142}... | collective-permute-start | bytes 552968 | tf_op jit(solution)/shard_map/ppermute | solution.py:39
  100.5 10.1 %collective-permute-start.29 = (bf16[32,1152]{1,0:T(8,128)(2,1)S(1)}, bf16[32,1152]{1,0:T(8,128)(2,1)S(1)}, u32[]{:S(2)}, u32[]{:S(2)}) collective-permute-start(bf16[32,1152]{1,0:T(8,128)(2,1)S(1)} %get-tuple-element.113), channel_id=1, source_target_pairs={{0,242},{4,246},{8,250},{12,254},{16,2},{20,6},{24,10},{28,14},{32... | collective-permute-start | bytes 221192 | tf_op jit(solution)/shard_map/ppermute | solution.py:44
  105.1 6.4 %collective-permute-start.25 = (bf16[4,18,1152]{2,1,0:T(8,128)(2,1)S(1)}, bf16[4,18,1152]{2,1,0:T(8,128)(2,1)S(1)}, u32[]{:S(2)}, u32[]{:S(2)}) collective-permute-start(bf16[4,18,1152]{2,1,0:T(8,128)(2,1)S(1)} %fusion.1), channel_id=1, source_target_pairs={{0,4},{2,6},{4,0},{6,2},{8,12},{10,14},{12,8},{14,10},{16,20},{18,... | collective-permute-start | bytes 497672 | tf_op jit(solution)/shard_map/ppermute | solution.py:557
  111.6 7.1 %collective-permute-start.26 = (bf16[18,1152]{1,0:T(8,128)(2,1)S(1)}, bf16[18,1152]{1,0:T(8,128)(2,1)S(1)}, u32[]{:S(2)}, u32[]{:S(2)}) collective-permute-start(bf16[18,1152]{1,0:T(8,128)(2,1)S(1)} %get-tuple-element.128), channel_id=1, source_target_pairs={{0,16},{2,18},{4,20},{6,22},{8,24},{10,26},{12,28},{14,30},{16,0},... | collective-permute-start | bytes 124424 | tf_op jit(solution)/shard_map/ppermute | solution.py:39
  114.0 6.1 %collective-permute-start.27 = (bf16[18,1152]{1,0:T(8,128)(2,1)S(1)}, bf16[18,1152]{1,0:T(8,128)(2,1)S(1)}, u32[]{:S(2)}, u32[]{:S(2)}) collective-permute-start(bf16[18,1152]{1,0:T(8,128)(2,1)S(1)} %get-tuple-element.130), channel_id=1, source_target_pairs={{0,8},{2,10},{4,12},{6,14},{8,16},{10,18},{12,20},{14,22},{16,24},... | collective-permute-start | bytes 124424 | tf_op jit(solution)/shard_map/ppermute | solution.py:39
  114.0 6.7 %collective-permute-start.28 = (bf16[18,1152]{1,0:T(8,128)(2,1)S(1)}, bf16[18,1152]{1,0:T(8,128)(2,1)S(1)}, u32[]{:S(2)}, u32[]{:S(2)}) collective-permute-start(bf16[18,1152]{1,0:T(8,128)(2,1)S(1)} %get-tuple-element.129), channel_id=1, source_target_pairs={{0,24},{2,26},{4,28},{6,30},{8,0},{10,2},{12,4},{14,6},{16,8},{18,... | collective-permute-start | bytes 124424 | tf_op jit(solution)/shard_map/ppermute | solution.py:39
  117.7 3.6 %collective-permute-start.30 = (bf16[32,1152]{1,0:T(8,128)(2,1)S(1)}, bf16[32,1152]{1,0:T(8,128)(2,1)S(1)}, u32[]{:S(2)}, u32[]{:S(2)}) collective-permute-start(bf16[32,1152]{1,0:T(8,128)(2,1)S(1)} %divide_convert_fusion.1), channel_id=1, source_target_pairs={{0,1},{1,0},{2,3},{3,2},{4,5},{5,4},{6,7},{7,6},{8,9},{9,8},{10,11... | collective-permute-start | bytes 221192 | tf_op jit(solution)/shard_map/ppermute | solution.py:48
  121.3 4.6 %collective-permute-start.31 = (f32[9,1152]{1,0:T(8,128)S(1)}, f32[9,1152]{1,0:T(8,128)S(1)}, u32[]{:S(2)}, u32[]{:S(2)}) collective-permute-start(f32[9,1152]{1,0:T(8,128)S(1)} %slice_select_fusion), channel_id=1, source_target_pairs={{0,2},{2,0},{4,6},{6,4},{8,10},{10,8},{12,14},{14,12},{16,18},{18,... | collective-permute-start | bytes 124424 | tf_op jit(solution)/shard_map/ppermute | solution.py:39

commit v2 on v1

--- a/solution.py
+++ b/solution.py
@@ -495,10 +495,8 @@
     zero_theirs = tensor_swap(zero_row)
 
     near = 2 * half
-    returned = torus_send(text_sibling, core=1)
     image_swapped = tensor_swap(image_swapped)
-    zero_row, returned, cotangent_other = lax.optimization_barrier((zero_row, returned, cotangent_other))
-    text_next = ring_send((text_own[near:] + returned[near:].astype(f32)).astype(bf16), -4)
+    zero_row, cotangent_other = lax.optimization_barrier((zero_row, cotangent_other))
 
     base_other, slope_other = hidden_base(
         spot, columns, cotangent_other, share_other, down_weight, hidden_other, LIGHT
@@ -506,7 +504,7 @@
     zero_theirs, base_other, slope_other = lax.optimization_barrier((zero_theirs, base_other, slope_other))
     pooled = pooled_row(spot, scalars, image_raw, image_other, zero_row, zero_theirs)
     pooled_other = torus_send(pooled, core=1)
-    pooled_other, text_next, image_swapped = lax.optimization_barrier((pooled_other, text_next, image_swapped))
+    pooled_other, image_swapped = lax.optimization_barrier((pooled_other, image_swapped))
 
     split = 5 * LANES
     a_keep, a_sent1, a_sent2, a_sent3, c_keep, c_sent = up_terms(
@@ -519,7 +517,11 @@
         down_weight,
         [pooled, pooled_other],
     )
-    a_keep, image_part, late_text, late_image = lax.optimization_barrier((a_keep, image_part, text_raw, image_raw))
+    a_keep, image_part, late_text, late_image, text_own, text_sibling = lax.optimization_barrier(
+        (a_keep, image_part, text_raw, image_raw, text_own, text_sibling)
+    )
+    returned = torus_send(text_sibling, core=1)
+    text_next = ring_send((text_own[near:] + returned[near:].astype(f32)).astype(bf16), -4)
     c_come = torus_send(c_sent, yh=1)
     a_come = [torus_send(part, x=dx) for dx, part in ((2, a_sent2), (1, a_sent1), (3, a_sent3))]
     c_keep = c_keep + c_come.astype(f32)

time: 127 us -> 129 us (1.016)
  starting transfers between devices: 45.4 us -> 55.4 us
  waiting for transfers between devices: 30 us -> 23 us
  other arithmetic: 7.17 us -> 4.63 us
    ppermute x20, waiting for transfers between devices: 22.2 us -> 14.2 us  [torus_send(): return lax.ppermute(array, 'dp', torus_pairs(**shift))]
    ppermute x20, starting transfers between devices: 21.6 us -> 29.1 us  [torus_send(): return lax.ppermute(array, 'dp', torus_pairs(**shift))]
    ppermute x5, waiting for transfers between devices: 0.52 us -> 3.74 us  [tensor_swap(): return lax.ppermute(array, 'tensor', [(0, 1), (1, 0)])]
    ppermute x6, starting transfers between devices: 19.6 us -> 22.1 us  [ring_send(): return lax.ppermute(array, 'dp', pairs)]
    ppermute x6, waiting for transfers between devices: 6.51 us -> 5.07 us  [ring_send(): return lax.ppermute(array, 'dp', pairs)]
    unnamed x34 -> x38, local copies, waits for them, and re-layouts: 2.69 us -> 3.38 us
  transfers between devices with their start and end apart: 32 -> 32, of which waited for: 14 -> 12; matrix products, arithmetic and copies ran while one was open for 6% -> 4% of each run, Pallas kernels for 17% -> 17%
where the time goes in v2:
time: 129 us; the launch traced here: 128 us
  starting transfers between devices  55.4 us (43%)
  Pallas kernels  36.4 us (28%)
  waiting for transfers between devices  23 us (18%)
  local copies, waits for them, and re-layouts  5.79 us (4%)
  other arithmetic  4.63 us (4%)
  between operations  2.52 us (2%)
    ppermute x20, starting transfers between devices, torus_send(): return lax.ppermute(array, 'dp', torus_pairs(**shift))  29.1 us
    ppermute x6, starting transfers between devices, ring_send(): return lax.ppermute(array, 'dp', pairs)  22.1 us
    pallas_call x2, Pallas kernels, hidden_base(): pl.pallas_call(base_kernel, grid_spec=pltpu.PrefetchScalarGridSpec(num_sc...  17.9 us
    ppermute x20, waiting for transfers between devices, torus_send(): return lax.ppermute(array, 'dp', torus_pairs(**shift))  14.2 us
    pallas_call x1, Pallas kernels, up_terms(): pl.pallas_call(terms_kernel, grid_spec=pltpu.PrefetchScalarGridSpec(num_s...  12.6 us
    ppermute x6, waiting for transfers between devices, ring_send(): return lax.ppermute(array, 'dp', pairs)  5.07 us
    ppermute x5, starting transfers between devices, tensor_swap(): return lax.ppermute(array, 'tensor', [(0, 1), (1, 0)])  4.14 us
    ppermute x5, waiting for transfers between devices, tensor_swap(): return lax.ppermute(array, 'tensor', [(0, 1), (1, 0)])  3.74 us
  transfers between devices with their start and end apart: 32, of which 12 were waited for; matrix products, arithmetic and copies ran while one was open for 4% of the time, Pallas kernels for 17%

profile of v2, /device:TPU:1, one launch (start us, length us, event | category | flops | bytes accessed | tf_op | source)
XLA Modules:
  0.0 127.7 jit_solution(9707729278833350676)
XLA Ops:
  0.6 0.7 pad_add_fusion.place_ref
  1.3 1.7 %shard_map.148 = bf16[32,1152]{1,0:T(8,128)(2,1)} custom-call(s32[2]{0:T(128)} %pad_add_fusion.place_ref, bf16[64,1152]{1,0:T(8,128)(2,1)} %raw_ref.1), custom_call_target="tpu_custom_call" | custom-call | tf_op jit(solution)/shard_map/pallas_call | solution.py:87
  3.0 3.2 %collective-permute-start.10 = (bf16[729,2152]{1,0:T(8,128)(2,1)}, bf16[729,2152]{1,0:T(8,128)(2,1)}, u32[]{:S(2)}, u32[]{:S(2)}) collective-permute-start(bf16[729,2152]{1,0:T(8,128)(2,1)} %hidden_hbm), channel_id=1, source_target_pairs={{0,2},{2,0},{4,6},{6,4},{8,10},{10,8},{12,14},{14,12},{16,18},{18,... | collective-permute-start | bytes 9412856 | tf_op jit(solution)/shard_map/ppermute | solution.py:39
  6.3 0.2 collective-permute-start.6
  6.4 0.3 collective-permute-start.8
  6.8 1.4 %copy-done.3 = bf16[729,1152]{1,0:T(8,128)(2,1)S(1)} copy-done((bf16[729,1152]{1,0:T(8,128)(2,1)S(1)}, bf16[729,1152]{1,0:T(8,128)(2,1)}, u32[]{:S(2)}) %copy-start.3) | copy-done | bytes 1679640
  8.2 0.8 shard_map.153.normed0_hbm
  9.1 0.3 collective-permute-start.13
  11.3 0.6 stack.56.targets_ref
  11.9 8.0 %collective-permute-start.3 = (bf16[32,1152]{1,0:T(8,128)(2,1)S(1)}, bf16[32,1152]{1,0:T(8,128)(2,1)S(1)}, u32[]{:S(2)}, u32[]{:S(2)}) collective-permute-start(bf16[32,1152]{1,0:T(8,128)(2,1)S(1)} %copy-done.13), channel_id=1, source_target_pairs={{2,16},{6,20},{10,24},{14,28},{18,32},{22,36},{26,40},{30,44},{34,... | collective-permute-start | bytes 221192 | tf_op jit(solution)/shard_map/ppermute | solution.py:44
  20.0 1.4 %collective-permute-start.1 = (bf16[32,1152]{1,0:T(8,128)(2,1)S(1)}, bf16[32,1152]{1,0:T(8,128)(2,1)S(1)}, u32[]{:S(2)}, u32[]{:S(2)}) collective-permute-start(bf16[32,1152]{1,0:T(8,128)(2,1)S(1)} %copy-done.1), channel_id=1, source_target_pairs={{0,1},{1,0},{2,3},{3,2},{4,5},{5,4},{6,7},{7,6},{8,9},{9,8},{10,11... | collective-permute-start | bytes 221192 | tf_op jit(solution)/shard_map/ppermute | solution.py:48
  21.4 2.2 %collective-permute-done.1.other_ref = bf16[32,1152]{1,0:T(8,128)(2,1)S(1)} collective-permute-done((bf16[32,1152]{1,0:T(8,128)(2,1)S(1)}, bf16[32,1152]{1,0:T(8,128)(2,1)S(1)}, u32[]{:S(2)}, u32[]{:S(2)}) %collective-permute-start.1) | collective-permute-done | bytes 73760 | tf_op jit(solution)/shard_map/ppermute | solution.py:48
  23.6 1.2 collective-permute-start.2
  24.8 1.0 collective-permute-start.4
  25.8 0.6 broadcast_in_dim.8.share_ref
  26.4 9.0 %shard_map.149 = (bf16[729,1152]{1,0:T(8,128)(2,1)}, bf16[729,1152]{1,0:T(8,128)(2,1)}) custom-call(s32[2]{0:T(128)} %pad_add_fusion.place_ref, f32[8,768]{1,0:T(8,128)} %broadcast_in_dim.8.share_ref, bf16[2152,1152]{1,0:T(8,128)(2,1)} %weight_hbm.5, bf16[729,2152]{1,0:T(8,128)(2,1)} %hidden_hbm, bf16[729,1152]{1,0:T(8,128)(2,1)} %cotangent_hbm, ...), custom_call_target="tpu_custom_call" | custom-call | flops 10000000000 | bytes 1 | tf_op jit(solution)/shard_map/pallas_call | solution.py:249
  35.4 2.1 %collective-permute-start.7 = (bf16[64,1152]{1,0:T(8,128)(2,1)S(1)}, bf16[64,1152]{1,0:T(8,128)(2,1)S(1)}, u32[]{:S(2)}, u32[]{:S(2)}) collective-permute-start(bf16[64,1152]{1,0:T(8,128)(2,1)S(1)} %pad_maximum_fusion.1.refs_0_), channel_id=1, source_target_pairs={{0,2},{2,0},{4,6},{6,4},{8,10},{10,8},{12,14},{14,12},{16,18},{18,... | collective-permute-start | bytes 442376 | tf_op jit(solution)/shard_map/ppermute | solution.py:39
  37.5 0.3 collective-permute-done.2.refs_1_
  37.8 0.4 collective-permute-start.5
  38.3 0.8 collective-permute-done.5.refs_3_
  39.1 0.6 broadcast_in_dim.9.share_ref
  39.8 1.6 %shard_map.150 = (f32[32,1152]{1,0:T(8,128)S(1)}, bf16[32,1152]{1,0:T(8,128)(2,1)S(1)}, f32[1,1152]{1,0:T(1,128)S(1)}, f32[128,1152]{1,0:T(8,128)S(1)}, bf16[128...) custom-call(s32[2]{0:T(128)S(1)} %copy-done.5, f32[2]{0:T(128)S(1)} %pad_maximum_fusion.3.scalar_ref, ...), custom_call_target="tpu_custom_call" | custom-call | flops 1 | bytes 1 | tf_op jit(solution)/shard_map/pallas_call | solution.py:125
  41.4 0.7 copy-done.8
  42.1 0.4 collective-permute-start.12
  42.4 1.1 collective-permute-start.9
  43.5 8.9 %shard_map.151 = (bf16[729,1152]{1,0:T(8,128)(2,1)}, bf16[729,1152]{1,0:T(8,128)(2,1)}) custom-call(s32[2]{0:T(128)} %pad_add_fusion.place_ref, f32[8,768]{1,0:T(8,128)} %broadcast_in_dim.9.share_ref, bf16[2152,1152]{1,0:T(8,128)(2,1)} %weight_hbm.5, bf16[729,2152]{1,0:T(8,128)(2,1)} %collective-permute-done.10.hidden_tail.hidden_hbm, ...), custom_call_target="tpu_custom_call" | custom-call | flops 1 | bytes 1 | tf_op jit(solution)/shard_map/pallas_call | solution.py:249
  52.5 0.6 copy-done.15
  53.1 1.7 %shard_map.152.pooled0_ref = bf16[1,1152]{1,0:T(2,128)(2,1)} custom-call(s32[2]{0:T(128)} %pad_add_fusion.place_ref, f32[2]{0:T(128)} %copy-done.7, bf16[32,1152]{1,0:T(8,128)(2,1)} %own_ref.1, bf16[32,1152]{1,0:T(8,128)(2,1)} %copy-done.4, f32[1,1152]{1,0:T(1,128)} %copy-done.6, f32[1,1152]{1,0:T(1,128)} %copy-done.15), custom_call_target="tpu_custom_call" | custom-call | tf_op jit(solution)/shard_map/pallas_call | solution.py:162
  54.8 0.9 collective-permute-start.11
  55.7 1.0 collective-permute-done.11.pooled1_ref
  56.7 0.6 copy-done.14
  57.3 12.6 %shard_map.154 = (f32[2,144,640]{2,1,0:T(8,128)}, bf16[2,144,640]{2,1,0:T(8,128)(2,1)}, bf16[2,144,640]{2,1,0:T(8,128)(2,1)}, bf16[2,144,640]{2,1,0:T(8,128)(2,1...) custom-call(s32[2]{0:T(128)} %pad_add_fusion.place_ref, s32[8]{0:T(128)} %stack.56.targets_ref, ...), custom_call_target="tpu_custom_call" | custom-call | flops 1 | bytes 1 | tf_op jit(solution)/shard_map/pallas_call | solution.py:377
  70.0 0.1 fusion.4
  70.1 0.4 collective-permute-start.15
  70.5 2.2 %collective-permute-start.14 = (bf16[4,144,512]{2,1,0:T(8,128)(2,1)}, bf16[4,144,512]{2,1,0:T(8,128)(2,1)S(1)}, u32[]{:S(2)}, u32[]{:S(2)}) collective-permute-start(bf16[4,144,512]{2,1,0:T(8,128)(2,1)} %get-tuple-element.94), channel_id=1, source_target_pairs={{0,128},{2,130},{4,132},{6,134},{8,136},{10,138},{12,140},{14,142}... | collective-permute-start | bytes 1769480 | tf_op jit(solution)/shard_map/ppermute | solution.py:39
  72.8 0.2 multiply_reduce_fusion
  73.0 0.7 divide_convert_fusion
  73.7 1.3 %collective-permute-start.17 = (bf16[2,144,640]{2,1,0:T(8,128)(2,1)}, bf16[2,144,640]{2,1,0:T(8,128)(2,1)S(1)}, u32[]{:S(2)}, u32[]{:S(2)}) collective-permute-start(bf16[2,144,640]{2,1,0:T(8,128)(2,1)} %get-tuple-element.104), channel_id=1, source_target_pairs={{0,64},{2,66},{4,68},{6,70},{8,72},{10,74},{12,76},{14,78},{16,80}... | collective-permute-start | bytes 1105928 | tf_op jit(solution)/shard_map/ppermute | solution.py:39
  75.0 0.3 collective-permute-start.18
  75.3 2.4 %collective-permute-start.19 = (bf16[2,144,640]{2,1,0:T(8,128)(2,1)}, bf16[2,144,640]{2,1,0:T(8,128)(2,1)S(1)}, u32[]{:S(2)}, u32[]{:S(2)}) collective-permute-start(bf16[2,144,640]{2,1,0:T(8,128)(2,1)} %get-tuple-element.106), channel_id=1, source_target_pairs={{0,96},{2,98},{4,100},{6,102},{8,104},{10,106},{12,108},{14,110},{... | collective-permute-start | bytes 1105928 | tf_op jit(solution)/shard_map/ppermute | solution.py:39
  77.7 0.1 fusion.3
  77.9 3.2 %collective-permute-start.16 = (bf16[64,1152]{1,0:T(8,128)(2,1)S(1)}, bf16[64,1152]{1,0:T(8,128)(2,1)S(1)}, u32[]{:S(2)}, u32[]{:S(2)}) collective-permute-start(bf16[64,1152]{1,0:T(8,128)(2,1)S(1)} %add_convert_fusion), channel_id=1, source_target_pairs={{0,248},{2,250},{4,252},{6,254},{8,0},{10,2},{12,4},{14,6},{16,8},... | collective-permute-start | bytes 442376 | tf_op jit(solution)/shard_map/ppermute | solution.py:44
  81.1 5.8 %collective-permute-done.14 = bf16[4,144,512]{2,1,0:T(8,128)(2,1)S(1)} collective-permute-done((bf16[4,144,512]{2,1,0:T(8,128)(2,1)}, bf16[4,144,512]{2,1,0:T(8,128)(2,1)S(1)}, u32[]{:S(2)}, u32[]{:S(2)}) %collective-permute-start.14) | collective-permute-done | bytes 589856 | tf_op jit(solution)/shard_map/ppermute | solution.py:39
  86.9 0.2 convert_add_fusion
  87.2 8.4 %collective-permute-start.24 = (bf16[32,1152]{1,0:T(8,128)(2,1)S(1)}, bf16[32,1152]{1,0:T(8,128)(2,1)S(1)}, u32[]{:S(2)}, u32[]{:S(2)}) collective-permute-start(bf16[32,1152]{1,0:T(8,128)(2,1)S(1)} %slice.107), channel_id=1, source_target_pairs={{0,252},{2,254},{4,0},{6,2},{8,4},{10,6},{12,8},{14,10},{16,12},{1... | collective-permute-start | bytes 221192 | tf_op jit(solution)/shard_map/ppermute | solution.py:44
  95.9 2.7 %collective-permute-start.23 = (bf16[144,512]{1,0:T(8,128)(2,1)S(1)}, bf16[144,512]{1,0:T(8,128)(2,1)S(1)}, u32[]{:S(2)}, u32[]{:S(2)}) collective-permute-start(bf16[144,512]{1,0:T(8,128)(2,1)S(1)} %get-tuple-element.126), channel_id=1, source_target_pairs={{0,96},{2,98},{4,100},{6,102},{8,104},{10,106},{12,108},{14,110},{... | collective-permute-start | bytes 442376 | tf_op jit(solution)/shard_map/ppermute | solution.py:39
  98.6 0.2 add_add_fusion
  98.8 0.8 collective-permute-start.20
  99.6 1.8 %collective-permute-done.21 = bf16[144,512]{1,0:T(8,128)(2,1)S(1)} collective-permute-done((bf16[144,512]{1,0:T(8,128)(2,1)S(1)}, bf16[144,512]{1,0:T(8,128)(2,1)S(1)}, u32[]{:S(2)}, u32[]{:S(2)}) %collective-permute-start.21) | collective-permute-done | bytes 147488 | tf_op jit(solution)/shard_map/ppermute | solution.py:39
  101.4 1.3 %collective-permute-start.29 = (bf16[32,1152]{1,0:T(8,128)(2,1)S(1)}, bf16[32,1152]{1,0:T(8,128)(2,1)S(1)}, u32[]{:S(2)}, u32[]{:S(2)}) collective-permute-start(bf16[32,1152]{1,0:T(8,128)(2,1)S(1)} %get-tuple-element.113), channel_id=1, source_target_pairs={{0,242},{4,246},{8,250},{12,254},{16,2},{20,6},{24,10},{28,14},{32... | collective-permute-start | bytes 221192 | tf_op jit(solution)/shard_map/ppermute | solution.py:44
  102.7 3.0 %collective-permute-done.22 = bf16[144,512]{1,0:T(8,128)(2,1)S(1)} collective-permute-done((bf16[144,512]{1,0:T(8,128)(2,1)S(1)}, bf16[144,512]{1,0:T(8,128)(2,1)S(1)}, u32[]{:S(2)}, u32[]{:S(2)}) %collective-permute-start.22) | collective-permute-done | bytes 147488 | tf_op jit(solution)/shard_map/ppermute | solution.py:39
  106.2 4.8 %collective-permute-done.29 = bf16[32,1152]{1,0:T(8,128)(2,1)S(1)} collective-permute-done((bf16[32,1152]{1,0:T(8,128)(2,1)S(1)}, bf16[32,1152]{1,0:T(8,128)(2,1)S(1)}, u32[]{:S(2)}, u32[]{:S(2)}) %collective-permute-start.29) | collective-permute-done | bytes 73760 | tf_op jit(solution)/shard_map/ppermute | solution.py:44
  111.0 0.2 multiply_reduce_fusion.1
  111.3 2.3 %collective-permute-start.26 = (bf16[18,1152]{1,0:T(8,128)(2,1)S(1)}, bf16[18,1152]{1,0:T(8,128)(2,1)S(1)}, u32[]{:S(2)}, u32[]{:S(2)}) collective-permute-start(bf16[18,1152]{1,0:T(8,128)(2,1)S(1)} %get-tuple-element.128), channel_id=1, source_target_pairs={{0,16},{2,18},{4,20},{6,22},{8,24},{10,26},{12,28},{14,30},{16,0},... | collective-permute-start | bytes 124424 | tf_op jit(solution)/shard_map/ppermute | solution.py:39
  113.6 0.8 collective-permute-start.27
  114.4 2.7 %collective-permute-start.28 = (bf16[18,1152]{1,0:T(8,128)(2,1)S(1)}, bf16[18,1152]{1,0:T(8,128)(2,1)S(1)}, u32[]{:S(2)}, u32[]{:S(2)}) collective-permute-start(bf16[18,1152]{1,0:T(8,128)(2,1)S(1)} %get-tuple-element.129), channel_id=1, source_target_pairs={{0,24},{2,26},{4,28},{6,30},{8,0},{10,2},{12,4},{14,6},{16,8},{18,... | collective-permute-start | bytes 124424 | tf_op jit(solution)/shard_map/ppermute | solution.py:39
  117.3 0.3 collective-permute-start.30
  117.5 0.8 collective-permute-done.26
  118.4 0.6 collective-permute-done.27
  119.0 1.5 %collective-permute-done.30 = bf16[32,1152]{1,0:T(8,128)(2,1)S(1)} collective-permute-done((bf16[32,1152]{1,0:T(8,128)(2,1)S(1)}, bf16[32,1152]{1,0:T(8,128)(2,1)S(1)}, u32[]{:S(2)}, u32[]{:S(2)}) %collective-permute-start.30) | collective-permute-done | bytes 73760 | tf_op jit(solution)/shard_map/ppermute | solution.py:48
  120.6 5.5 %collective-permute-start.31 = (f32[9,1152]{1,0:T(8,128)S(1)}, f32[9,1152]{1,0:T(8,128)S(1)}, u32[]{:S(2)}, u32[]{:S(2)}) collective-permute-start(f32[9,1152]{1,0:T(8,128)S(1)} %slice_select_fusion), channel_id=1, source_target_pairs={{0,2},{2,0},{4,6},{6,4},{8,10},{10,8},{12,14},{14,12},{16,18},{18,... | collective-permute-start | bytes 124424 | tf_op jit(solution)/shard_map/ppermute | solution.py:39
  126.1 0.7 maximum_select_fusion
  126.8 0.2 collective-permute-done.31
  127.0 0.7 pad_maximum_fusion.2
  (94 shorter events, 1.8 us)
Async XLA Ops:
  1.3 8.1 %copy-start.17 = (s32[4]{0:T(128)S(1)}, s32[4]{0:T(128)}, u32[]{:S(2)}) copy-start(s32[4]{0:T(128)} %constant.187.clone) | copy-start | bytes 52
  1.3 8.2 %copy-start.18 = (s32[32]{0:T(128)S(1)}, s32[32]{0:T(128)}, u32[]{:S(2)}) copy-start(s32[32]{0:T(128)} %param.17) | copy-start | bytes 388
  1.3 9.7 %copy-start.16 = (f32[729]{0:T(1024)S(1)}, f32[729]{0:T(1024)}, u32[]{:S(2)}) copy-start(f32[729]{0:T(1024)} %param.21) | copy-start | bytes 8752
  3.0 17.0 %copy-start.1 = (bf16[32,1152]{1,0:T(8,128)(2,1)S(1)}, bf16[32,1152]{1,0:T(8,128)(2,1)}, u32[]{:S(2)}) copy-start(bf16[32,1152]{1,0:T(8,128)(2,1)} %own_ref.1) | copy-start | bytes 221188
  3.0 40.5 %collective-permute-start.10 = (bf16[729,2152]{1,0:T(8,128)(2,1)}, bf16[729,2152]{1,0:T(8,128)(2,1)}, u32[]{:S(2)}, u32[]{:S(2)}) collective-permute-start(bf16[729,2152]{1,0:T(8,128)(2,1)} %hidden_hbm), channel_id=1, source_target_pairs={{0,2},{2,0},{4,6},{6,4},{8,10},{10,8},{12,14},{14,12},{16,18},{18,... | collective-permute-start | bytes 9412856 | tf_op jit(solution)/shard_map/ppermute | solution.py:39
  6.3 13.7 %collective-permute-start = (bf16[32,1152]{1,0:T(8,128)(2,1)}, bf16[32,1152]{1,0:T(8,128)(2,1)S(1)}, u32[]{:S(2)}, u32[]{:S(2)}) collective-permute-start(bf16[32,1152]{1,0:T(8,128)(2,1)} %shard_map.148), channel_id=1, source_target_pairs={{0,4},{2,6},{4,8},{6,10},{8,12},{10,14},{12,16},{14,18},{16,20},{1... | collective-permute-start | bytes 221192 | tf_op jit(solution)/shard_map/ppermute | solution.py:44
  6.3 5.7 %collective-permute-start.6 = (f32[729]{0:T(1024)}, f32[729]{0:T(1024)S(1)}, u32[]{:S(2)}, u32[]{:S(2)}) collective-permute-start(f32[729]{0:T(1024)} %param.21), channel_id=1, source_target_pairs={{0,2},{2,0},{4,6},{6,4},{8,10},{10,8},{12,14},{14,12},{16,18},{18,... | collective-permute-start | bytes 8756 | tf_op jit(solution)/shard_map/ppermute | solution.py:39
  6.4 37.1 %collective-permute-start.8 = (bf16[729,1152]{1,0:T(8,128)(2,1)}, bf16[729,1152]{1,0:T(8,128)(2,1)}, u32[]{:S(2)}, u32[]{:S(2)}) collective-permute-start(bf16[729,1152]{1,0:T(8,128)(2,1)} %cotangent_hbm), channel_id=1, source_target_pairs={{0,2},{2,0},{4,6},{6,4},{8,10},{10,8},{12,14},{14,12},{16,18},{18,... | collective-permute-start | bytes 5038856 | tf_op jit(solution)/shard_map/ppermute | solution.py:39
  6.8 1.5 %copy-start.3 = (bf16[729,1152]{1,0:T(8,128)(2,1)S(1)}, bf16[729,1152]{1,0:T(8,128)(2,1)}, u32[]{:S(2)}) copy-start(bf16[729,1152]{1,0:T(8,128)(2,1)} %normed_ref) | copy-start | bytes 5038852
  8.2 3.7 %copy-start.13 = (bf16[32,1152]{1,0:T(8,128)(2,1)S(1)}, bf16[32,1152]{1,0:T(8,128)(2,1)}, u32[]{:S(2)}) copy-start(bf16[32,1152]{1,0:T(8,128)(2,1)} %shard_map.148) | copy-start | bytes 221188
  9.1 26.3 %copy-start = (bf16[1152,768]{1,0:T(8,128)(2,1)}, bf16[1152,768]{1,0:T(8,128)(2,1)S(1)}, u32[]{:S(2)}) copy-start(bf16[1152,768]{1,0:T(8,128)(2,1)S(1)} %shard_map.153.normed0_hbm) | copy-start | bytes 5308420
  9.1 47.7 %collective-permute-start.13 = (bf16[1152,768]{1,0:T(8,128)(2,1)S(1)}, bf16[1152,768]{1,0:T(8,128)(2,1)}, u32[]{:S(2)}, u32[]{:S(2)}) collective-permute-start(bf16[1152,768]{1,0:T(8,128)(2,1)S(1)} %shard_map.153.normed0_hbm), channel_id=1, source_target_pairs={{0,2},{2,0},{4,6},{6,4},{8,10},{10,8},{12,14},{14,12},{16,18},{18,... | collective-permute-start | bytes 5308424 | tf_op jit(solution)/shard_map/ppermute | solution.py:39
  11.0 28.7 %copy-start.7 = (f32[2]{0:T(128)}, f32[2]{0:T(128)S(1)}, u32[]{:S(2)}) copy-start(f32[2]{0:T(128)S(1)} %pad_maximum_fusion.3.scalar_ref) | copy-start | bytes 28
  11.9 12.8 %collective-permute-start.3 = (bf16[32,1152]{1,0:T(8,128)(2,1)S(1)}, bf16[32,1152]{1,0:T(8,128)(2,1)S(1)}, u32[]{:S(2)}, u32[]{:S(2)}) collective-permute-start(bf16[32,1152]{1,0:T(8,128)(2,1)S(1)} %copy-done.13), channel_id=1, source_target_pairs={{2,16},{6,20},{10,24},{14,28},{18,32},{22,36},{26,40},{30,44},{34,... | collective-permute-start | bytes 221192 | tf_op jit(solution)/shard_map/ppermute | solution.py:44
  20.0 3.6 %collective-permute-start.1 = (bf16[32,1152]{1,0:T(8,128)(2,1)S(1)}, bf16[32,1152]{1,0:T(8,128)(2,1)S(1)}, u32[]{:S(2)}, u32[]{:S(2)}) collective-permute-start(bf16[32,1152]{1,0:T(8,128)(2,1)S(1)} %copy-done.1), channel_id=1, source_target_pairs={{0,1},{1,0},{2,3},{3,2},{4,5},{5,4},{6,7},{7,6},{8,9},{9,8},{10,11... | collective-permute-start | bytes 221192 | tf_op jit(solution)/shard_map/ppermute | solution.py:48
  23.6 16.2 %copy-start.4 = (bf16[32,1152]{1,0:T(8,128)(2,1)}, bf16[32,1152]{1,0:T(8,128)(2,1)S(1)}, u32[]{:S(2)}) copy-start(bf16[32,1152]{1,0:T(8,128)(2,1)S(1)} %collective-permute-done.1.other_ref) | copy-start | bytes 221188
  23.6 14.2 %collective-permute-start.2 = (bf16[64,1152]{1,0:T(8,128)(2,1)S(1)}, bf16[64,1152]{1,0:T(8,128)(2,1)S(1)}, u32[]{:S(2)}, u32[]{:S(2)}) collective-permute-start(bf16[64,1152]{1,0:T(8,128)(2,1)S(1)} %pad_maximum_fusion.1.refs_0_), channel_id=1, source_target_pairs={{0,8},{2,10},{4,12},{6,14},{8,16},{10,18},{12,20},{14,22},{16,24},... | collective-permute-start | bytes 442376 | tf_op jit(solution)/shard_map/ppermute | solution.py:44
  24.8 10.6 %collective-permute-start.4 = (s32[32]{0:T(128)S(1)}, s32[32]{0:T(128)S(1)}, u32[]{:S(2)}, u32[]{:S(2)}) collective-permute-start(s32[32]{0:T(128)S(1)} %copy-done.18), channel_id=1, source_target_pairs={{0,1},{1,0},{2,3},{3,2},{4,5},{5,4},{6,7},{7,6},{8,9},{9,8},{10,11... | collective-permute-start | bytes 392 | tf_op jit(solution)/shard_map/ppermute | solution.py:48
  26.4 13.4 %copy-start.5 = (s32[2]{0:T(128)S(1)}, s32[2]{0:T(128)}, u32[]{:S(2)}) copy-start(s32[2]{0:T(128)} %pad_add_fusion.place_ref) | copy-start | bytes 28
  35.4 4.3 %collective-permute-start.7 = (bf16[64,1152]{1,0:T(8,128)(2,1)S(1)}, bf16[64,1152]{1,0:T(8,128)(2,1)S(1)}, u32[]{:S(2)}, u32[]{:S(2)}) collective-permute-start(bf16[64,1152]{1,0:T(8,128)(2,1)S(1)} %pad_maximum_fusion.1.refs_0_), channel_id=1, source_target_pairs={{0,2},{2,0},{4,6},{6,4},{8,10},{10,8},{12,14},{14,12},{16,18},{18,... | collective-permute-start | bytes 442376 | tf_op jit(solution)/shard_map/ppermute | solution.py:39
  37.8 1.4 %collective-permute-start.5 = (bf16[64,1152]{1,0:T(8,128)(2,1)S(1)}, bf16[64,1152]{1,0:T(8,128)(2,1)S(1)}, u32[]{:S(2)}, u32[]{:S(2)}) collective-permute-start(bf16[64,1152]{1,0:T(8,128)(2,1)S(1)} %collective-permute-done.2.refs_1_), channel_id=1, source_target_pairs={{0,2},{2,0},{4,6},{6,4},{8,10},{10,8},{12,14},{14,12},{16,18},{18,... | collective-permute-start | bytes 442376 | tf_op jit(solution)/shard_map/ppermute | solution.py:39
  41.3 0.7 copy-start.8
  42.0 10.4 %copy-start.6 = (f32[1,1152]{1,0:T(1,128)}, f32[1,1152]{1,0:T(1,128)S(1)}, u32[]{:S(2)}) copy-start(f32[1,1152]{1,0:T(1,128)S(1)} %get-tuple-element.80.mine_ref) | copy-start | bytes 13828
  42.1 13.7 %collective-permute-start.12 = (bf16[32,1152]{1,0:T(8,128)(2,1)S(1)}, bf16[32,1152]{1,0:T(8,128)(2,1)S(1)}, u32[]{:S(2)}, u32[]{:S(2)}) collective-permute-start(bf16[32,1152]{1,0:T(8,128)(2,1)S(1)} %get-tuple-element.86), channel_id=1, source_target_pairs={{0,1},{1,0},{2,3},{3,2},{4,5},{5,4},{6,7},{7,6},{8,9},{9,8},{10,11... | collective-permute-start | bytes 221192 | tf_op jit(solution)/shard_map/ppermute | solution.py:48
  42.4 10.0 %collective-permute-start.9 = (f32[1,1152]{1,0:T(1,128)S(1)}, f32[1,1152]{1,0:T(1,128)S(1)}, u32[]{:S(2)}, u32[]{:S(2)}) collective-permute-start(f32[1,1152]{1,0:T(1,128)S(1)} %get-tuple-element.80.mine_ref), channel_id=1, source_target_pairs={{0,1},{1,0},{2,3},{3,2},{4,5},{5,4},{6,7},{7,6},{8,9},{9,8},{10,11... | collective-permute-start | bytes 13832 | tf_op jit(solution)/shard_map/ppermute | solution.py:48
  52.5 0.6 copy-start.15
  54.8 1.9 %collective-permute-start.11 = (bf16[1,1152]{1,0:T(2,128)(2,1)}, bf16[1,1152]{1,0:T(2,128)(2,1)S(1)}, u32[]{:S(2)}, u32[]{:S(2)}) collective-permute-start(bf16[1,1152]{1,0:T(2,128)(2,1)} %shard_map.152.pooled0_ref), channel_id=1, source_target_pairs={{0,2},{2,0},{4,6},{6,4},{8,10},{10,8},{12,14},{14,12},{16,18},{18,... | collective-permute-start | bytes 6920 | tf_op jit(solution)/shard_map/ppermute | solution.py:39
  55.7 14.2 %copy-start.2 = (bf16[32,1152]{1,0:T(8,128)(2,1)S(1)}, bf16[32,1152]{1,0:T(8,128)(2,1)}, u32[]{:S(2)}) copy-start(bf16[32,1152]{1,0:T(8,128)(2,1)} %own_ref.1) | copy-start | bytes 221188
  55.7 14.4 %copy-start.9 = (bf16[128,1152]{1,0:T(8,128)(2,1)S(1)}, bf16[128,1152]{1,0:T(8,128)(2,1)}, u32[]{:S(2)}) copy-start(bf16[128,1152]{1,0:T(8,128)(2,1)} %copy-done.8) | copy-start | bytes 884740
  55.7 22.0 %copy-start.11 = (bf16[64,1152]{1,0:T(8,128)(2,1)S(1)}, bf16[64,1152]{1,0:T(8,128)(2,1)}, u32[]{:S(2)}) copy-start(bf16[64,1152]{1,0:T(8,128)(2,1)} %raw_ref.1) | copy-start | bytes 442372
  56.7 0.6 copy-start.14
  69.9 16.9 %copy-start.10 = (f32[4,144,512]{2,1,0:T(8,128)S(1)}, f32[4,144,512]{2,1,0:T(8,128)}, u32[]{:S(2)}) copy-start(f32[4,144,512]{2,1,0:T(8,128)} %get-tuple-element.93) | copy-start | bytes 3538948
  70.1 7.7 %collective-permute-start.15 = (bf16[128,1152]{1,0:T(8,128)(2,1)S(1)}, bf16[128,1152]{1,0:T(8,128)(2,1)S(1)}, u32[]{:S(2)}, u32[]{:S(2)}) collective-permute-start(bf16[128,1152]{1,0:T(8,128)(2,1)S(1)} %copy-done.9), channel_id=1, source_target_pairs={{0,2},{2,0},{4,6},{6,4},{8,10},{10,8},{12,14},{14,12},{16,18},{18,... | collective-permute-start | bytes 884744 | tf_op jit(solution)/shard_map/ppermute | solution.py:39
  70.5 16.3 %collective-permute-start.14 = (bf16[4,144,512]{2,1,0:T(8,128)(2,1)}, bf16[4,144,512]{2,1,0:T(8,128)(2,1)S(1)}, u32[]{:S(2)}, u32[]{:S(2)}) collective-permute-start(bf16[4,144,512]{2,1,0:T(8,128)(2,1)} %get-tuple-element.94), channel_id=1, source_target_pairs={{0,128},{2,130},{4,132},{6,134},{8,136},{10,138},{12,140},{14,142}... | collective-permute-start | bytes 1769480 | tf_op jit(solution)/shard_map/ppermute | solution.py:39
  73.7 22.1 %collective-permute-start.17 = (bf16[2,144,640]{2,1,0:T(8,128)(2,1)}, bf16[2,144,640]{2,1,0:T(8,128)(2,1)S(1)}, u32[]{:S(2)}, u32[]{:S(2)}) collective-permute-start(bf16[2,144,640]{2,1,0:T(8,128)(2,1)} %get-tuple-element.104), channel_id=1, source_target_pairs={{0,64},{2,66},{4,68},{6,70},{8,72},{10,74},{12,76},{14,78},{16,80}... | collective-permute-start | bytes 1105928 | tf_op jit(solution)/shard_map/ppermute | solution.py:39
  75.0 20.9 %collective-permute-start.18 = (bf16[2,144,640]{2,1,0:T(8,128)(2,1)}, bf16[2,144,640]{2,1,0:T(8,128)(2,1)S(1)}, u32[]{:S(2)}, u32[]{:S(2)}) collective-permute-start(bf16[2,144,640]{2,1,0:T(8,128)(2,1)} %get-tuple-element.105), channel_id=1, source_target_pairs={{0,32},{2,34},{4,36},{6,38},{8,40},{10,42},{12,44},{14,46},{16,48}... | collective-permute-start | bytes 1105928 | tf_op jit(solution)/shard_map/ppermute | solution.py:39
  75.3 23.2 %collective-permute-start.19 = (bf16[2,144,640]{2,1,0:T(8,128)(2,1)}, bf16[2,144,640]{2,1,0:T(8,128)(2,1)S(1)}, u32[]{:S(2)}, u32[]{:S(2)}) collective-permute-start(bf16[2,144,640]{2,1,0:T(8,128)(2,1)} %get-tuple-element.106), channel_id=1, source_target_pairs={{0,96},{2,98},{4,100},{6,102},{8,104},{10,106},{12,108},{14,110},{... | collective-permute-start | bytes 1105928 | tf_op jit(solution)/shard_map/ppermute | solution.py:39
  77.9 9.2 %collective-permute-start.16 = (bf16[64,1152]{1,0:T(8,128)(2,1)S(1)}, bf16[64,1152]{1,0:T(8,128)(2,1)S(1)}, u32[]{:S(2)}, u32[]{:S(2)}) collective-permute-start(bf16[64,1152]{1,0:T(8,128)(2,1)S(1)} %add_convert_fusion), channel_id=1, source_target_pairs={{0,248},{2,250},{4,252},{6,254},{8,0},{10,2},{12,4},{14,6},{16,8},... | collective-permute-start | bytes 442376 | tf_op jit(solution)/shard_map/ppermute | solution.py:44
  87.1 11.5 %copy-start.12 = (f32[2,144,640]{2,1,0:T(8,128)S(1)}, f32[2,144,640]{2,1,0:T(8,128)}, u32[]{:S(2)}) copy-start(f32[2,144,640]{2,1,0:T(8,128)} %get-tuple-element.103) | copy-start | bytes 2211844
  87.2 18.7 %collective-permute-start.24 = (bf16[32,1152]{1,0:T(8,128)(2,1)S(1)}, bf16[32,1152]{1,0:T(8,128)(2,1)S(1)}, u32[]{:S(2)}, u32[]{:S(2)}) collective-permute-start(bf16[32,1152]{1,0:T(8,128)(2,1)S(1)} %slice.107), channel_id=1, source_target_pairs={{0,252},{2,254},{4,0},{6,2},{8,4},{10,6},{12,8},{14,10},{16,12},{1... | collective-permute-start | bytes 221192 | tf_op jit(solution)/shard_map/ppermute | solution.py:44
  95.7 5.7 %collective-permute-start.21 = (bf16[144,512]{1,0:T(8,128)(2,1)S(1)}, bf16[144,512]{1,0:T(8,128)(2,1)S(1)}, u32[]{:S(2)}, u32[]{:S(2)}) collective-permute-start(bf16[144,512]{1,0:T(8,128)(2,1)S(1)} %get-tuple-element.125), channel_id=1, source_target_pairs={{0,64},{2,66},{4,68},{6,70},{8,72},{10,74},{12,76},{14,78},{16,80}... | collective-permute-start | bytes 442376 | tf_op jit(solution)/shard_map/ppermute | solution.py:39
  95.8 9.9 %collective-permute-start.22 = (bf16[144,512]{1,0:T(8,128)(2,1)S(1)}, bf16[144,512]{1,0:T(8,128)(2,1)S(1)}, u32[]{:S(2)}, u32[]{:S(2)}) collective-permute-start(bf16[144,512]{1,0:T(8,128)(2,1)S(1)} %get-tuple-element.127), channel_id=1, source_target_pairs={{0,32},{2,34},{4,36},{6,38},{8,40},{10,42},{12,44},{14,46},{16,48}... | collective-permute-start | bytes 442376 | tf_op jit(solution)/shard_map/ppermute | solution.py:39
  95.9 9.8 %collective-permute-start.23 = (bf16[144,512]{1,0:T(8,128)(2,1)S(1)}, bf16[144,512]{1,0:T(8,128)(2,1)S(1)}, u32[]{:S(2)}, u32[]{:S(2)}) collective-permute-start(bf16[144,512]{1,0:T(8,128)(2,1)S(1)} %get-tuple-element.126), channel_id=1, source_target_pairs={{0,96},{2,98},{4,100},{6,102},{8,104},{10,106},{12,108},{14,110},{... | collective-permute-start | bytes 442376 | tf_op jit(solution)/shard_map/ppermute | solution.py:39
  98.8 7.0 %collective-permute-start.20 = (bf16[144,640]{1,0:T(8,128)(2,1)S(1)}, bf16[144,640]{1,0:T(8,128)(2,1)S(1)}, u32[]{:S(2)}, u32[]{:S(2)}) collective-permute-start(bf16[144,640]{1,0:T(8,128)(2,1)S(1)} %fusion.2), channel_id=1, source_target_pairs={{0,128},{2,130},{4,132},{6,134},{8,136},{10,138},{12,140},{14,142}... | collective-permute-start | bytes 552968 | tf_op jit(solution)/shard_map/ppermute | solution.py:39
  101.4 9.6 %collective-permute-start.29 = (bf16[32,1152]{1,0:T(8,128)(2,1)S(1)}, bf16[32,1152]{1,0:T(8,128)(2,1)S(1)}, u32[]{:S(2)}, u32[]{:S(2)}) collective-permute-start(bf16[32,1152]{1,0:T(8,128)(2,1)S(1)} %get-tuple-element.113), channel_id=1, source_target_pairs={{0,242},{4,246},{8,250},{12,254},{16,2},{20,6},{24,10},{28,14},{32... | collective-permute-start | bytes 221192 | tf_op jit(solution)/shard_map/ppermute | solution.py:44
  106.0 5.1 %collective-permute-start.25 = (bf16[4,18,1152]{2,1,0:T(8,128)(2,1)S(1)}, bf16[4,18,1152]{2,1,0:T(8,128)(2,1)S(1)}, u32[]{:S(2)}, u32[]{:S(2)}) collective-permute-start(bf16[4,18,1152]{2,1,0:T(8,128)(2,1)S(1)} %fusion.1), channel_id=1, source_target_pairs={{0,4},{2,6},{4,0},{6,2},{8,12},{10,14},{12,8},{14,10},{16,20},{18,... | collective-permute-start | bytes 497672 | tf_op jit(solution)/shard_map/ppermute | solution.py:559
  111.3 7.1 %collective-permute-start.26 = (bf16[18,1152]{1,0:T(8,128)(2,1)S(1)}, bf16[18,1152]{1,0:T(8,128)(2,1)S(1)}, u32[]{:S(2)}, u32[]{:S(2)}) collective-permute-start(bf16[18,1152]{1,0:T(8,128)(2,1)S(1)} %get-tuple-element.128), channel_id=1, source_target_pairs={{0,16},{2,18},{4,20},{6,22},{8,24},{10,26},{12,28},{14,30},{16,0},... | collective-permute-start | bytes 124424 | tf_op jit(solution)/shard_map/ppermute | solution.py:39
  113.6 5.4 %collective-permute-start.27 = (bf16[18,1152]{1,0:T(8,128)(2,1)S(1)}, bf16[18,1152]{1,0:T(8,128)(2,1)S(1)}, u32[]{:S(2)}, u32[]{:S(2)}) collective-permute-start(bf16[18,1152]{1,0:T(8,128)(2,1)S(1)} %get-tuple-element.130), channel_id=1, source_target_pairs={{0,8},{2,10},{4,12},{6,14},{8,16},{10,18},{12,20},{14,22},{16,24},... | collective-permute-start | bytes 124424 | tf_op jit(solution)/shard_map/ppermute | solution.py:39
  114.4 4.6 %collective-permute-start.28 = (bf16[18,1152]{1,0:T(8,128)(2,1)S(1)}, bf16[18,1152]{1,0:T(8,128)(2,1)S(1)}, u32[]{:S(2)}, u32[]{:S(2)}) collective-permute-start(bf16[18,1152]{1,0:T(8,128)(2,1)S(1)} %get-tuple-element.129), channel_id=1, source_target_pairs={{0,24},{2,26},{4,28},{6,30},{8,0},{10,2},{12,4},{14,6},{16,8},{18,... | collective-permute-start | bytes 124424 | tf_op jit(solution)/shard_map/ppermute | solution.py:39
  117.3 3.3 %collective-permute-start.30 = (bf16[32,1152]{1,0:T(8,128)(2,1)S(1)}, bf16[32,1152]{1,0:T(8,128)(2,1)S(1)}, u32[]{:S(2)}, u32[]{:S(2)}) collective-permute-start(bf16[32,1152]{1,0:T(8,128)(2,1)S(1)} %divide_convert_fusion.1), channel_id=1, source_target_pairs={{0,1},{1,0},{2,3},{3,2},{4,5},{5,4},{6,7},{7,6},{8,9},{9,8},{10,11... | collective-permute-start | bytes 221192 | tf_op jit(solution)/shard_map/ppermute | solution.py:48
  120.6 6.4 %collective-permute-start.31 = (f32[9,1152]{1,0:T(8,128)S(1)}, f32[9,1152]{1,0:T(8,128)S(1)}, u32[]{:S(2)}, u32[]{:S(2)}) collective-permute-start(f32[9,1152]{1,0:T(8,128)S(1)} %slice_select_fusion), channel_id=1, source_target_pairs={{0,2},{2,0},{4,6},{6,4},{8,10},{10,8},{12,14},{14,12},{16,18},{18,... | collective-permute-start | bytes 124424 | tf_op jit(solution)/shard_map/ppermute | solution.py:39

commit v3 on v1

--- a/solution.py
+++ b/solution.py
@@ -147,24 +147,6 @@
         other,
         *window,
     )
-
-
-def pooled_kernel(place_ref, scalar_ref, own_ref, other_ref, mine_ref, theirs_ref, pooled_ref):
-    raw = jnp.where(place_ref[1] == 0, own_ref[:1, :].astype(f32), other_ref[:1, :].astype(f32))
-    unit, length = unit_rows(raw)
-    direction = scalar_ref[0] * (mine_ref[...] + theirs_ref[...])
-    pooled_ref[...] = project_back(unit, length, direction).astype(bf16)
-
-
-def pooled_row(place, scalars, own, other, mine, theirs):
-    smem = pl.BlockSpec(memory_space=pltpu.SMEM)
-    vmem = pl.BlockSpec(memory_space=pltpu.VMEM)
-    return pl.pallas_call(
-        pooled_kernel,
-        in_specs=[smem, smem] + [vmem] * 4,
-        out_specs=vmem,
-        out_shape=jax.ShapeDtypeStruct(mine.shape, bf16),
-    )(place, scalars, own, other, mine, theirs)
 
 
 def transpose_kernel(patches, normed_ref, out_ref):
@@ -282,8 +264,8 @@
 def terms_kernel(
     place_ref,
     targets_ref,
-    pooled0_ref,
-    pooled1_ref,
+    row0_ref,
+    row1_ref,
     weight_tail,
     normed0_hbm,
     normed1_hbm,
@@ -329,9 +311,11 @@
             (base_hbm.at[:, part_a], base.at[i, :, part_a]),
         ]
     loads = copy_all(pairs, sems, 0)
-    pooled = jnp.concatenate(
-        [jnp.broadcast_to(ref[...].astype(f32), (8, width)) for ref in (pooled0_ref, pooled1_ref)], axis=0
-    ).astype(bf16)
+    pooled = []
+    for ref in (row0_ref, row1_ref):
+        unit, length = unit_rows(ref[1:2, :])
+        pooled.append(jnp.broadcast_to(project_back(unit, length, ref[0:1, :]), (8, width)))
+    pooled = jnp.concatenate(pooled, axis=0).astype(bf16)
     loads[0].wait()
     lift = jnp.concatenate([dot_nt(pooled, weight[...]), dot_nt(pooled, weight_tail[...])], axis=1)
 
@@ -366,13 +350,13 @@
         copy.wait()
 
 
-def up_terms(place, targets, split, normed_t, base, slope, weight, pooled):
+def up_terms(place, targets, split, normed_t, base, slope, weight, rows):
     width, depth = normed_t[0].shape
     patches, columns = base[0].shape
     height = width // (N_YH * N_X)
     hbm = pl.BlockSpec(memory_space=pl.ANY)
     tiles = columns // LANES - 1
-    row = pl.BlockSpec((1, width), lambda i, place, targets: (0, 0))
+    row = pl.BlockSpec((2, width), lambda i, place, targets: (0, 0))
     part_a, part_c = (N_YH, height, split), (N_X, height, columns - split)
     return pl.pallas_call(
         terms_kernel,
@@ -408,7 +392,7 @@
         ],
         compiler_params=pltpu.CompilerParams(vmem_limit_bytes=60 * 2**20),
         cost_estimate=LIGHT,
-    )(place, targets, *pooled, weight, *normed_t, *base, *slope, weight)
+    )(place, targets, *rows, weight, *normed_t, *base, *slope, weight)
 
 
 def per_device(
@@ -504,9 +488,10 @@
         spot, columns, cotangent_other, share_other, down_weight, hidden_other, LIGHT
     )
     zero_theirs, base_other, slope_other = lax.optimization_barrier((zero_theirs, base_other, slope_other))
-    pooled = pooled_row(spot, scalars, image_raw, image_other, zero_row, zero_theirs)
-    pooled_other = torus_send(pooled, core=1)
-    pooled_other, text_next, image_swapped = lax.optimization_barrier((pooled_other, text_next, image_swapped))
+    zero_raw = jnp.where(tensor_index == 0, image_raw[:1], image_other[:1]).astype(f32)
+    zero_both = jnp.concatenate([logit_scale * (zero_row + zero_theirs), zero_raw], axis=0)
+    zero_sibling = torus_send(zero_both, core=1)
+    zero_sibling, text_next, image_swapped = lax.optimization_barrier((zero_sibling, text_next, image_swapped))
 
     split = 5 * LANES
     a_keep, a_sent1, a_sent2, a_sent3, c_keep, c_sent = up_terms(
@@ -517,7 +502,7 @@
         [base_own, base_other],
         [slope_own, slope_other],
         down_weight,
-        [pooled, pooled_other],
+        [zero_both, zero_sibling],
     )
     a_keep, image_part, late_text, late_image = lax.optimization_barrier((a_keep, image_part, text_raw, image_raw))
     c_come = torus_send(c_sent, yh=1)

time: 127 us -> 125 us (0.984)
  starting transfers between devices: 45.4 us -> 49.4 us
  waiting for transfers between devices: 30 us -> 26.8 us
  Pallas kernels: 36.3 us -> 34.6 us
    ppermute x5, starting transfers between devices: 3.35 us -> 5.29 us  [tensor_swap(): return lax.ppermute(array, 'tensor', [(0, 1), (1, 0)])]
    ppermute x6, starting transfers between devices: 19.6 us -> 21.4 us  [ring_send(): return lax.ppermute(array, 'dp', pairs)]
    pallas_call x1 -> x0, Pallas kernels: 1.73 us -> none  [pooled_row(): pl.pallas_call(pooled_kernel, in_specs=[smem, smem] + [vmem] * 4, out_spe...]
    ppermute x20, waiting for transfers between devices: 22.2 us -> 20.6 us  [torus_send(): return lax.ppermute(array, 'dp', torus_pairs(**shift))]
    ppermute x6, waiting for transfers between devices: 6.51 us -> 5.23 us  [ring_send(): return lax.ppermute(array, 'dp', pairs)]
    unnamed x34 -> x26, local copies, waits for them, and re-layouts: 2.69 us -> 2.09 us
  transfers between devices with their start and end apart: 32 -> 32, of which waited for: 14 -> 13; matrix products, arithmetic and copies ran while one was open for 6% -> 6% of each run, Pallas kernels for 17% -> 16%
where the time goes in v3:
time: 125 us
  starting transfers between devices  49.4 us (40%)
  Pallas kernels  34.6 us (28%)
  waiting for transfers between devices  26.8 us (21%)
  other arithmetic  7.2 us (6%)
  local copies, waits for them, and re-layouts  4.53 us (4%)
  between operations  2.43 us (2%)
    ppermute x20, starting transfers between devices, torus_send(): return lax.ppermute(array, 'dp', torus_pairs(**shift))  21.6 us
    ppermute x6, starting transfers between devices, ring_send(): return lax.ppermute(array, 'dp', pairs)  21.4 us
    ppermute x20, waiting for transfers between devices, torus_send(): return lax.ppermute(array, 'dp', torus_pairs(**shift))  20.6 us
    pallas_call x2, Pallas kernels, hidden_base(): pl.pallas_call(base_kernel, grid_spec=pltpu.PrefetchScalarGridSpec(num_sc...  17.9 us
    pallas_call x1, Pallas kernels, up_terms(): pl.pallas_call(terms_kernel, grid_spec=pltpu.PrefetchScalarGridSpec(num_s...  12.6 us
    ppermute x5, starting transfers between devices, tensor_swap(): return lax.ppermute(array, 'tensor', [(0, 1), (1, 0)])  5.29 us
    ppermute x6, waiting for transfers between devices, ring_send(): return lax.ppermute(array, 'dp', pairs)  5.23 us
  transfers between devices with their start and end apart: 32, of which 13 were waited for; matrix products, arithmetic and copies ran while one was open for 6% of the time, Pallas kernels for 16%

profile of v3, /device:TPU:1, one launch (start us, length us, event | category | flops | bytes accessed | tf_op | source)
XLA Modules:
  0.0 124.9 jit_solution(6531224133415251606)
XLA Ops:
  0.6 0.6 pad_add_fusion.place_ref
  1.3 1.7 %shard_map.148 = bf16[32,1152]{1,0:T(8,128)(2,1)} custom-call(s32[2]{0:T(128)} %pad_add_fusion.place_ref, bf16[64,1152]{1,0:T(8,128)(2,1)} %raw_ref.1), custom_call_target="tpu_custom_call" | custom-call | tf_op jit(solution)/shard_map/pallas_call | solution.py:87
  2.9 2.5 %collective-permute-start = (bf16[32,1152]{1,0:T(8,128)(2,1)}, bf16[32,1152]{1,0:T(8,128)(2,1)S(1)}, u32[]{:S(2)}, u32[]{:S(2)}) collective-permute-start(bf16[32,1152]{1,0:T(8,128)(2,1)} %shard_map.148), channel_id=1, source_target_pairs={{0,4},{2,6},{4,8},{6,10},{8,12},{10,14},{12,16},{14,18},{16,20},{1... | collective-permute-start | bytes 221192 | tf_op jit(solution)/shard_map/ppermute | solution.py:44
  5.4 8.7 %collective-permute-start.3 = (bf16[32,1152]{1,0:T(8,128)(2,1)}, bf16[32,1152]{1,0:T(8,128)(2,1)S(1)}, u32[]{:S(2)}, u32[]{:S(2)}) collective-permute-start(bf16[32,1152]{1,0:T(8,128)(2,1)} %shard_map.148), channel_id=1, source_target_pairs={{2,16},{6,20},{10,24},{14,28},{18,32},{22,36},{26,40},{30,44},{34,... | collective-permute-start | bytes 221192 | tf_op jit(solution)/shard_map/ppermute | solution.py:44
  14.1 1.4 %collective-permute-start.1 = (bf16[32,1152]{1,0:T(8,128)(2,1)}, bf16[32,1152]{1,0:T(8,128)(2,1)S(1)}, u32[]{:S(2)}, u32[]{:S(2)}) collective-permute-start(bf16[32,1152]{1,0:T(8,128)(2,1)} %own_ref), channel_id=1, source_target_pairs={{0,1},{1,0},{2,3},{3,2},{4,5},{5,4},{6,7},{7,6},{8,9},{9,8},{10,11... | collective-permute-start | bytes 221192 | tf_op jit(solution)/shard_map/ppermute | solution.py:48
  15.5 0.5 collective-permute-start.11
  16.0 0.7 fusion.13
  16.7 0.7 iota_multiply_fusion
  18.9 1.5 %copy-done.1 = bf16[729,1152]{1,0:T(8,128)(2,1)S(1)} copy-done((bf16[729,1152]{1,0:T(8,128)(2,1)S(1)}, bf16[729,1152]{1,0:T(8,128)(2,1)}, u32[]{:S(2)}) %copy-start.1) | copy-done | bytes 1679640
  20.4 0.8 shard_map.152.normed0_hbm
  21.6 0.7 stack.56.targets_ref
  22.3 1.3 %collective-permute-start.2 = (bf16[64,1152]{1,0:T(8,128)(2,1)S(1)}, bf16[64,1152]{1,0:T(8,128)(2,1)S(1)}, u32[]{:S(2)}, u32[]{:S(2)}) collective-permute-start(bf16[64,1152]{1,0:T(8,128)(2,1)S(1)} %pad_maximum_fusion.1.refs_0_), channel_id=1, source_target_pairs={{0,8},{2,10},{4,12},{6,14},{8,16},{10,18},{12,20},{14,22},{16,24},... | collective-permute-start | bytes 442376 | tf_op jit(solution)/shard_map/ppermute | solution.py:44
  23.6 0.2 collective-permute-start.4
  23.7 0.6 broadcast_in_dim.8.share_ref
  24.4 9.0 %shard_map.149 = (bf16[729,1152]{1,0:T(8,128)(2,1)}, bf16[729,1152]{1,0:T(8,128)(2,1)}) custom-call(s32[2]{0:T(128)} %pad_add_fusion.place_ref, f32[8,768]{1,0:T(8,128)} %broadcast_in_dim.8.share_ref, bf16[2152,1152]{1,0:T(8,128)(2,1)} %weight_hbm.5, bf16[729,2152]{1,0:T(8,128)(2,1)} %hidden_hbm, bf16[729,1152]{1,0:T(8,128)(2,1)} %cotangent_hbm, ...), custom_call_target="tpu_custom_call" | custom-call | flops 10000000000 | bytes 1 | tf_op jit(solution)/shard_map/pallas_call | solution.py:231
  33.4 1.1 collective-permute-start.15
  34.5 0.1 collective-permute-start.7
  34.6 0.9 collective-permute-done.2.refs_1_
  35.5 1.4 %collective-permute-start.5 = (bf16[64,1152]{1,0:T(8,128)(2,1)S(1)}, bf16[64,1152]{1,0:T(8,128)(2,1)S(1)}, u32[]{:S(2)}, u32[]{:S(2)}) collective-permute-start(bf16[64,1152]{1,0:T(8,128)(2,1)S(1)} %collective-permute-done.2.refs_1_), channel_id=1, source_target_pairs={{0,2},{2,0},{4,6},{6,4},{8,10},{10,8},{12,14},{14,12},{16,18},{18,... | collective-permute-start | bytes 442376 | tf_op jit(solution)/shard_map/ppermute | solution.py:39
  37.0 0.1 copy.18.value_ref
  37.1 1.1 collective-permute-done.5.refs_3_
  38.3 0.6 broadcast_in_dim.9.share_ref
  38.9 1.6 %shard_map.150 = (f32[32,1152]{1,0:T(8,128)S(1)}, bf16[32,1152]{1,0:T(8,128)(2,1)S(1)}, f32[1,1152]{1,0:T(1,128)S(1)}, f32[128,1152]{1,0:T(8,128)S(1)}, bf16[128...) custom-call(s32[2]{0:T(128)S(1)} %copy-done.3, f32[2]{0:T(128)S(1)} %pad_maximum_fusion.4.scalar_ref, ...), custom_call_target="tpu_custom_call" | custom-call | flops 1 | bytes 1 | tf_op jit(solution)/shard_map/pallas_call | solution.py:125
  40.4 0.5 collective-permute-start.8
  40.9 1.7 %collective-permute-start.10 = (f32[1,1152]{1,0:T(1,128)S(1)}, f32[1,1152]{1,0:T(1,128)S(1)}, u32[]{:S(2)}, u32[]{:S(2)}) collective-permute-start(f32[1,1152]{1,0:T(1,128)S(1)} %get-tuple-element.81), channel_id=1, source_target_pairs={{0,1},{1,0},{2,3},{3,2},{4,5},{5,4},{6,7},{7,6},{8,9},{9,8},{10,11... | collective-permute-start | bytes 13832 | tf_op jit(solution)/shard_map/ppermute | solution.py:48
  42.6 0.9 collective-permute-start.14
  43.5 6.7 %collective-permute-start.13 = (bf16[64,1152]{1,0:T(8,128)(2,1)S(1)}, bf16[64,1152]{1,0:T(8,128)(2,1)S(1)}, u32[]{:S(2)}, u32[]{:S(2)}) collective-permute-start(bf16[64,1152]{1,0:T(8,128)(2,1)S(1)} %add_convert_fusion), channel_id=1, source_target_pairs={{0,248},{2,250},{4,252},{6,254},{8,0},{10,2},{12,4},{14,6},{16,8},... | collective-permute-start | bytes 442376 | tf_op jit(solution)/shard_map/ppermute | solution.py:44
  50.3 8.9 %shard_map.151 = (bf16[729,1152]{1,0:T(8,128)(2,1)}, bf16[729,1152]{1,0:T(8,128)(2,1)}) custom-call(s32[2]{0:T(128)} %pad_add_fusion.place_ref, f32[8,768]{1,0:T(8,128)} %broadcast_in_dim.9.share_ref, bf16[2152,1152]{1,0:T(8,128)(2,1)} %weight_hbm.5, bf16[729,2152]{1,0:T(8,128)(2,1)} %collective-permute-done.11.hidden_tail.hidden_hbm, ...), custom_call_target="tpu_custom_call" | custom-call | flops 1 | bytes 1 | tf_op jit(solution)/shard_map/pallas_call | solution.py:231
  59.3 0.9 collective-permute-start.12
  60.2 0.8 collective-permute-done.12.row1_ref
  61.0 0.6 copy-done.10
  61.6 12.6 %shard_map.153 = (f32[2,144,640]{2,1,0:T(8,128)}, bf16[2,144,640]{2,1,0:T(8,128)(2,1)}, bf16[2,144,640]{2,1,0:T(8,128)(2,1)}, bf16[2,144,640]{2,1,0:T(8,128)(2,1...) custom-call(s32[2]{0:T(128)} %pad_add_fusion.place_ref, s32[8]{0:T(128)} %stack.56.targets_ref, ...), custom_call_target="tpu_custom_call" | custom-call | flops 1 | bytes 1 | tf_op jit(solution)/shard_map/pallas_call | solution.py:361
  74.2 0.1 fusion.4
  74.3 2.8 %collective-permute-start.16 = (bf16[4,144,512]{2,1,0:T(8,128)(2,1)}, bf16[4,144,512]{2,1,0:T(8,128)(2,1)S(1)}, u32[]{:S(2)}, u32[]{:S(2)}) collective-permute-start(bf16[4,144,512]{2,1,0:T(8,128)(2,1)} %get-tuple-element.97), channel_id=1, source_target_pairs={{0,128},{2,130},{4,132},{6,134},{8,136},{10,138},{12,140},{14,142}... | collective-permute-start | bytes 1769480 | tf_op jit(solution)/shard_map/ppermute | solution.py:39
  77.1 2.7 %collective-permute-start.19 = (bf16[2,144,640]{2,1,0:T(8,128)(2,1)}, bf16[2,144,640]{2,1,0:T(8,128)(2,1)S(1)}, u32[]{:S(2)}, u32[]{:S(2)}) collective-permute-start(bf16[2,144,640]{2,1,0:T(8,128)(2,1)} %get-tuple-element.106), channel_id=1, source_target_pairs={{0,96},{2,98},{4,100},{6,102},{8,104},{10,106},{12,108},{14,110},{... | collective-permute-start | bytes 1105928 | tf_op jit(solution)/shard_map/ppermute | solution.py:39
  79.8 0.1 fusion.3
  79.9 0.2 multiply_reduce_fusion
  80.1 0.7 divide_convert_fusion
  80.9 10.0 %collective-permute-done.16 = bf16[4,144,512]{2,1,0:T(8,128)(2,1)S(1)} collective-permute-done((bf16[4,144,512]{2,1,0:T(8,128)(2,1)}, bf16[4,144,512]{2,1,0:T(8,128)(2,1)S(1)}, u32[]{:S(2)}, u32[]{:S(2)}) %collective-permute-start.16) | collective-permute-done | bytes 589856 | tf_op jit(solution)/shard_map/ppermute | solution.py:39
  90.9 1.5 %convert_add_fusion = f32[4,144,512]{2,1,0:T(8,128)S(1)} fusion(f32[4,144,512]{2,1,0:T(8,128)} %get-tuple-element.96, bf16[4,144,512]{2,1,0:T(8,128)(2,1)S(1)} %collective-permute-done.16), kind=kLoop, calls=%fused_computation | loop fusion | flops 589824 | bytes 2949120 | tf_op jit(solution)/shard_map/add | solution.py:510
  92.4 0.9 collective-permute-start.24
  93.5 0.1 collective-permute-start.21
  93.7 3.0 %collective-permute-done.18 = bf16[2,144,640]{2,1,0:T(8,128)(2,1)S(1)} collective-permute-done((bf16[2,144,640]{2,1,0:T(8,128)(2,1)}, bf16[2,144,640]{2,1,0:T(8,128)(2,1)S(1)}, u32[]{:S(2)}, u32[]{:S(2)}) %collective-permute-start.18) | collective-permute-done | bytes 368672 | tf_op jit(solution)/shard_map/ppermute | solution.py:39
  96.7 0.2 add_add_fusion
  96.9 1.5 %collective-permute-start.20 = (bf16[144,640]{1,0:T(8,128)(2,1)S(1)}, bf16[144,640]{1,0:T(8,128)(2,1)S(1)}, u32[]{:S(2)}, u32[]{:S(2)}) collective-permute-start(bf16[144,640]{1,0:T(8,128)(2,1)S(1)} %fusion.2), channel_id=1, source_target_pairs={{0,128},{2,130},{4,132},{6,134},{8,136},{10,138},{12,140},{14,142}... | collective-permute-start | bytes 552968 | tf_op jit(solution)/shard_map/ppermute | solution.py:39
  98.3 0.9 collective-permute-done.21
  99.2 1.3 %collective-permute-start.29 = (bf16[32,1152]{1,0:T(8,128)(2,1)S(1)}, bf16[32,1152]{1,0:T(8,128)(2,1)S(1)}, u32[]{:S(2)}, u32[]{:S(2)}) collective-permute-start(bf16[32,1152]{1,0:T(8,128)(2,1)S(1)} %get-tuple-element.113), channel_id=1, source_target_pairs={{0,242},{4,246},{8,250},{12,254},{16,2},{20,6},{24,10},{28,14},{32... | collective-permute-start | bytes 221192 | tf_op jit(solution)/shard_map/ppermute | solution.py:44
  100.5 2.7 %collective-permute-done.22 = bf16[144,512]{1,0:T(8,128)(2,1)S(1)} collective-permute-done((bf16[144,512]{1,0:T(8,128)(2,1)S(1)}, bf16[144,512]{1,0:T(8,128)(2,1)S(1)}, u32[]{:S(2)}, u32[]{:S(2)}) %collective-permute-start.22) | collective-permute-done | bytes 147488 | tf_op jit(solution)/shard_map/ppermute | solution.py:39
  103.5 1.0 collective-permute-start.25
  104.5 4.3 %collective-permute-done.29 = bf16[32,1152]{1,0:T(8,128)(2,1)S(1)} collective-permute-done((bf16[32,1152]{1,0:T(8,128)(2,1)S(1)}, bf16[32,1152]{1,0:T(8,128)(2,1)S(1)}, u32[]{:S(2)}, u32[]{:S(2)}) %collective-permute-start.29) | collective-permute-done | bytes 73760 | tf_op jit(solution)/shard_map/ppermute | solution.py:44
  108.8 0.2 multiply_reduce_fusion.1
  109.0 0.8 collective-permute-done.25
  109.9 0.1 collective-permute-start.26
  110.0 3.7 %collective-permute-start.27 = (bf16[18,1152]{1,0:T(8,128)(2,1)S(1)}, bf16[18,1152]{1,0:T(8,128)(2,1)S(1)}, u32[]{:S(2)}, u32[]{:S(2)}) collective-permute-start(bf16[18,1152]{1,0:T(8,128)(2,1)S(1)} %get-tuple-element.130), channel_id=1, source_target_pairs={{0,8},{2,10},{4,12},{6,14},{8,16},{10,18},{12,20},{14,22},{16,24},... | collective-permute-start | bytes 124424 | tf_op jit(solution)/shard_map/ppermute | solution.py:39
  113.7 1.4 %collective-permute-start.28 = (bf16[18,1152]{1,0:T(8,128)(2,1)S(1)}, bf16[18,1152]{1,0:T(8,128)(2,1)S(1)}, u32[]{:S(2)}, u32[]{:S(2)}) collective-permute-start(bf16[18,1152]{1,0:T(8,128)(2,1)S(1)} %get-tuple-element.129), channel_id=1, source_target_pairs={{0,24},{2,26},{4,28},{6,30},{8,0},{10,2},{12,4},{14,6},{16,8},{18,... | collective-permute-start | bytes 124424 | tf_op jit(solution)/shard_map/ppermute | solution.py:39
  115.1 0.1 divide_convert_fusion.1
  115.2 1.1 collective-permute-start.30
  116.3 0.8 collective-permute-done.26
  117.1 1.1 collective-permute-done.27
  118.3 0.2 collective-permute-done.30
  118.5 4.8 %collective-permute-start.31 = (f32[9,1152]{1,0:T(8,128)S(1)}, f32[9,1152]{1,0:T(8,128)S(1)}, u32[]{:S(2)}, u32[]{:S(2)}) collective-permute-start(f32[9,1152]{1,0:T(8,128)S(1)} %slice_select_fusion), channel_id=1, source_target_pairs={{0,2},{2,0},{4,6},{6,4},{8,10},{10,8},{12,14},{14,12},{16,18},{18,... | collective-permute-start | bytes 124424 | tf_op jit(solution)/shard_map/ppermute | solution.py:39
  123.3 0.7 maximum_select_fusion
  124.0 0.2 collective-permute-done.31
  124.2 0.7 pad_maximum_fusion.2
  (84 shorter events, 1.5 us)
Async XLA Ops:
  2.9 19.3 %collective-permute-start = (bf16[32,1152]{1,0:T(8,128)(2,1)}, bf16[32,1152]{1,0:T(8,128)(2,1)S(1)}, u32[]{:S(2)}, u32[]{:S(2)}) collective-permute-start(bf16[32,1152]{1,0:T(8,128)(2,1)} %shard_map.148), channel_id=1, source_target_pairs={{0,4},{2,6},{4,8},{6,10},{8,12},{10,14},{12,16},{14,18},{16,20},{1... | collective-permute-start | bytes 221192 | tf_op jit(solution)/shard_map/ppermute | solution.py:44
  5.4 28.0 %collective-permute-start.3 = (bf16[32,1152]{1,0:T(8,128)(2,1)}, bf16[32,1152]{1,0:T(8,128)(2,1)S(1)}, u32[]{:S(2)}, u32[]{:S(2)}) collective-permute-start(bf16[32,1152]{1,0:T(8,128)(2,1)} %shard_map.148), channel_id=1, source_target_pairs={{2,16},{6,20},{10,24},{14,28},{18,32},{22,36},{26,40},{30,44},{34,... | collective-permute-start | bytes 221192 | tf_op jit(solution)/shard_map/ppermute | solution.py:44
  14.1 8.1 %collective-permute-start.1 = (bf16[32,1152]{1,0:T(8,128)(2,1)}, bf16[32,1152]{1,0:T(8,128)(2,1)S(1)}, u32[]{:S(2)}, u32[]{:S(2)}) collective-permute-start(bf16[32,1152]{1,0:T(8,128)(2,1)} %own_ref), channel_id=1, source_target_pairs={{0,1},{1,0},{2,3},{3,2},{4,5},{5,4},{6,7},{7,6},{8,9},{9,8},{10,11... | collective-permute-start | bytes 221192 | tf_op jit(solution)/shard_map/ppermute | solution.py:48
  15.5 6.7 %collective-permute-start.6 = (f32[729]{0:T(1024)}, f32[729]{0:T(1024)S(1)}, u32[]{:S(2)}, u32[]{:S(2)}) collective-permute-start(f32[729]{0:T(1024)} %param.21), channel_id=1, source_target_pairs={{0,2},{2,0},{4,6},{6,4},{8,10},{10,8},{12,14},{14,12},{16,18},{18,... | collective-permute-start | bytes 8756 | tf_op jit(solution)/shard_map/ppermute | solution.py:39
  15.5 34.8 %collective-permute-start.11 = (bf16[729,2152]{1,0:T(8,128)(2,1)}, bf16[729,2152]{1,0:T(8,128)(2,1)}, u32[]{:S(2)}, u32[]{:S(2)}) collective-permute-start(bf16[729,2152]{1,0:T(8,128)(2,1)} %hidden_hbm), channel_id=1, source_target_pairs={{0,2},{2,0},{4,6},{6,4},{8,10},{10,8},{12,14},{14,12},{16,18},{18,... | collective-permute-start | bytes 9412856 | tf_op jit(solution)/shard_map/ppermute | solution.py:39
  18.9 1.5 %copy-start.1 = (bf16[729,1152]{1,0:T(8,128)(2,1)S(1)}, bf16[729,1152]{1,0:T(8,128)(2,1)}, u32[]{:S(2)}) copy-start(bf16[729,1152]{1,0:T(8,128)(2,1)} %normed_ref) | copy-start | bytes 5038852
  20.3 0.9 copy-start.11
  20.4 1.9 %copy-start.8 = (bf16[32,1152]{1,0:T(8,128)(2,1)S(1)}, bf16[32,1152]{1,0:T(8,128)(2,1)}, u32[]{:S(2)}) copy-start(bf16[32,1152]{1,0:T(8,128)(2,1)} %shard_map.148) | copy-start | bytes 221188
  20.4 3.2 %copy-start.12 = (s32[32]{0:T(128)S(1)}, s32[32]{0:T(128)}, u32[]{:S(2)}) copy-start(s32[32]{0:T(128)} %param.17) | copy-start | bytes 388
  21.2 12.2 %copy-start = (bf16[1152,768]{1,0:T(8,128)(2,1)}, bf16[1152,768]{1,0:T(8,128)(2,1)S(1)}, u32[]{:S(2)}) copy-start(bf16[1152,768]{1,0:T(8,128)(2,1)S(1)} %shard_map.152.normed0_hbm) | copy-start | bytes 5308420
  22.2 21.3 %collective-permute-start.9 = (bf16[729,1152]{1,0:T(8,128)(2,1)}, bf16[729,1152]{1,0:T(8,128)(2,1)}, u32[]{:S(2)}, u32[]{:S(2)}) collective-permute-start(bf16[729,1152]{1,0:T(8,128)(2,1)} %cotangent_hbm), channel_id=1, source_target_pairs={{0,2},{2,0},{4,6},{6,4},{8,10},{10,8},{12,14},{14,12},{16,18},{18,... | collective-permute-start | bytes 5038856 | tf_op jit(solution)/shard_map/ppermute | solution.py:39
  22.3 13.2 %collective-permute-start.2 = (bf16[64,1152]{1,0:T(8,128)(2,1)S(1)}, bf16[64,1152]{1,0:T(8,128)(2,1)S(1)}, u32[]{:S(2)}, u32[]{:S(2)}) collective-permute-start(bf16[64,1152]{1,0:T(8,128)(2,1)S(1)} %pad_maximum_fusion.1.refs_0_), channel_id=1, source_target_pairs={{0,8},{2,10},{4,12},{6,14},{8,16},{10,18},{12,20},{14,22},{16,24},... | collective-permute-start | bytes 442376 | tf_op jit(solution)/shard_map/ppermute | solution.py:44
  23.6 11.0 %collective-permute-start.4 = (s32[32]{0:T(128)S(1)}, s32[32]{0:T(128)S(1)}, u32[]{:S(2)}, u32[]{:S(2)}) collective-permute-start(s32[32]{0:T(128)S(1)} %copy-done.12), channel_id=1, source_target_pairs={{0,1},{1,0},{2,3},{3,2},{4,5},{5,4},{6,7},{7,6},{8,9},{9,8},{10,11... | collective-permute-start | bytes 392 | tf_op jit(solution)/shard_map/ppermute | solution.py:48
  24.4 14.5 %copy-start.2 = (bf16[32,1152]{1,0:T(8,128)(2,1)S(1)}, bf16[32,1152]{1,0:T(8,128)(2,1)}, u32[]{:S(2)}) copy-start(bf16[32,1152]{1,0:T(8,128)(2,1)} %own_ref) | copy-start | bytes 221188
  24.4 14.5 %copy-start.3 = (s32[2]{0:T(128)S(1)}, s32[2]{0:T(128)}, u32[]{:S(2)}) copy-start(s32[2]{0:T(128)} %pad_add_fusion.place_ref) | copy-start | bytes 28
  33.4 27.6 %collective-permute-start.15 = (bf16[1152,768]{1,0:T(8,128)(2,1)S(1)}, bf16[1152,768]{1,0:T(8,128)(2,1)}, u32[]{:S(2)}, u32[]{:S(2)}) collective-permute-start(bf16[1152,768]{1,0:T(8,128)(2,1)S(1)} %shard_map.152.normed0_hbm), channel_id=1, source_target_pairs={{0,2},{2,0},{4,6},{6,4},{8,10},{10,8},{12,14},{14,12},{16,18},{18,... | collective-permute-start | bytes 5308424 | tf_op jit(solution)/shard_map/ppermute | solution.py:39
  34.5 4.3 %collective-permute-start.7 = (bf16[64,1152]{1,0:T(8,128)(2,1)S(1)}, bf16[64,1152]{1,0:T(8,128)(2,1)S(1)}, u32[]{:S(2)}, u32[]{:S(2)}) collective-permute-start(bf16[64,1152]{1,0:T(8,128)(2,1)S(1)} %pad_maximum_fusion.1.refs_0_), channel_id=1, source_target_pairs={{0,2},{2,0},{4,6},{6,4},{8,10},{10,8},{12,14},{14,12},{16,18},{18,... | collective-permute-start | bytes 442376 | tf_op jit(solution)/shard_map/ppermute | solution.py:39
  35.5 2.7 %collective-permute-start.5 = (bf16[64,1152]{1,0:T(8,128)(2,1)S(1)}, bf16[64,1152]{1,0:T(8,128)(2,1)S(1)}, u32[]{:S(2)}, u32[]{:S(2)}) collective-permute-start(bf16[64,1152]{1,0:T(8,128)(2,1)S(1)} %collective-permute-done.2.refs_1_), channel_id=1, source_target_pairs={{0,2},{2,0},{4,6},{6,4},{8,10},{10,8},{12,14},{14,12},{16,18},{18,... | collective-permute-start | bytes 442376 | tf_op jit(solution)/shard_map/ppermute | solution.py:39
  40.4 2.1 %collective-permute-start.8 = (bf16[128,1152]{1,0:T(8,128)(2,1)S(1)}, bf16[128,1152]{1,0:T(8,128)(2,1)S(1)}, u32[]{:S(2)}, u32[]{:S(2)}) collective-permute-start(bf16[128,1152]{1,0:T(8,128)(2,1)S(1)} %get-tuple-element.80), channel_id=1, source_target_pairs={{0,2},{2,0},{4,6},{6,4},{8,10},{10,8},{12,14},{14,12},{16,18},{18,... | collective-permute-start | bytes 884744 | tf_op jit(solution)/shard_map/ppermute | solution.py:39
  40.9 18.3 %collective-permute-start.10 = (f32[1,1152]{1,0:T(1,128)S(1)}, f32[1,1152]{1,0:T(1,128)S(1)}, u32[]{:S(2)}, u32[]{:S(2)}) collective-permute-start(f32[1,1152]{1,0:T(1,128)S(1)} %get-tuple-element.81), channel_id=1, source_target_pairs={{0,1},{1,0},{2,3},{3,2},{4,5},{5,4},{6,7},{7,6},{8,9},{9,8},{10,11... | collective-permute-start | bytes 13832 | tf_op jit(solution)/shard_map/ppermute | solution.py:48
  42.6 16.6 %copy-start.6 = (bf16[128,1152]{1,0:T(8,128)(2,1)}, bf16[128,1152]{1,0:T(8,128)(2,1)S(1)}, u32[]{:S(2)}) copy-start(bf16[128,1152]{1,0:T(8,128)(2,1)S(1)} %collective-permute-done.8) | copy-start | bytes 884740
  42.6 17.6 %collective-permute-start.14 = (bf16[32,1152]{1,0:T(8,128)(2,1)S(1)}, bf16[32,1152]{1,0:T(8,128)(2,1)S(1)}, u32[]{:S(2)}, u32[]{:S(2)}) collective-permute-start(bf16[32,1152]{1,0:T(8,128)(2,1)S(1)} %get-tuple-element.89), channel_id=1, source_target_pairs={{0,1},{1,0},{2,3},{3,2},{4,5},{5,4},{6,7},{7,6},{8,9},{9,8},{10,11... | collective-permute-start | bytes 221192 | tf_op jit(solution)/shard_map/ppermute | solution.py:48
  43.5 16.6 %collective-permute-start.13 = (bf16[64,1152]{1,0:T(8,128)(2,1)S(1)}, bf16[64,1152]{1,0:T(8,128)(2,1)S(1)}, u32[]{:S(2)}, u32[]{:S(2)}) collective-permute-start(bf16[64,1152]{1,0:T(8,128)(2,1)S(1)} %add_convert_fusion), channel_id=1, source_target_pairs={{0,248},{2,250},{4,252},{6,254},{8,0},{10,2},{12,4},{14,6},{16,8},... | collective-permute-start | bytes 442376 | tf_op jit(solution)/shard_map/ppermute | solution.py:44
  59.2 1.7 %copy-start.9 = (f32[2,1152]{1,0:T(2,128)}, f32[2,1152]{1,0:T(2,128)S(1)}, u32[]{:S(2)}) copy-start(f32[2,1152]{1,0:T(2,128)S(1)} %pad_maximum_fusion.3.row0_ref) | copy-start | bytes 27652
  59.3 1.7 %collective-permute-start.12 = (f32[2,1152]{1,0:T(2,128)S(1)}, f32[2,1152]{1,0:T(2,128)S(1)}, u32[]{:S(2)}, u32[]{:S(2)}) collective-permute-start(f32[2,1152]{1,0:T(2,128)S(1)} %pad_maximum_fusion.3.row0_ref), channel_id=1, source_target_pairs={{0,2},{2,0},{4,6},{6,4},{8,10},{10,8},{12,14},{14,12},{16,18},{18,... | collective-permute-start | bytes 27656 | tf_op jit(solution)/shard_map/ppermute | solution.py:39
  60.1 19.7 %copy-start.4 = (bf16[64,1152]{1,0:T(8,128)(2,1)S(1)}, bf16[64,1152]{1,0:T(8,128)(2,1)}, u32[]{:S(2)}) copy-start(bf16[64,1152]{1,0:T(8,128)(2,1)} %raw_ref.1) | copy-start | bytes 442372
  61.0 0.6 copy-start.10
  74.3 16.6 %collective-permute-start.16 = (bf16[4,144,512]{2,1,0:T(8,128)(2,1)}, bf16[4,144,512]{2,1,0:T(8,128)(2,1)S(1)}, u32[]{:S(2)}, u32[]{:S(2)}) collective-permute-start(bf16[4,144,512]{2,1,0:T(8,128)(2,1)} %get-tuple-element.97), channel_id=1, source_target_pairs={{0,128},{2,130},{4,132},{6,134},{8,136},{10,138},{12,140},{14,142}... | collective-permute-start | bytes 1769480 | tf_op jit(solution)/shard_map/ppermute | solution.py:39
  77.1 16.5 %collective-permute-start.17 = (bf16[2,144,640]{2,1,0:T(8,128)(2,1)}, bf16[2,144,640]{2,1,0:T(8,128)(2,1)S(1)}, u32[]{:S(2)}, u32[]{:S(2)}) collective-permute-start(bf16[2,144,640]{2,1,0:T(8,128)(2,1)} %get-tuple-element.104), channel_id=1, source_target_pairs={{0,64},{2,66},{4,68},{6,70},{8,72},{10,74},{12,76},{14,78},{16,80}... | collective-permute-start | bytes 1105928 | tf_op jit(solution)/shard_map/ppermute | solution.py:39
  77.1 19.5 %collective-permute-start.18 = (bf16[2,144,640]{2,1,0:T(8,128)(2,1)}, bf16[2,144,640]{2,1,0:T(8,128)(2,1)S(1)}, u32[]{:S(2)}, u32[]{:S(2)}) collective-permute-start(bf16[2,144,640]{2,1,0:T(8,128)(2,1)} %get-tuple-element.105), channel_id=1, source_target_pairs={{0,32},{2,34},{4,36},{6,38},{8,40},{10,42},{12,44},{14,46},{16,48}... | collective-permute-start | bytes 1105928 | tf_op jit(solution)/shard_map/ppermute | solution.py:39
  77.1 19.5 %collective-permute-start.19 = (bf16[2,144,640]{2,1,0:T(8,128)(2,1)}, bf16[2,144,640]{2,1,0:T(8,128)(2,1)S(1)}, u32[]{:S(2)}, u32[]{:S(2)}) collective-permute-start(bf16[2,144,640]{2,1,0:T(8,128)(2,1)} %get-tuple-element.106), channel_id=1, source_target_pairs={{0,96},{2,98},{4,100},{6,102},{8,104},{10,106},{12,108},{14,110},{... | collective-permute-start | bytes 1105928 | tf_op jit(solution)/shard_map/ppermute | solution.py:39
  80.1 12.2 %copy-start.7 = (bf16[128,1152]{1,0:T(8,128)(2,1)S(1)}, bf16[128,1152]{1,0:T(8,128)(2,1)}, u32[]{:S(2)}) copy-start(bf16[128,1152]{1,0:T(8,128)(2,1)} %copy-done.6) | copy-start | bytes 884740
  92.3 4.3 %copy-start.5 = (f32[2,144,640]{2,1,0:T(8,128)S(1)}, f32[2,144,640]{2,1,0:T(8,128)}, u32[]{:S(2)}) copy-start(f32[2,144,640]{2,1,0:T(8,128)} %get-tuple-element.103) | copy-start | bytes 2211844
  92.4 10.9 %collective-permute-start.24 = (bf16[32,1152]{1,0:T(8,128)(2,1)S(1)}, bf16[32,1152]{1,0:T(8,128)(2,1)S(1)}, u32[]{:S(2)}, u32[]{:S(2)}) collective-permute-start(bf16[32,1152]{1,0:T(8,128)(2,1)S(1)} %slice.116), channel_id=1, source_target_pairs={{0,252},{2,254},{4,0},{6,2},{8,4},{10,6},{12,8},{14,10},{16,12},{1... | collective-permute-start | bytes 221192 | tf_op jit(solution)/shard_map/ppermute | solution.py:44
  93.5 5.7 %collective-permute-start.21 = (bf16[144,512]{1,0:T(8,128)(2,1)S(1)}, bf16[144,512]{1,0:T(8,128)(2,1)S(1)}, u32[]{:S(2)}, u32[]{:S(2)}) collective-permute-start(bf16[144,512]{1,0:T(8,128)(2,1)S(1)} %get-tuple-element.125), channel_id=1, source_target_pairs={{0,64},{2,66},{4,68},{6,70},{8,72},{10,74},{12,76},{14,78},{16,80}... | collective-permute-start | bytes 442376 | tf_op jit(solution)/shard_map/ppermute | solution.py:39
  93.6 9.5 %collective-permute-start.22 = (bf16[144,512]{1,0:T(8,128)(2,1)S(1)}, bf16[144,512]{1,0:T(8,128)(2,1)S(1)}, u32[]{:S(2)}, u32[]{:S(2)}) collective-permute-start(bf16[144,512]{1,0:T(8,128)(2,1)S(1)} %get-tuple-element.127), channel_id=1, source_target_pairs={{0,32},{2,34},{4,36},{6,38},{8,40},{10,42},{12,44},{14,46},{16,48}... | collective-permute-start | bytes 442376 | tf_op jit(solution)/shard_map/ppermute | solution.py:39
  96.6 6.5 %collective-permute-start.23 = (bf16[144,512]{1,0:T(8,128)(2,1)S(1)}, bf16[144,512]{1,0:T(8,128)(2,1)S(1)}, u32[]{:S(2)}, u32[]{:S(2)}) collective-permute-start(bf16[144,512]{1,0:T(8,128)(2,1)S(1)} %get-tuple-element.126), channel_id=1, source_target_pairs={{0,96},{2,98},{4,100},{6,102},{8,104},{10,106},{12,108},{14,110},{... | collective-permute-start | bytes 442376 | tf_op jit(solution)/shard_map/ppermute | solution.py:39
  96.9 6.4 %collective-permute-start.20 = (bf16[144,640]{1,0:T(8,128)(2,1)S(1)}, bf16[144,640]{1,0:T(8,128)(2,1)S(1)}, u32[]{:S(2)}, u32[]{:S(2)}) collective-permute-start(bf16[144,640]{1,0:T(8,128)(2,1)S(1)} %fusion.2), channel_id=1, source_target_pairs={{0,128},{2,130},{4,132},{6,134},{8,136},{10,138},{12,140},{14,142}... | collective-permute-start | bytes 552968 | tf_op jit(solution)/shard_map/ppermute | solution.py:39
  99.2 9.7 %collective-permute-start.29 = (bf16[32,1152]{1,0:T(8,128)(2,1)S(1)}, bf16[32,1152]{1,0:T(8,128)(2,1)S(1)}, u32[]{:S(2)}, u32[]{:S(2)}) collective-permute-start(bf16[32,1152]{1,0:T(8,128)(2,1)S(1)} %get-tuple-element.113), channel_id=1, source_target_pairs={{0,242},{4,246},{8,250},{12,254},{16,2},{20,6},{24,10},{28,14},{32... | collective-permute-start | bytes 221192 | tf_op jit(solution)/shard_map/ppermute | solution.py:44
  103.5 6.4 %collective-permute-start.25 = (bf16[4,18,1152]{2,1,0:T(8,128)(2,1)S(1)}, bf16[4,18,1152]{2,1,0:T(8,128)(2,1)S(1)}, u32[]{:S(2)}, u32[]{:S(2)}) collective-permute-start(bf16[4,18,1152]{2,1,0:T(8,128)(2,1)S(1)} %fusion.1), channel_id=1, source_target_pairs={{0,4},{2,6},{4,0},{6,2},{8,12},{10,14},{12,8},{14,10},{16,20},{18,... | collective-permute-start | bytes 497672 | tf_op jit(solution)/shard_map/ppermute | solution.py:542
  109.9 7.2 %collective-permute-start.26 = (bf16[18,1152]{1,0:T(8,128)(2,1)S(1)}, bf16[18,1152]{1,0:T(8,128)(2,1)S(1)}, u32[]{:S(2)}, u32[]{:S(2)}) collective-permute-start(bf16[18,1152]{1,0:T(8,128)(2,1)S(1)} %get-tuple-element.128), channel_id=1, source_target_pairs={{0,16},{2,18},{4,20},{6,22},{8,24},{10,26},{12,28},{14,30},{16,0},... | collective-permute-start | bytes 124424 | tf_op jit(solution)/shard_map/ppermute | solution.py:39
  110.0 8.2 %collective-permute-start.27 = (bf16[18,1152]{1,0:T(8,128)(2,1)S(1)}, bf16[18,1152]{1,0:T(8,128)(2,1)S(1)}, u32[]{:S(2)}, u32[]{:S(2)}) collective-permute-start(bf16[18,1152]{1,0:T(8,128)(2,1)S(1)} %get-tuple-element.130), channel_id=1, source_target_pairs={{0,8},{2,10},{4,12},{6,14},{8,16},{10,18},{12,20},{14,22},{16,24},... | collective-permute-start | bytes 124424 | tf_op jit(solution)/shard_map/ppermute | solution.py:39
  113.7 4.5 %collective-permute-start.28 = (bf16[18,1152]{1,0:T(8,128)(2,1)S(1)}, bf16[18,1152]{1,0:T(8,128)(2,1)S(1)}, u32[]{:S(2)}, u32[]{:S(2)}) collective-permute-start(bf16[18,1152]{1,0:T(8,128)(2,1)S(1)} %get-tuple-element.129), channel_id=1, source_target_pairs={{0,24},{2,26},{4,28},{6,30},{8,0},{10,2},{12,4},{14,6},{16,8},{18,... | collective-permute-start | bytes 124424 | tf_op jit(solution)/shard_map/ppermute | solution.py:39
  115.2 3.3 %collective-permute-start.30 = (bf16[32,1152]{1,0:T(8,128)(2,1)S(1)}, bf16[32,1152]{1,0:T(8,128)(2,1)S(1)}, u32[]{:S(2)}, u32[]{:S(2)}) collective-permute-start(bf16[32,1152]{1,0:T(8,128)(2,1)S(1)} %divide_convert_fusion.1), channel_id=1, source_target_pairs={{0,1},{1,0},{2,3},{3,2},{4,5},{5,4},{6,7},{7,6},{8,9},{9,8},{10,11... | collective-permute-start | bytes 221192 | tf_op jit(solution)/shard_map/ppermute | solution.py:48
  118.5 5.7 %collective-permute-start.31 = (f32[9,1152]{1,0:T(8,128)S(1)}, f32[9,1152]{1,0:T(8,128)S(1)}, u32[]{:S(2)}, u32[]{:S(2)}) collective-permute-start(f32[9,1152]{1,0:T(8,128)S(1)} %slice_select_fusion), channel_id=1, source_target_pairs={{0,2},{2,0},{4,6},{6,4},{8,10},{10,8},{12,14},{14,12},{16,18},{18,... | collective-permute-start | bytes 124424 | tf_op jit(solution)/shard_map/ppermute | solution.py:39

commit v4 on v3

--- a/solution.py
+++ b/solution.py
@@ -195,7 +195,7 @@
         sems,
         0,
     )
-    share = share_ref[...].T[:patches, :1]
+    share = jnp.broadcast_to(share_ref[...], (8, share_ref.shape[1])).T[:patches, :1]
 
     def block(weight_rows, hidden_block, where, ready):
         kept = gelu_slope(hidden_block.astype(f32))
@@ -450,7 +450,7 @@
     hidden_other = torus_send(hidden_pre, core=1)
     share_other = torus_send(pool_share, core=1)
     share_own, share_other = [
-        jnp.broadcast_to(jnp.pad(part, (0, 6 * LANES - part.shape[0]))[None, :], (8, 6 * LANES))
+        jnp.pad(part, (0, 6 * LANES - part.shape[0]))[None, :]
         for part in (pool_share, share_other)
     ]
     base_own, slope_own = hidden_base(

time: 125 us -> 125 us (level)
  transfers between devices with their start and end apart: 32 -> 32, of which waited for: 13 -> 12; matrix products, arithmetic and copies ran while one was open for 6% -> 7% of each run, Pallas kernels for 16% -> 16%
where the time goes in v4:
time: 125 us
  starting transfers between devices  49.1 us (39%)
  Pallas kernels  34.4 us (28%)
  waiting for transfers between devices  27.2 us (22%)
  other arithmetic  7.2 us (6%)
  local copies, waits for them, and re-layouts  4.55 us (4%)
  between operations  2.42 us (2%)
    ppermute x20, starting transfers between devices, torus_send(): return lax.ppermute(array, 'dp', torus_pairs(**shift))  21.7 us
    ppermute x6, starting transfers between devices, ring_send(): return lax.ppermute(array, 'dp', pairs)  20.7 us
    ppermute x20, waiting for transfers between devices, torus_send(): return lax.ppermute(array, 'dp', torus_pairs(**shift))  20.5 us
    pallas_call x2, Pallas kernels, hidden_base(): pl.pallas_call(base_kernel, grid_spec=pltpu.PrefetchScalarGridSpec(num_sc...  17.8 us
    pallas_call x1, Pallas kernels, up_terms(): pl.pallas_call(terms_kernel, grid_spec=pltpu.PrefetchScalarGridSpec(num_s...  12.6 us
    ppermute x6, waiting for transfers between devices, ring_send(): return lax.ppermute(array, 'dp', pairs)  5.91 us
    ppermute x5, starting transfers between devices, tensor_swap(): return lax.ppermute(array, 'tensor', [(0, 1), (1, 0)])  5.6 us
  transfers between devices with their start and end apart: 32, of which 12 were waited for; matrix products, arithmetic and copies ran while one was open for 7% of the time, Pallas kernels for 16%

profile of v4, /device:TPU:1, one launch (start us, length us, event | category | flops | bytes accessed | tf_op | source)
XLA Modules:
  0.0 124.9 jit_solution(15743288943627989977)
XLA Ops:
  0.6 0.6 pad_add_fusion.place_ref
  1.3 1.7 %shard_map.148 = bf16[32,1152]{1,0:T(8,128)(2,1)} custom-call(s32[2]{0:T(128)} %pad_add_fusion.place_ref, bf16[64,1152]{1,0:T(8,128)(2,1)} %raw_ref.1), custom_call_target="tpu_custom_call" | custom-call | tf_op jit(solution)/shard_map/pallas_call | solution.py:87
  2.9 2.5 %collective-permute-start = (bf16[32,1152]{1,0:T(8,128)(2,1)}, bf16[32,1152]{1,0:T(8,128)(2,1)S(1)}, u32[]{:S(2)}, u32[]{:S(2)}) collective-permute-start(bf16[32,1152]{1,0:T(8,128)(2,1)} %shard_map.148), channel_id=1, source_target_pairs={{0,4},{2,6},{4,8},{6,10},{8,12},{10,14},{12,16},{14,18},{16,20},{1... | collective-permute-start | bytes 221192 | tf_op jit(solution)/shard_map/ppermute | solution.py:44
  5.4 8.7 %collective-permute-start.3 = (bf16[32,1152]{1,0:T(8,128)(2,1)}, bf16[32,1152]{1,0:T(8,128)(2,1)S(1)}, u32[]{:S(2)}, u32[]{:S(2)}) collective-permute-start(bf16[32,1152]{1,0:T(8,128)(2,1)} %shard_map.148), channel_id=1, source_target_pairs={{2,16},{6,20},{10,24},{14,28},{18,32},{22,36},{26,40},{30,44},{34,... | collective-permute-start | bytes 221192 | tf_op jit(solution)/shard_map/ppermute | solution.py:44
  14.1 1.4 %collective-permute-start.1 = (bf16[32,1152]{1,0:T(8,128)(2,1)}, bf16[32,1152]{1,0:T(8,128)(2,1)S(1)}, u32[]{:S(2)}, u32[]{:S(2)}) collective-permute-start(bf16[32,1152]{1,0:T(8,128)(2,1)} %own_ref), channel_id=1, source_target_pairs={{0,1},{1,0},{2,3},{3,2},{4,5},{5,4},{6,7},{7,6},{8,9},{9,8},{10,11... | collective-permute-start | bytes 221192 | tf_op jit(solution)/shard_map/ppermute | solution.py:48
  15.5 0.5 collective-permute-start.11
  16.0 0.7 fusion.13
  16.7 0.7 iota_multiply_fusion
  18.9 1.5 %copy-done.1 = bf16[729,1152]{1,0:T(8,128)(2,1)S(1)} copy-done((bf16[729,1152]{1,0:T(8,128)(2,1)S(1)}, bf16[729,1152]{1,0:T(8,128)(2,1)}, u32[]{:S(2)}) %copy-start.1) | copy-done | bytes 1679640
  20.4 0.8 shard_map.152.normed0_hbm
  21.3 0.7 broadcast_in_dim.8.share_ref
  22.2 0.6 stack.56.targets_ref
  22.9 0.6 broadcast_in_dim.9.share_ref
  23.5 1.3 %collective-permute-start.2 = (bf16[64,1152]{1,0:T(8,128)(2,1)S(1)}, bf16[64,1152]{1,0:T(8,128)(2,1)S(1)}, u32[]{:S(2)}, u32[]{:S(2)}) collective-permute-start(bf16[64,1152]{1,0:T(8,128)(2,1)S(1)} %pad_maximum_fusion.1.refs_0_), channel_id=1, source_target_pairs={{0,8},{2,10},{4,12},{6,14},{8,16},{10,18},{12,20},{14,22},{16,24},... | collective-permute-start | bytes 442376 | tf_op jit(solution)/shard_map/ppermute | solution.py:44
  24.8 0.2 collective-permute-start.4
  25.0 8.9 %shard_map.149 = (bf16[729,1152]{1,0:T(8,128)(2,1)}, bf16[729,1152]{1,0:T(8,128)(2,1)}) custom-call(s32[2]{0:T(128)} %pad_add_fusion.place_ref, f32[1,768]{1,0:T(1,128)} %broadcast_in_dim.8.share_ref, bf16[2152,1152]{1,0:T(8,128)(2,1)} %weight_hbm.5, bf16[729,2152]{1,0:T(8,128)(2,1)} %hidden_hbm, bf16[729,1152]{1,0:T(8,128)(2,1)} %cotangent_hbm, ...), custom_call_target="tpu_custom_call" | custom-call | flops 10000000000 | bytes 1 | tf_op jit(solution)/shard_map/pallas_call | solution.py:231
  33.9 1.1 collective-permute-start.15
  35.0 0.1 collective-permute-start.7
  35.1 1.6 %collective-permute-done.2.refs_1_ = bf16[64,1152]{1,0:T(8,128)(2,1)S(1)} collective-permute-done((bf16[64,1152]{1,0:T(8,128)(2,1)S(1)}, bf16[64,1152]{1,0:T(8,128)(2,1)S(1)}, u32[]{:S(2)}, u32[]{:S(2)}) %collective-permute-start.2) | collective-permute-done | bytes 147488 | tf_op jit(solution)/shard_map/ppermute | solution.py:44
  36.7 1.5 %collective-permute-start.5 = (bf16[64,1152]{1,0:T(8,128)(2,1)S(1)}, bf16[64,1152]{1,0:T(8,128)(2,1)S(1)}, u32[]{:S(2)}, u32[]{:S(2)}) collective-permute-start(bf16[64,1152]{1,0:T(8,128)(2,1)S(1)} %collective-permute-done.2.refs_1_), channel_id=1, source_target_pairs={{0,2},{2,0},{4,6},{6,4},{8,10},{10,8},{12,14},{14,12},{16,18},{18,... | collective-permute-start | bytes 442376 | tf_op jit(solution)/shard_map/ppermute | solution.py:39
  38.3 0.1 copy.18.value_ref
  38.4 0.8 collective-permute-done.5.refs_3_
  39.2 1.6 %shard_map.150 = (f32[32,1152]{1,0:T(8,128)S(1)}, bf16[32,1152]{1,0:T(8,128)(2,1)S(1)}, f32[1,1152]{1,0:T(1,128)S(1)}, f32[128,1152]{1,0:T(8,128)S(1)}, bf16[128...) custom-call(s32[2]{0:T(128)S(1)} %copy-done.3, f32[2]{0:T(128)S(1)} %pad_maximum_fusion.4.scalar_ref, ...), custom_call_target="tpu_custom_call" | custom-call | flops 1 | bytes 1 | tf_op jit(solution)/shard_map/pallas_call | solution.py:125
  40.8 0.5 collective-permute-start.8
  41.2 2.0 %collective-permute-start.10 = (f32[1,1152]{1,0:T(1,128)S(1)}, f32[1,1152]{1,0:T(1,128)S(1)}, u32[]{:S(2)}, u32[]{:S(2)}) collective-permute-start(f32[1,1152]{1,0:T(1,128)S(1)} %get-tuple-element.81), channel_id=1, source_target_pairs={{0,1},{1,0},{2,3},{3,2},{4,5},{5,4},{6,7},{7,6},{8,9},{9,8},{10,11... | collective-permute-start | bytes 13832 | tf_op jit(solution)/shard_map/ppermute | solution.py:48
  43.2 0.9 collective-permute-start.14
  44.2 6.0 %collective-permute-start.13 = (bf16[64,1152]{1,0:T(8,128)(2,1)S(1)}, bf16[64,1152]{1,0:T(8,128)(2,1)S(1)}, u32[]{:S(2)}, u32[]{:S(2)}) collective-permute-start(bf16[64,1152]{1,0:T(8,128)(2,1)S(1)} %add_convert_fusion), channel_id=1, source_target_pairs={{0,248},{2,250},{4,252},{6,254},{8,0},{10,2},{12,4},{14,6},{16,8},... | collective-permute-start | bytes 442376 | tf_op jit(solution)/shard_map/ppermute | solution.py:44
  50.2 8.9 %shard_map.151 = (bf16[729,1152]{1,0:T(8,128)(2,1)}, bf16[729,1152]{1,0:T(8,128)(2,1)}) custom-call(s32[2]{0:T(128)} %pad_add_fusion.place_ref, f32[1,768]{1,0:T(1,128)} %broadcast_in_dim.9.share_ref, bf16[2152,1152]{1,0:T(8,128)(2,1)} %weight_hbm.5, bf16[729,2152]{1,0:T(8,128)(2,1)} %collective-permute-done.11.hidden_tail.hidden_hbm, ...), custom_call_target="tpu_custom_call" | custom-call | flops 1 | bytes 1 | tf_op jit(solution)/shard_map/pallas_call | solution.py:231
  59.2 0.9 collective-permute-start.12
  60.0 0.8 collective-permute-done.12.row1_ref
  60.9 0.6 copy-done.10
  61.5 12.6 %shard_map.153 = (f32[2,144,640]{2,1,0:T(8,128)}, bf16[2,144,640]{2,1,0:T(8,128)(2,1)}, bf16[2,144,640]{2,1,0:T(8,128)(2,1)}, bf16[2,144,640]{2,1,0:T(8,128)(2,1...) custom-call(s32[2]{0:T(128)} %pad_add_fusion.place_ref, s32[8]{0:T(128)} %stack.56.targets_ref, ...), custom_call_target="tpu_custom_call" | custom-call | flops 1 | bytes 1 | tf_op jit(solution)/shard_map/pallas_call | solution.py:361
  74.1 0.1 fusion.4
  74.2 2.8 %collective-permute-start.16 = (bf16[4,144,512]{2,1,0:T(8,128)(2,1)}, bf16[4,144,512]{2,1,0:T(8,128)(2,1)S(1)}, u32[]{:S(2)}, u32[]{:S(2)}) collective-permute-start(bf16[4,144,512]{2,1,0:T(8,128)(2,1)} %get-tuple-element.97), channel_id=1, source_target_pairs={{0,128},{2,130},{4,132},{6,134},{8,136},{10,138},{12,140},{14,142}... | collective-permute-start | bytes 1769480 | tf_op jit(solution)/shard_map/ppermute | solution.py:39
  77.0 2.7 %collective-permute-start.19 = (bf16[2,144,640]{2,1,0:T(8,128)(2,1)}, bf16[2,144,640]{2,1,0:T(8,128)(2,1)S(1)}, u32[]{:S(2)}, u32[]{:S(2)}) collective-permute-start(bf16[2,144,640]{2,1,0:T(8,128)(2,1)} %get-tuple-element.106), channel_id=1, source_target_pairs={{0,96},{2,98},{4,100},{6,102},{8,104},{10,106},{12,108},{14,110},{... | collective-permute-start | bytes 1105928 | tf_op jit(solution)/shard_map/ppermute | solution.py:39
  79.7 0.1 fusion.3
  79.8 0.2 multiply_reduce_fusion
  80.0 0.7 divide_convert_fusion
  80.7 10.0 %collective-permute-done.16 = bf16[4,144,512]{2,1,0:T(8,128)(2,1)S(1)} collective-permute-done((bf16[4,144,512]{2,1,0:T(8,128)(2,1)}, bf16[4,144,512]{2,1,0:T(8,128)(2,1)S(1)}, u32[]{:S(2)}, u32[]{:S(2)}) %collective-permute-start.16) | collective-permute-done | bytes 589856 | tf_op jit(solution)/shard_map/ppermute | solution.py:39
  90.8 1.5 %convert_add_fusion = f32[4,144,512]{2,1,0:T(8,128)S(1)} fusion(f32[4,144,512]{2,1,0:T(8,128)} %get-tuple-element.96, bf16[4,144,512]{2,1,0:T(8,128)(2,1)S(1)} %collective-permute-done.16), kind=kLoop, calls=%fused_computation | loop fusion | flops 589824 | bytes 2949120 | tf_op jit(solution)/shard_map/add | solution.py:510
  92.3 0.9 collective-permute-start.24
  93.3 0.1 collective-permute-start.21
  93.5 3.0 %collective-permute-done.18 = bf16[2,144,640]{2,1,0:T(8,128)(2,1)S(1)} collective-permute-done((bf16[2,144,640]{2,1,0:T(8,128)(2,1)}, bf16[2,144,640]{2,1,0:T(8,128)(2,1)S(1)}, u32[]{:S(2)}, u32[]{:S(2)}) %collective-permute-start.18) | collective-permute-done | bytes 368672 | tf_op jit(solution)/shard_map/ppermute | solution.py:39
  96.5 0.2 add_add_fusion
  96.7 1.5 %collective-permute-start.20 = (bf16[144,640]{1,0:T(8,128)(2,1)S(1)}, bf16[144,640]{1,0:T(8,128)(2,1)S(1)}, u32[]{:S(2)}, u32[]{:S(2)}) collective-permute-start(bf16[144,640]{1,0:T(8,128)(2,1)S(1)} %fusion.2), channel_id=1, source_target_pairs={{0,128},{2,130},{4,132},{6,134},{8,136},{10,138},{12,140},{14,142}... | collective-permute-start | bytes 552968 | tf_op jit(solution)/shard_map/ppermute | solution.py:39
  98.2 0.8 collective-permute-done.21
  99.0 1.3 %collective-permute-start.29 = (bf16[32,1152]{1,0:T(8,128)(2,1)S(1)}, bf16[32,1152]{1,0:T(8,128)(2,1)S(1)}, u32[]{:S(2)}, u32[]{:S(2)}) collective-permute-start(bf16[32,1152]{1,0:T(8,128)(2,1)S(1)} %get-tuple-element.113), channel_id=1, source_target_pairs={{0,242},{4,246},{8,250},{12,254},{16,2},{20,6},{24,10},{28,14},{32... | collective-permute-start | bytes 221192 | tf_op jit(solution)/shard_map/ppermute | solution.py:44
  100.3 2.6 %collective-permute-done.22 = bf16[144,512]{1,0:T(8,128)(2,1)S(1)} collective-permute-done((bf16[144,512]{1,0:T(8,128)(2,1)S(1)}, bf16[144,512]{1,0:T(8,128)(2,1)S(1)}, u32[]{:S(2)}, u32[]{:S(2)}) %collective-permute-start.22) | collective-permute-done | bytes 147488 | tf_op jit(solution)/shard_map/ppermute | solution.py:39
  103.2 0.1 reshape.92
  103.3 1.1 collective-permute-start.25
  104.4 4.3 %collective-permute-done.29 = bf16[32,1152]{1,0:T(8,128)(2,1)S(1)} collective-permute-done((bf16[32,1152]{1,0:T(8,128)(2,1)S(1)}, bf16[32,1152]{1,0:T(8,128)(2,1)S(1)}, u32[]{:S(2)}, u32[]{:S(2)}) %collective-permute-start.29) | collective-permute-done | bytes 73760 | tf_op jit(solution)/shard_map/ppermute | solution.py:44
  108.7 0.2 multiply_reduce_fusion.1
  108.9 0.8 collective-permute-done.25
  109.7 0.3 collective-permute-start.26
  110.1 3.7 %collective-permute-start.27 = (bf16[18,1152]{1,0:T(8,128)(2,1)S(1)}, bf16[18,1152]{1,0:T(8,128)(2,1)S(1)}, u32[]{:S(2)}, u32[]{:S(2)}) collective-permute-start(bf16[18,1152]{1,0:T(8,128)(2,1)S(1)} %get-tuple-element.130), channel_id=1, source_target_pairs={{0,8},{2,10},{4,12},{6,14},{8,16},{10,18},{12,20},{14,22},{16,24},... | collective-permute-start | bytes 124424 | tf_op jit(solution)/shard_map/ppermute | solution.py:39
  113.8 1.1 collective-permute-start.28
  114.9 0.1 divide_convert_fusion.1
  115.0 1.1 collective-permute-start.30
  116.2 0.8 collective-permute-done.26
  117.0 1.3 %collective-permute-done.27 = bf16[18,1152]{1,0:T(8,128)(2,1)S(1)} collective-permute-done((bf16[18,1152]{1,0:T(8,128)(2,1)S(1)}, bf16[18,1152]{1,0:T(8,128)(2,1)S(1)}, u32[]{:S(2)}, u32[]{:S(2)}) %collective-permute-start.27) | collective-permute-done | bytes 41504 | tf_op jit(solution)/shard_map/ppermute | solution.py:39
  118.4 4.9 %collective-permute-start.31 = (f32[9,1152]{1,0:T(8,128)S(1)}, f32[9,1152]{1,0:T(8,128)S(1)}, u32[]{:S(2)}, u32[]{:S(2)}) collective-permute-start(f32[9,1152]{1,0:T(8,128)S(1)} %slice_select_fusion), channel_id=1, source_target_pairs={{0,2},{2,0},{4,6},{6,4},{8,10},{10,8},{12,14},{14,12},{16,18},{18,... | collective-permute-start | bytes 124424 | tf_op jit(solution)/shard_map/ppermute | solution.py:39
  123.2 0.7 maximum_select_fusion
  123.9 0.2 collective-permute-done.31
  124.2 0.7 pad_maximum_fusion.2
  (84 shorter events, 1.4 us)
Async XLA Ops:
  2.9 20.5 %collective-permute-start = (bf16[32,1152]{1,0:T(8,128)(2,1)}, bf16[32,1152]{1,0:T(8,128)(2,1)S(1)}, u32[]{:S(2)}, u32[]{:S(2)}) collective-permute-start(bf16[32,1152]{1,0:T(8,128)(2,1)} %shard_map.148), channel_id=1, source_target_pairs={{0,4},{2,6},{4,8},{6,10},{8,12},{10,14},{12,16},{14,18},{16,20},{1... | collective-permute-start | bytes 221192 | tf_op jit(solution)/shard_map/ppermute | solution.py:44
  5.4 28.5 %collective-permute-start.3 = (bf16[32,1152]{1,0:T(8,128)(2,1)}, bf16[32,1152]{1,0:T(8,128)(2,1)S(1)}, u32[]{:S(2)}, u32[]{:S(2)}) collective-permute-start(bf16[32,1152]{1,0:T(8,128)(2,1)} %shard_map.148), channel_id=1, source_target_pairs={{2,16},{6,20},{10,24},{14,28},{18,32},{22,36},{26,40},{30,44},{34,... | collective-permute-start | bytes 221192 | tf_op jit(solution)/shard_map/ppermute | solution.py:44
  14.1 9.4 %collective-permute-start.1 = (bf16[32,1152]{1,0:T(8,128)(2,1)}, bf16[32,1152]{1,0:T(8,128)(2,1)S(1)}, u32[]{:S(2)}, u32[]{:S(2)}) collective-permute-start(bf16[32,1152]{1,0:T(8,128)(2,1)} %own_ref), channel_id=1, source_target_pairs={{0,1},{1,0},{2,3},{3,2},{4,5},{5,4},{6,7},{7,6},{8,9},{9,8},{10,11... | collective-permute-start | bytes 221192 | tf_op jit(solution)/shard_map/ppermute | solution.py:48
  15.5 7.3 %collective-permute-start.6 = (f32[729]{0:T(1024)}, f32[729]{0:T(1024)S(1)}, u32[]{:S(2)}, u32[]{:S(2)}) collective-permute-start(f32[729]{0:T(1024)} %param.21), channel_id=1, source_target_pairs={{0,2},{2,0},{4,6},{6,4},{8,10},{10,8},{12,14},{14,12},{16,18},{18,... | collective-permute-start | bytes 8756 | tf_op jit(solution)/shard_map/ppermute | solution.py:39
  15.5 34.7 %collective-permute-start.11 = (bf16[729,2152]{1,0:T(8,128)(2,1)}, bf16[729,2152]{1,0:T(8,128)(2,1)}, u32[]{:S(2)}, u32[]{:S(2)}) collective-permute-start(bf16[729,2152]{1,0:T(8,128)(2,1)} %hidden_hbm), channel_id=1, source_target_pairs={{0,2},{2,0},{4,6},{6,4},{8,10},{10,8},{12,14},{14,12},{16,18},{18,... | collective-permute-start | bytes 9412856 | tf_op jit(solution)/shard_map/ppermute | solution.py:39
  18.9 1.5 %copy-start.1 = (bf16[729,1152]{1,0:T(8,128)(2,1)S(1)}, bf16[729,1152]{1,0:T(8,128)(2,1)}, u32[]{:S(2)}) copy-start(bf16[729,1152]{1,0:T(8,128)(2,1)} %normed_ref) | copy-start | bytes 5038852
  20.3 1.0 copy-start.11
  20.4 3.1 %copy-start.8 = (bf16[32,1152]{1,0:T(8,128)(2,1)S(1)}, bf16[32,1152]{1,0:T(8,128)(2,1)}, u32[]{:S(2)}) copy-start(bf16[32,1152]{1,0:T(8,128)(2,1)} %shard_map.148) | copy-start | bytes 221188
  20.4 4.4 %copy-start.12 = (s32[32]{0:T(128)S(1)}, s32[32]{0:T(128)}, u32[]{:S(2)}) copy-start(s32[32]{0:T(128)} %param.17) | copy-start | bytes 388
  21.2 12.7 %copy-start = (bf16[1152,768]{1,0:T(8,128)(2,1)}, bf16[1152,768]{1,0:T(8,128)(2,1)S(1)}, u32[]{:S(2)}) copy-start(bf16[1152,768]{1,0:T(8,128)(2,1)S(1)} %shard_map.152.normed0_hbm) | copy-start | bytes 5308420
  22.9 21.3 %collective-permute-start.9 = (bf16[729,1152]{1,0:T(8,128)(2,1)}, bf16[729,1152]{1,0:T(8,128)(2,1)}, u32[]{:S(2)}, u32[]{:S(2)}) collective-permute-start(bf16[729,1152]{1,0:T(8,128)(2,1)} %cotangent_hbm), channel_id=1, source_target_pairs={{0,2},{2,0},{4,6},{6,4},{8,10},{10,8},{12,14},{14,12},{16,18},{18,... | collective-permute-start | bytes 5038856 | tf_op jit(solution)/shard_map/ppermute | solution.py:39
  23.5 15.7 %copy-start.2 = (bf16[32,1152]{1,0:T(8,128)(2,1)S(1)}, bf16[32,1152]{1,0:T(8,128)(2,1)}, u32[]{:S(2)}) copy-start(bf16[32,1152]{1,0:T(8,128)(2,1)} %own_ref) | copy-start | bytes 221188
  23.5 15.7 %copy-start.3 = (s32[2]{0:T(128)S(1)}, s32[2]{0:T(128)}, u32[]{:S(2)}) copy-start(s32[2]{0:T(128)} %pad_add_fusion.place_ref) | copy-start | bytes 28
  23.5 13.2 %collective-permute-start.2 = (bf16[64,1152]{1,0:T(8,128)(2,1)S(1)}, bf16[64,1152]{1,0:T(8,128)(2,1)S(1)}, u32[]{:S(2)}, u32[]{:S(2)}) collective-permute-start(bf16[64,1152]{1,0:T(8,128)(2,1)S(1)} %pad_maximum_fusion.1.refs_0_), channel_id=1, source_target_pairs={{0,8},{2,10},{4,12},{6,14},{8,16},{10,18},{12,20},{14,22},{16,24},... | collective-permute-start | bytes 442376 | tf_op jit(solution)/shard_map/ppermute | solution.py:44
  24.8 10.2 %collective-permute-start.4 = (s32[32]{0:T(128)S(1)}, s32[32]{0:T(128)S(1)}, u32[]{:S(2)}, u32[]{:S(2)}) collective-permute-start(s32[32]{0:T(128)S(1)} %copy-done.12), channel_id=1, source_target_pairs={{0,1},{1,0},{2,3},{3,2},{4,5},{5,4},{6,7},{7,6},{8,9},{9,8},{10,11... | collective-permute-start | bytes 392 | tf_op jit(solution)/shard_map/ppermute | solution.py:48
  33.9 26.9 %collective-permute-start.15 = (bf16[1152,768]{1,0:T(8,128)(2,1)S(1)}, bf16[1152,768]{1,0:T(8,128)(2,1)}, u32[]{:S(2)}, u32[]{:S(2)}) collective-permute-start(bf16[1152,768]{1,0:T(8,128)(2,1)S(1)} %shard_map.152.normed0_hbm), channel_id=1, source_target_pairs={{0,2},{2,0},{4,6},{6,4},{8,10},{10,8},{12,14},{14,12},{16,18},{18,... | collective-permute-start | bytes 5308424 | tf_op jit(solution)/shard_map/ppermute | solution.py:39
  35.0 4.2 %collective-permute-start.7 = (bf16[64,1152]{1,0:T(8,128)(2,1)S(1)}, bf16[64,1152]{1,0:T(8,128)(2,1)S(1)}, u32[]{:S(2)}, u32[]{:S(2)}) collective-permute-start(bf16[64,1152]{1,0:T(8,128)(2,1)S(1)} %pad_maximum_fusion.1.refs_0_), channel_id=1, source_target_pairs={{0,2},{2,0},{4,6},{6,4},{8,10},{10,8},{12,14},{14,12},{16,18},{18,... | collective-permute-start | bytes 442376 | tf_op jit(solution)/shard_map/ppermute | solution.py:39
  36.7 2.5 %collective-permute-start.5 = (bf16[64,1152]{1,0:T(8,128)(2,1)S(1)}, bf16[64,1152]{1,0:T(8,128)(2,1)S(1)}, u32[]{:S(2)}, u32[]{:S(2)}) collective-permute-start(bf16[64,1152]{1,0:T(8,128)(2,1)S(1)} %collective-permute-done.2.refs_1_), channel_id=1, source_target_pairs={{0,2},{2,0},{4,6},{6,4},{8,10},{10,8},{12,14},{14,12},{16,18},{18,... | collective-permute-start | bytes 442376 | tf_op jit(solution)/shard_map/ppermute | solution.py:39
  40.8 2.4 %collective-permute-start.8 = (bf16[128,1152]{1,0:T(8,128)(2,1)S(1)}, bf16[128,1152]{1,0:T(8,128)(2,1)S(1)}, u32[]{:S(2)}, u32[]{:S(2)}) collective-permute-start(bf16[128,1152]{1,0:T(8,128)(2,1)S(1)} %get-tuple-element.80), channel_id=1, source_target_pairs={{0,2},{2,0},{4,6},{6,4},{8,10},{10,8},{12,14},{14,12},{16,18},{18,... | collective-permute-start | bytes 884744 | tf_op jit(solution)/shard_map/ppermute | solution.py:39
  41.2 17.9 %collective-permute-start.10 = (f32[1,1152]{1,0:T(1,128)S(1)}, f32[1,1152]{1,0:T(1,128)S(1)}, u32[]{:S(2)}, u32[]{:S(2)}) collective-permute-start(f32[1,1152]{1,0:T(1,128)S(1)} %get-tuple-element.81), channel_id=1, source_target_pairs={{0,1},{1,0},{2,3},{3,2},{4,5},{5,4},{6,7},{7,6},{8,9},{9,8},{10,11... | collective-permute-start | bytes 13832 | tf_op jit(solution)/shard_map/ppermute | solution.py:48
  43.2 15.9 %copy-start.6 = (bf16[128,1152]{1,0:T(8,128)(2,1)}, bf16[128,1152]{1,0:T(8,128)(2,1)S(1)}, u32[]{:S(2)}) copy-start(bf16[128,1152]{1,0:T(8,128)(2,1)S(1)} %collective-permute-done.8) | copy-start | bytes 884740
  43.2 16.8 %collective-permute-start.14 = (bf16[32,1152]{1,0:T(8,128)(2,1)S(1)}, bf16[32,1152]{1,0:T(8,128)(2,1)S(1)}, u32[]{:S(2)}, u32[]{:S(2)}) collective-permute-start(bf16[32,1152]{1,0:T(8,128)(2,1)S(1)} %get-tuple-element.89), channel_id=1, source_target_pairs={{0,1},{1,0},{2,3},{3,2},{4,5},{5,4},{6,7},{7,6},{8,9},{9,8},{10,11... | collective-permute-start | bytes 221192 | tf_op jit(solution)/shard_map/ppermute | solution.py:48
  44.2 15.9 %collective-permute-start.13 = (bf16[64,1152]{1,0:T(8,128)(2,1)S(1)}, bf16[64,1152]{1,0:T(8,128)(2,1)S(1)}, u32[]{:S(2)}, u32[]{:S(2)}) collective-permute-start(bf16[64,1152]{1,0:T(8,128)(2,1)S(1)} %add_convert_fusion), channel_id=1, source_target_pairs={{0,248},{2,250},{4,252},{6,254},{8,0},{10,2},{12,4},{14,6},{16,8},... | collective-permute-start | bytes 442376 | tf_op jit(solution)/shard_map/ppermute | solution.py:44
  59.1 1.7 %copy-start.9 = (f32[2,1152]{1,0:T(2,128)}, f32[2,1152]{1,0:T(2,128)S(1)}, u32[]{:S(2)}) copy-start(f32[2,1152]{1,0:T(2,128)S(1)} %pad_maximum_fusion.3.row0_ref) | copy-start | bytes 27652
  59.2 1.7 %collective-permute-start.12 = (f32[2,1152]{1,0:T(2,128)S(1)}, f32[2,1152]{1,0:T(2,128)S(1)}, u32[]{:S(2)}, u32[]{:S(2)}) collective-permute-start(f32[2,1152]{1,0:T(2,128)S(1)} %pad_maximum_fusion.3.row0_ref), channel_id=1, source_target_pairs={{0,2},{2,0},{4,6},{6,4},{8,10},{10,8},{12,14},{14,12},{16,18},{18,... | collective-permute-start | bytes 27656 | tf_op jit(solution)/shard_map/ppermute | solution.py:39
  60.0 19.6 %copy-start.4 = (bf16[64,1152]{1,0:T(8,128)(2,1)S(1)}, bf16[64,1152]{1,0:T(8,128)(2,1)}, u32[]{:S(2)}) copy-start(bf16[64,1152]{1,0:T(8,128)(2,1)} %raw_ref.1) | copy-start | bytes 442372
  60.9 0.6 copy-start.10
  74.2 16.6 %collective-permute-start.16 = (bf16[4,144,512]{2,1,0:T(8,128)(2,1)}, bf16[4,144,512]{2,1,0:T(8,128)(2,1)S(1)}, u32[]{:S(2)}, u32[]{:S(2)}) collective-permute-start(bf16[4,144,512]{2,1,0:T(8,128)(2,1)} %get-tuple-element.97), channel_id=1, source_target_pairs={{0,128},{2,130},{4,132},{6,134},{8,136},{10,138},{12,140},{14,142}... | collective-permute-start | bytes 1769480 | tf_op jit(solution)/shard_map/ppermute | solution.py:39
  77.0 16.5 %collective-permute-start.17 = (bf16[2,144,640]{2,1,0:T(8,128)(2,1)}, bf16[2,144,640]{2,1,0:T(8,128)(2,1)S(1)}, u32[]{:S(2)}, u32[]{:S(2)}) collective-permute-start(bf16[2,144,640]{2,1,0:T(8,128)(2,1)} %get-tuple-element.104), channel_id=1, source_target_pairs={{0,64},{2,66},{4,68},{6,70},{8,72},{10,74},{12,76},{14,78},{16,80}... | collective-permute-start | bytes 1105928 | tf_op jit(solution)/shard_map/ppermute | solution.py:39
  77.0 19.5 %collective-permute-start.18 = (bf16[2,144,640]{2,1,0:T(8,128)(2,1)}, bf16[2,144,640]{2,1,0:T(8,128)(2,1)S(1)}, u32[]{:S(2)}, u32[]{:S(2)}) collective-permute-start(bf16[2,144,640]{2,1,0:T(8,128)(2,1)} %get-tuple-element.105), channel_id=1, source_target_pairs={{0,32},{2,34},{4,36},{6,38},{8,40},{10,42},{12,44},{14,46},{16,48}... | collective-permute-start | bytes 1105928 | tf_op jit(solution)/shard_map/ppermute | solution.py:39
  77.0 19.5 %collective-permute-start.19 = (bf16[2,144,640]{2,1,0:T(8,128)(2,1)}, bf16[2,144,640]{2,1,0:T(8,128)(2,1)S(1)}, u32[]{:S(2)}, u32[]{:S(2)}) collective-permute-start(bf16[2,144,640]{2,1,0:T(8,128)(2,1)} %get-tuple-element.106), channel_id=1, source_target_pairs={{0,96},{2,98},{4,100},{6,102},{8,104},{10,106},{12,108},{14,110},{... | collective-permute-start | bytes 1105928 | tf_op jit(solution)/shard_map/ppermute | solution.py:39
  80.0 12.2 %copy-start.7 = (bf16[128,1152]{1,0:T(8,128)(2,1)S(1)}, bf16[128,1152]{1,0:T(8,128)(2,1)}, u32[]{:S(2)}) copy-start(bf16[128,1152]{1,0:T(8,128)(2,1)} %copy-done.6) | copy-start | bytes 884740
  92.2 4.3 %copy-start.5 = (f32[2,144,640]{2,1,0:T(8,128)S(1)}, f32[2,144,640]{2,1,0:T(8,128)}, u32[]{:S(2)}) copy-start(f32[2,144,640]{2,1,0:T(8,128)} %get-tuple-element.103) | copy-start | bytes 2211844
  92.3 10.8 %collective-permute-start.24 = (bf16[32,1152]{1,0:T(8,128)(2,1)S(1)}, bf16[32,1152]{1,0:T(8,128)(2,1)S(1)}, u32[]{:S(2)}, u32[]{:S(2)}) collective-permute-start(bf16[32,1152]{1,0:T(8,128)(2,1)S(1)} %slice.116), channel_id=1, source_target_pairs={{0,252},{2,254},{4,0},{6,2},{8,4},{10,6},{12,8},{14,10},{16,12},{1... | collective-permute-start | bytes 221192 | tf_op jit(solution)/shard_map/ppermute | solution.py:44
  93.3 5.7 %collective-permute-start.21 = (bf16[144,512]{1,0:T(8,128)(2,1)S(1)}, bf16[144,512]{1,0:T(8,128)(2,1)S(1)}, u32[]{:S(2)}, u32[]{:S(2)}) collective-permute-start(bf16[144,512]{1,0:T(8,128)(2,1)S(1)} %get-tuple-element.125), channel_id=1, source_target_pairs={{0,64},{2,66},{4,68},{6,70},{8,72},{10,74},{12,76},{14,78},{16,80}... | collective-permute-start | bytes 442376 | tf_op jit(solution)/shard_map/ppermute | solution.py:39
  93.5 9.5 %collective-permute-start.22 = (bf16[144,512]{1,0:T(8,128)(2,1)S(1)}, bf16[144,512]{1,0:T(8,128)(2,1)S(1)}, u32[]{:S(2)}, u32[]{:S(2)}) collective-permute-start(bf16[144,512]{1,0:T(8,128)(2,1)S(1)} %get-tuple-element.127), channel_id=1, source_target_pairs={{0,32},{2,34},{4,36},{6,38},{8,40},{10,42},{12,44},{14,46},{16,48}... | collective-permute-start | bytes 442376 | tf_op jit(solution)/shard_map/ppermute | solution.py:39
  96.5 6.4 %collective-permute-start.23 = (bf16[144,512]{1,0:T(8,128)(2,1)S(1)}, bf16[144,512]{1,0:T(8,128)(2,1)S(1)}, u32[]{:S(2)}, u32[]{:S(2)}) collective-permute-start(bf16[144,512]{1,0:T(8,128)(2,1)S(1)} %get-tuple-element.126), channel_id=1, source_target_pairs={{0,96},{2,98},{4,100},{6,102},{8,104},{10,106},{12,108},{14,110},{... | collective-permute-start | bytes 442376 | tf_op jit(solution)/shard_map/ppermute | solution.py:39
  96.7 6.3 %collective-permute-start.20 = (bf16[144,640]{1,0:T(8,128)(2,1)S(1)}, bf16[144,640]{1,0:T(8,128)(2,1)S(1)}, u32[]{:S(2)}, u32[]{:S(2)}) collective-permute-start(bf16[144,640]{1,0:T(8,128)(2,1)S(1)} %fusion.2), channel_id=1, source_target_pairs={{0,128},{2,130},{4,132},{6,134},{8,136},{10,138},{12,140},{14,142}... | collective-permute-start | bytes 552968 | tf_op jit(solution)/shard_map/ppermute | solution.py:39
  99.0 9.7 %collective-permute-start.29 = (bf16[32,1152]{1,0:T(8,128)(2,1)S(1)}, bf16[32,1152]{1,0:T(8,128)(2,1)S(1)}, u32[]{:S(2)}, u32[]{:S(2)}) collective-permute-start(bf16[32,1152]{1,0:T(8,128)(2,1)S(1)} %get-tuple-element.113), channel_id=1, source_target_pairs={{0,242},{4,246},{8,250},{12,254},{16,2},{20,6},{24,10},{28,14},{32... | collective-permute-start | bytes 221192 | tf_op jit(solution)/shard_map/ppermute | solution.py:44
  103.3 6.4 %collective-permute-start.25 = (bf16[4,18,1152]{2,1,0:T(8,128)(2,1)S(1)}, bf16[4,18,1152]{2,1,0:T(8,128)(2,1)S(1)}, u32[]{:S(2)}, u32[]{:S(2)}) collective-permute-start(bf16[4,18,1152]{2,1,0:T(8,128)(2,1)S(1)} %fusion.1), channel_id=1, source_target_pairs={{0,4},{2,6},{4,0},{6,2},{8,12},{10,14},{12,8},{14,10},{16,20},{18,... | collective-permute-start | bytes 497672 | tf_op jit(solution)/shard_map/ppermute | solution.py:542
  109.7 7.2 %collective-permute-start.26 = (bf16[18,1152]{1,0:T(8,128)(2,1)S(1)}, bf16[18,1152]{1,0:T(8,128)(2,1)S(1)}, u32[]{:S(2)}, u32[]{:S(2)}) collective-permute-start(bf16[18,1152]{1,0:T(8,128)(2,1)S(1)} %get-tuple-element.128), channel_id=1, source_target_pairs={{0,16},{2,18},{4,20},{6,22},{8,24},{10,26},{12,28},{14,30},{16,0},... | collective-permute-start | bytes 124424 | tf_op jit(solution)/shard_map/ppermute | solution.py:39
  110.1 8.2 %collective-permute-start.27 = (bf16[18,1152]{1,0:T(8,128)(2,1)S(1)}, bf16[18,1152]{1,0:T(8,128)(2,1)S(1)}, u32[]{:S(2)}, u32[]{:S(2)}) collective-permute-start(bf16[18,1152]{1,0:T(8,128)(2,1)S(1)} %get-tuple-element.130), channel_id=1, source_target_pairs={{0,8},{2,10},{4,12},{6,14},{8,16},{10,18},{12,20},{14,22},{16,24},... | collective-permute-start | bytes 124424 | tf_op jit(solution)/shard_map/ppermute | solution.py:39
  113.8 4.5 %collective-permute-start.28 = (bf16[18,1152]{1,0:T(8,128)(2,1)S(1)}, bf16[18,1152]{1,0:T(8,128)(2,1)S(1)}, u32[]{:S(2)}, u32[]{:S(2)}) collective-permute-start(bf16[18,1152]{1,0:T(8,128)(2,1)S(1)} %get-tuple-element.129), channel_id=1, source_target_pairs={{0,24},{2,26},{4,28},{6,30},{8,0},{10,2},{12,4},{14,6},{16,8},{18,... | collective-permute-start | bytes 124424 | tf_op jit(solution)/shard_map/ppermute | solution.py:39
  115.0 3.3 %collective-permute-start.30 = (bf16[32,1152]{1,0:T(8,128)(2,1)S(1)}, bf16[32,1152]{1,0:T(8,128)(2,1)S(1)}, u32[]{:S(2)}, u32[]{:S(2)}) collective-permute-start(bf16[32,1152]{1,0:T(8,128)(2,1)S(1)} %divide_convert_fusion.1), channel_id=1, source_target_pairs={{0,1},{1,0},{2,3},{3,2},{4,5},{5,4},{6,7},{7,6},{8,9},{9,8},{10,11... | collective-permute-start | bytes 221192 | tf_op jit(solution)/shard_map/ppermute | solution.py:48
  118.4 5.8 %collective-permute-start.31 = (f32[9,1152]{1,0:T(8,128)S(1)}, f32[9,1152]{1,0:T(8,128)S(1)}, u32[]{:S(2)}, u32[]{:S(2)}) collective-permute-start(f32[9,1152]{1,0:T(8,128)S(1)} %slice_select_fusion), channel_id=1, source_target_pairs={{0,2},{2,0},{4,6},{6,4},{8,10},{10,8},{12,14},{14,12},{16,18},{18,... | collective-permute-start | bytes 124424 | tf_op jit(solution)/shard_map/ppermute | solution.py:39
